TPU v7x, 32 devices: a whole 2x2x4 slice. The times are simulated.
32 devices in a mesh: seq: 8 (over z, y), head: 4 (over x, core).
Axes of the slice: x: 2, y: 2, z: 4, core: 2. Of those that a mesh axis runs over, the one named last changes fastest.
Arguments:
- queries: float32 [1024, 4096], P('seq', 'head'), may hold values from -6 to 6
- key_rows: float32 [1024, 4096], P('seq', 'head'), may hold values from -6 to 6
- value_rows: float32 [1024, 4096], P('seq', 'head'), may hold values from -6 to 6
- target: float32 [1024, 4096], P('seq', 'head'), may hold values from -6 to 6
- norm_gain: float32 [4096], P('head'), may hold values from 0.1 to 1.9
- valid_mask: int32 [1024], P('seq'), may hold values from 0 to 1, as said below
Outputs:
- grad_queries: float32 [1024, 4096], P('seq', 'head')
- grad_keys: float32 [1024, 4096], P('seq', 'head')
- grad_values: float32 [1024, 4096], P('seq', 'head')
- loss_value: float32 [], replicated
Inputs may be any that keep to these rules, and one draw needn't show every extreme that they name: `valid_mask`: the last token of the sequence is valid.
All inputs are finite; a program needn't handle non-finite values.
Results may differ from a plain program's by a relative error of at most 0.0003.
Values sent between devices are 32-bit elements; how exact they have to be, the bound alone decides.
No kernel may reach another device: no remote copies, remote signals or barrier semaphores. Data moves between devices by JAX's collectives and lax.ppermute only.
A program may use at most 64 MiB of HBM per device.

v0:
```python
import jax
import jax.numpy as jnp
from jax import lax
from jax.sharding import PartitionSpec as P

HEAD_DIM = 128
WIDTH = 4096


epsilon = 1e-06


def entering(part, axis, combine, identity, reverse):
    count = lax.axis_size(axis)
    place = lax.axis_index(axis)
    ahead = count - 1 - place if reverse else place
    gathered = lax.all_gather(part, axis)
    state = jnp.zeros_like(part) + jnp.asarray(identity, part.dtype)

    def one(lap, state):
        source = count - 1 - lap if reverse else lap
        return combine(state, lax.dynamic_index_in_dim(gathered, source, 0, False))

    return lax.fori_loop(0, ahead, one, state)


def combine_sum(earlier, later):
    return earlier + later


def shards(queries, key_rows, value_rows, target, norm_gain, valid_mask):
    highest = lax.Precision.HIGHEST
    length, columns = queries.shape
    heads_here = columns // HEAD_DIM
    query_heads = queries.reshape(length, heads_here, HEAD_DIM)
    key_heads = key_rows.reshape(length, heads_here, HEAD_DIM)
    value_heads = value_rows.reshape(length, heads_here, HEAD_DIM)
    causal = jnp.tril(jnp.ones((length, length), jnp.float32))
    mask_float = valid_mask.astype(jnp.float32)
    weighted = mask_float[:, None] * target
    local_count = jnp.sum(mask_float)
    token_total = lax.psum(local_count, "seq")
    scores = jnp.einsum("the,she->hts", query_heads, key_heads, precision=highest) * causal
    local_out = jnp.einsum("hts,shf->thf", scores, value_heads, precision=highest)
    kv_local = jnp.einsum("the,thf->hef", key_heads, value_heads, precision=highest)
    empty_state = jnp.zeros((heads_here, HEAD_DIM, HEAD_DIM), jnp.float32)
    prior_state = entering(kv_local, "seq", combine_sum, empty_state, False)
    attended = local_out + jnp.einsum("the,hef->thf", query_heads, prior_state, precision=highest)
    attended = attended.reshape(length, columns)
    squares = jnp.sum(attended * attended, axis=1)
    dots_local = jnp.sum(norm_gain * weighted * attended, axis=1)
    total_squares = lax.psum(squares, "head")
    inverse_rms = lax.rsqrt(total_squares / WIDTH + epsilon)
    normed = attended * inverse_rms[:, None] * norm_gain
    loss_local = jnp.sum(weighted * normed)
    gain_dots = lax.psum(dots_local, "head")
    grad_core = inverse_rms[:, None] * (
        norm_gain * weighted - attended * (inverse_rms * inverse_rms * gain_dots / WIDTH)[:, None]
    )
    whole_tokens = length * lax.axis_size("seq")
    loss_value = lax.psum(loss_local, ("seq", "head")) / token_total
    grad_out = whole_tokens / token_total * grad_core
    grad_heads = grad_out.reshape(length, heads_here, HEAD_DIM)
    grad_local = jnp.einsum("the,thf->hef", query_heads, grad_heads, precision=highest)
    later_state = entering(grad_local, "seq", combine_sum, empty_state, True)
    grad_scores = jnp.einsum("thf,shf->hts", grad_heads, value_heads, precision=highest) * causal
    grad_query = jnp.einsum("hts,she->the", grad_scores, key_heads, precision=highest)
    grad_query = grad_query + jnp.einsum("thf,hef->the", grad_heads, prior_state, precision=highest)
    grad_key = jnp.einsum("hts,the->she", grad_scores, query_heads, precision=highest)
    grad_key = grad_key + jnp.einsum("shf,hef->she", value_heads, later_state, precision=highest)
    grad_value = jnp.einsum("hts,thf->shf", scores, grad_heads, precision=highest)
    grad_value = grad_value + jnp.einsum("she,hef->shf", key_heads, later_state, precision=highest)
    grad_query = grad_query.reshape(length, columns)
    grad_key = grad_key.reshape(length, columns)
    grad_value = grad_value.reshape(length, columns)
    return (grad_query, grad_key, grad_value, loss_value)


def solution(mesh):
    return jax.shard_map(
        shards,
        mesh=mesh,
        in_specs=(
            P("seq", "head"),
            P("seq", "head"),
            P("seq", "head"),
            P("seq", "head"),
            P("head"),
            P("seq"),
        ),
        out_specs=(P("seq", "head"), P("seq", "head"), P("seq", "head"), P()),
        check_vma=False,
    )
```

profile of v0, /device:TPU:0, one launch (start us, length us, event | category | flops | bytes accessed | tf_op | source)
XLA Modules:
  0.0 210.4 jit_solution(1282957909632918667)
XLA Ops:
  7.3 1.2 copy.66
  8.7 2.7 %fusion.6 = f32[8,128,128]{2,1,0:T(8,128)} fusion(f32[128,8,128]{0,2,1:T(8,128)S(1)} %copy.38, f32[128,1024]{1,0:T(8,128)} %param.12), kind=kOutput, calls=%fused_computation.18 | convolution fusion | flops 201326592 | bytes 1572864 | tf_op jit(solution)/shard_map/the,thf->hef/dot_general | solution.py:45
  12.1 24.2 %psum.28 = f32[]{:T(128)} all-reduce(f32[]{:T(128)} %convert_reduce_fusion), channel_id=1, replica_groups=mesh['seq'=8,'head'=4] {'seq'}, use_global_device_ids=true, to_apply=%region_1.2 | all-reduce | flops 1 | bytes 8 | tf_op jit(solution)/shard_map/psum | solution.py:42
  37.0 1.2 convolution_multiply_fusion.1
  39.3 48.6 %all-gather.5.cloned.1.call-done = f32[64,128,128]{2,1,0:T(8,128)} async-done(((f32[8,128,128]{2,1,0:T(8,128)}), f32[64,128,128]{2,1,0:T(8,128)}) %all-gather.5.cloned.1.call-update) | async-done | bytes 4194320 | tf_op jit(solution)/shard_map/all_gather | solution.py:17
  88.9 5.7 %psum.29 = f32[128]{0:T(128)S(1)} all-reduce(f32[128]{0:T(128)S(1)} %get-tuple-element.115), channel_id=1, replica_groups=mesh['seq'=8,'head'=4] {'head'}, use_global_device_ids=true, to_apply=%region_5.6 | all-reduce | flops 128 | bytes 1024 | tf_op jit(solution)/shard_map/psum | solution.py:52
  94.8 1.9 multiply_reduce_fusion
  96.8 6.6 %psum.30 = f32[128]{0:T(128)S(1)} all-reduce(f32[128]{0:T(128)S(1)} %get-tuple-element.98), channel_id=1, replica_groups=mesh['seq'=8,'head'=4] {'head'}, use_global_device_ids=true, to_apply=%region_7.8 | all-reduce | flops 128 | bytes 1024 | tf_op jit(solution)/shard_map/psum | solution.py:56
  103.3 1.2 multiply_multiply_fusion
  106.5 46.2 %psum.31 = f32[]{:T(128)} all-reduce(f32[]{:T(128)} %get-tuple-element.97), channel_id=1, replica_groups=mesh['seq'=8,'head'=4] {'seq','head'}, use_global_device_ids=true, to_apply=%region_11.12 | all-reduce | flops 1 | bytes 8 | tf_op jit(solution)/shard_map/psum | solution.py:61
  155.0 2.2 %convolution_bitcast_fusion.4 = f32[128,8,128]{0,2,1:T(8,128)S(1)} fusion(f32[8,128,128]{2,1,0:T(8,128)S(1)} %convolution_multiply_fusion, f32[128,8,128]{0,2,1:T(8,128)} %copy-done.2), kind=kOutput, calls=%fused_computation.11 | convolution fusion | flops 201326592 | bytes 1572864 | tf_op jit(solution)/shard_map/hts,she->the/dot_general | solution.py:67
  157.3 1.4 fusion.1
  158.7 2.0 copy.57
  160.8 1.4 fusion.25
  162.2 1.8 convolution_bitcast_fusion.2
  164.0 23.8 %all-gather.7.cloned.1.call-done = f32[64,128,128]{2,1,0:T(8,128)} async-done(((f32[8,128,128]{2,1,0:T(8,128)}), f32[64,128,128]{2,1,0:T(8,128)}) %all-gather.7.cloned.1.call-update) | async-done | bytes 4194320 | tf_op jit(solution)/shard_map/all_gather | solution.py:17
  187.9 8.4 %while.23 = (s32[]{:T(128)}, f32[8,128,128]{2,1,0:T(8,128)S(1)}, s32[]{:T(128)}, f32[8,8,128,128]{3,2,1,0:T(8,128)}, s32[]{:T(128)}, /*index=5*/s32[]{:T(128)}, s32[]{:T(128)}, s32[]{:T(128)}) while((s32[]{:T(128)}, f32[8,128,128]{2,1,0:T(8,128)S(1)}, s32[]{:T(128)}, f32[8,8,128,128]{3,2,1,0:T(8,128)}, s32[]{:T(128)}, /*index=5*/s32[]{:T(128)}, ...), condition=%wide.region_9.10_spmd, body=%wide.region_8.9_spmd.sunk | while | flops 131078 | bytes 1573007 | solution.py:24
  187.9 1.3 bitcast_add_fusion.5
  189.2 1.2 bitcast_add_fusion.5
  190.4 1.2 bitcast_add_fusion.5
  191.6 1.2 bitcast_add_fusion.5
  192.8 1.2 bitcast_add_fusion.5
  196.4 2.0 fusion
  200.4 2.0 copy.58
  (42 shorter events, 10.5 us)
Async XLA Ops:
  7.2 29.8 %copy-start = (f32[128,1024]{1,0:T(8,128)S(1)}, f32[128,1024]{1,0:T(8,128)}, u32[]{:S(2)}) copy-start(f32[128,1024]{1,0:T(8,128)} %param.10) | copy-start | bytes 1572868
  7.2 29.8 %copy-start.3 = (f32[128,1024]{1,0:T(8,128)S(1)}, f32[128,1024]{1,0:T(8,128)}, u32[]{:S(2)}) copy-start(f32[128,1024]{1,0:T(8,128)} %param.11) | copy-start | bytes 1572868
  7.2 31.1 %copy-start.1 = (f32[128,1024]{1,0:T(8,128)S(1)}, f32[128,1024]{1,0:T(8,128)}, u32[]{:S(2)}) copy-start(f32[128,1024]{1,0:T(8,128)} %param.12) | copy-start | bytes 1572868
  7.2 4.3 %copy-start.8 = (s32[128]{0:T(128)S(1)}, s32[128]{0:T(128)}, u32[]{:S(2)}) copy-start(s32[128]{0:T(128)} %param.15) | copy-start | bytes 1540
  7.2 80.6 %all-gather.5.cloned.1.call-start = ((), (), s32[]{:S(2)}) async-start(), calls=%async_computation | async-start | bytes 4718592 | tf_op jit(solution)/shard_map/all_gather | solution.py:17
  8.7 28.2 %copy-start.2 = (f32[128,8,128]{0,2,1:T(8,128)}, f32[128,8,128]{0,2,1:T(8,128)S(1)}, u32[]{:S(2)}) copy-start(f32[128,8,128]{0,2,1:T(8,128)S(1)} %copy.38) | copy-start | bytes 1572868
  11.4 176.4 %all-gather.7.cloned.1.call-start = ((), (), s32[]{:S(2)}) async-start(), calls=%async_computation.1 | async-start | bytes 4718592 | tf_op jit(solution)/shard_map/all_gather | solution.py:17
  87.9 7.0 %copy-start.7 = (f32[1024]{0:T(1024)S(1)}, f32[1024]{0:T(1024)}, u32[]{:S(2)}) copy-start(f32[1024]{0:T(1024)} %param.14) | copy-start | bytes 12292
  187.8 8.5 %copy-start.6 = (f32[128,8,128]{0,2,1:T(8,128)S(1)}, f32[128,8,128]{0,2,1:T(8,128)}, u32[]{:S(2)}) copy-start(f32[128,8,128]{0,2,1:T(8,128)} %convolution_bitcast_fusion.2) | copy-start | bytes 1572868
  187.9 10.5 %copy-start.4 = (f32[128,1024]{1,0:T(8,128)S(1)}, f32[128,1024]{1,0:T(8,128)}, u32[]{:S(2)}) copy-start(f32[128,1024]{1,0:T(8,128)} %param.11) | copy-start | bytes 1572868
  187.9 10.5 %copy-start.5 = (f32[8,128,128]{2,1,0:T(8,128)S(1)}, f32[8,128,128]{2,1,0:T(8,128)}, u32[]{:S(2)}) copy-start(f32[8,128,128]{2,1,0:T(8,128)} %fusion.25) | copy-start | bytes 1572868
Sparse Core Ops, SparseCore 0:
  11.6 76.2 all-gather.4
  106.6 81.2 all-gather.6
where the time goes:
time: 211 us; the launch traced here: 210 us
  blocking collectives  82.7 us (39%)
  waiting for transfers between devices  72.4 us (34%)
  matrix products  17.5 us (8%)
  between operations  17.4 us (8%)
  other arithmetic  12.1 us (6%)
  local copies, waits for them, and re-layouts  8.04 us (4%)
    all_gather x2, waiting for transfers between devices, entering(): gathered = lax.all_gather(part, axis)  72.4 us
    psum x1, blocking collectives, shards(): loss_value = lax.psum(loss_local, ('seq', 'head')) / token_total  46.2 us
    psum x1, blocking collectives, shards(): token_total = lax.psum(local_count, 'seq')  24.2 us
    add x7, other arithmetic, combine_sum(): return earlier + later  8.28 us
    psum x1, blocking collectives, shards(): gain_dots = lax.psum(dots_local, 'head')  6.56 us
    unnamed x22, local copies, waits for them, and re-layouts  6.36 us
    psum x1, blocking collectives, shards(): total_squares = lax.psum(squares, 'head')  5.66 us
  transfers between devices with their start and end apart: 2, of which 2 were waited for; matrix products, arithmetic and copies ran while one was open for 6% of the time, Pallas kernels for 0%

commit v1 on v0

v1 whole, which is shorter than its diff:
```python
import functools

import jax
import jax.numpy as jnp
from jax import lax
from jax.experimental import pallas as pl
from jax.experimental.pallas import tpu as pltpu
from jax.sharding import PartitionSpec as P

HEAD_DIM = 128
TAIL = 8
epsilon = 1e-06
f32 = jnp.float32
bf16 = jnp.bfloat16


def split(x):
    high = x.astype(bf16)
    return high, (x - high.astype(f32)).astype(bf16)


def dot3(a, b, dims):
    d = functools.partial(lax.dot_general, dimension_numbers=(dims, ((), ())), preferred_element_type=f32)
    return d(a[0], b[0]) + (d(a[0], b[1]) + d(a[1], b[0]))


NN = ((1,), (0,))
NT = ((1,), (1,))
TN = ((0,), (0,))


def head_cols(h):
    return pl.ds(pl.multiple_of(h * HEAD_DIM, HEAD_DIM), HEAD_DIM)


def rows_of(i):
    return slice(i * HEAD_DIM, (i + 1) * HEAD_DIM)


def call(kernel, outs, n_in, flops, *args):
    nbytes = sum(a.size * 4 for a in args) + sum(o.size * 4 for o in outs)
    return pl.pallas_call(
        kernel,
        out_shape=outs,
        in_specs=[pl.BlockSpec(memory_space=pltpu.SMEM)] + [pl.BlockSpec(memory_space=pltpu.VMEM)] * (n_in - 1),
        out_specs=[pl.BlockSpec(memory_space=pltpu.VMEM)] * len(outs),
        compiler_params=pltpu.CompilerParams(vmem_limit_bytes=24 * 1024 * 1024),
        cost_estimate=pl.CostEstimate(flops=flops, bytes_accessed=nbytes, transcendentals=0),
    )(*args)


def shape(*s):
    return jax.ShapeDtypeStruct(s, f32)


def causal_mask(n):
    return lax.broadcasted_iota(jnp.int32, (n, n), 0) >= lax.broadcasted_iota(jnp.int32, (n, n), 1)


def state_kernel(group, own, place, k, v, mask, *out):
    count = jnp.sum(mask[...].astype(f32))
    for x in range(group):
        for i in range(own):
            cols = head_cols((place[0] ^ x) * own + i)
            out[x][rows_of(i), :] = dot3(split(k[:, cols]), split(v[:, cols]), TN)
        out[x][own * HEAD_DIM :, :] = jnp.full((TAIL, HEAD_DIM), count, f32)


def local_kernel(heads, place, q, k, v, scores, local):
    causal = causal_mask(q.shape[0])
    for h in range(heads):
        cols = head_cols(h)
        s = dot3(split(q[:, cols]), split(k[:, cols]), NT)
        s = jnp.where(causal, s, 0.0)
        scores[h] = s
        local[:, cols] = dot3(split(s), split(v[:, cols]), NN)


def pair_sum(parts):
    while len(parts) > 1:
        parts = [parts[i] + parts[i + 1] for i in range(0, len(parts), 2)]
    return parts[0]


def total_kernel(group, place, *refs):
    refs[group][...] = pair_sum([r[...] for r in refs[:group]])


def spread_kernel(group, own, reverse, place, *refs):
    parts = refs[:group]
    outer = refs[group]
    outs = refs[group + 1 :]
    here = place[0]
    body = slice(0, own * HEAD_DIM)
    for x in range(group):
        total = outer[body, :]
        for y in range(group):
            if y == x:
                continue
            ahead = (here ^ y) > (here ^ x) if reverse else (here ^ y) < (here ^ x)
            total = total + jnp.where(ahead, parts[y][body, :], 0.0)
        outs[x][...] = total


def attend_kernel(group, own, place, q, local, target, gain, mask, *refs):
    prior = refs[:group]
    attended, stats = refs[group:]
    length = q.shape[0]
    squares = jnp.zeros((length, HEAD_DIM), f32)
    dots = jnp.zeros((length, HEAD_DIM), f32)
    for x in range(group):
        for i in range(own):
            cols = head_cols((place[0] ^ x) * own + i)
            a = local[:, cols] + dot3(split(q[:, cols]), split(prior[x][rows_of(i), :]), NN)
            attended[:, cols] = a
            squares = squares + a * a
            dots = dots + gain[:, cols] * target[:, cols] * a
    stats[0:1, :] = jnp.sum(squares.T, axis=0, keepdims=True)
    stats[1:2, :] = jnp.sum(dots.T, axis=0, keepdims=True) * mask[...].astype(f32)
    stats[2:, :] = jnp.zeros((TAIL - 2, length), f32)


def grad_kernel(group, own, width, tokens, place, q, attended, target, gain, mask, count, *refs):
    n_stats = len(refs) - group - 1
    total = pair_sum([r[...] for r in refs[:n_stats]])
    grad = refs[n_stats]
    out = refs[n_stats + 1 :]
    length = q.shape[0]
    squares, dots = total[0:1, :], total[1:2, :]
    inverse_rms = lax.rsqrt(squares / width + epsilon)
    loss = jnp.sum(inverse_rms * dots)
    scale = tokens / count[0:1, :]
    left = scale * inverse_rms
    right = left * (inverse_rms * inverse_rms * dots / width)
    left = jnp.broadcast_to(left * mask[...].astype(f32), (length, length)).T
    right = jnp.broadcast_to(right, (length, length)).T
    for x in range(group):
        for i in range(own):
            cols = head_cols((place[0] ^ x) * own + i)
            g = left * (gain[:, cols] * target[:, cols]) - right * attended[:, cols]
            grad[:, cols] = g
            out[x][rows_of(i), :] = dot3(split(q[:, cols]), split(g), TN)
        out[x][own * HEAD_DIM :, :] = jnp.full((TAIL, HEAD_DIM), loss, f32)


def local_grad_kernel(group, own, place, q, k, v, grad, scores, *refs):
    prior = refs[:group]
    grad_q, grad_k, grad_v = refs[group:]
    causal = causal_mask(q.shape[0])
    for x in range(group):
        for i in range(own):
            h = (place[0] ^ x) * own + i
            cols = head_cols(h)
            g, kk = split(grad[:, cols]), split(k[:, cols])
            gs = split(jnp.where(causal, dot3(g, split(v[:, cols]), NT), 0.0))
            grad_q[:, cols] = dot3(gs, kk, NN) + dot3(g, split(prior[x][rows_of(i), :]), NT)
            grad_k[:, cols] = dot3(gs, split(q[:, cols]), TN)
            grad_v[:, cols] = dot3(split(scores[h]), g, TN)


def final_kernel(group, own, place, k, v, part_k, part_v, *refs):
    later = refs[:group]
    grad_k, grad_v = refs[group:]
    for x in range(group):
        for i in range(own):
            cols = head_cols((place[0] ^ x) * own + i)
            state = split(later[x][rows_of(i), :])
            grad_k[:, cols] = part_k[:, cols] + dot3(split(v[:, cols]), state, NT)
            grad_v[:, cols] = part_v[:, cols] + dot3(split(k[:, cols]), state, NN)


def swap(value, axis, step):
    count = lax.axis_size(axis)
    return lax.ppermute(value, axis, [(i, i ^ step) for i in range(count)])


def swap_all(parts, axis):
    return [parts[0]] + [swap(part, axis, x) for x, part in enumerate(parts) if x]


def scan_states(parts, group, own, place, reverse):
    count = lax.axis_size("seq")
    seat = lax.axis_index("seq")
    parts = swap_all(parts, "seq")
    rows = own * HEAD_DIM + TAIL
    (total,) = call(functools.partial(total_kernel, group), [shape(rows, HEAD_DIM)], group + 1, 0, place, *parts)
    outer = None
    step = group
    while step < count:
        other = swap(total, "seq", step)
        upper = (seat & step) != 0
        counts = jnp.logical_not(upper) if reverse else upper
        added = jnp.where(counts, other, 0.0)
        outer = added if outer is None else outer + added
        total = total + other
        step *= 2
    if outer is None:
        outer = jnp.zeros_like(total)
    spread = call(
        functools.partial(spread_kernel, group, own, reverse),
        [shape(own * HEAD_DIM, HEAD_DIM)] * group,
        group + 2,
        0,
        place,
        *parts,
        outer,
    )
    return swap_all(spread, "seq"), total[own * HEAD_DIM :, :]


def shards(queries, key_rows, value_rows, target, norm_gain, valid_mask):
    length, columns = queries.shape
    heads = columns // HEAD_DIM
    count, head_count = lax.axis_size("seq"), lax.axis_size("head")
    width, tokens = columns * head_count, length * count
    group = 1
    while group < 4 and count % (2 * group) == 0 and heads % (2 * group) == 0:
        group *= 2
    own = heads // group
    cube = 2 * HEAD_DIM**3 * heads
    place = jnp.reshape(lax.axis_index("seq") % group, (1,)).astype(jnp.int32)
    gain = norm_gain.reshape(1, columns)
    mask = valid_mask.reshape(1, length)
    state = shape(own * HEAD_DIM + TAIL, HEAD_DIM)
    wide = shape(length, columns)

    kv = call(functools.partial(state_kernel, group, own), [state] * group, 4, cube, place, key_rows, value_rows, mask)
    scores, local = call(
        functools.partial(local_kernel, heads),
        [shape(heads, length, length), wide],
        4,
        6 * cube,
        place,
        queries,
        key_rows,
        value_rows,
    )
    prior, token_total = scan_states(kv, group, own, place, False)
    attended, stats = call(
        functools.partial(attend_kernel, group, own),
        [wide, shape(TAIL, length)],
        6 + group,
        3 * cube,
        place,
        queries,
        local,
        target,
        gain,
        mask,
        *prior,
    )
    stats = swap_all([stats] * head_count, "head")
    grad, *outer = call(
        functools.partial(grad_kernel, group, own, width, tokens),
        [wide] + [state] * group,
        7 + head_count,
        3 * cube,
        place,
        queries,
        attended,
        target,
        gain,
        mask,
        token_total,
        *stats,
    )
    grad_query, part_key, part_value = call(
        functools.partial(local_grad_kernel, group, own),
        [wide] * 3,
        6 + group,
        15 * cube,
        place,
        queries,
        key_rows,
        value_rows,
        grad,
        scores,
        *prior,
    )
    later, loss_total = scan_states(outer, group, own, place, True)
    grad_key, grad_value = call(
        functools.partial(final_kernel, group, own),
        [wide] * 2,
        5 + group,
        6 * cube,
        place,
        key_rows,
        value_rows,
        part_key,
        part_value,
        *later,
    )
    loss_value = loss_total[0, 0] / token_total[0, 0]
    return (grad_query, grad_key, grad_value, loss_value)


def solution(mesh):
    return jax.shard_map(
        shards,
        mesh=mesh,
        in_specs=(
            P("seq", "head"),
            P("seq", "head"),
            P("seq", "head"),
            P("seq", "head"),
            P("head"),
            P("seq"),
        ),
        out_specs=(P("seq", "head"), P("seq", "head"), P("seq", "head"), P()),
        check_vma=False,
    )
```

time: 211 us -> 74.6 us (0.35)
  blocking collectives: 82.7 us -> 0 us
  waiting for transfers between devices: 72.4 us -> 30.5 us
  starting transfers between devices: 0.08 us -> 21.8 us
  matrix products: 17.5 us -> 0 us
  between operations: 17.4 us -> 3.87 us
  other arithmetic: 12.1 us -> 0.94 us
  Pallas kernels: 0 us -> 10.5 us
    psum x4 -> x0, blocking collectives: 82.7 us -> none  [the longest x1 46.2 us: shards(): loss_value = lax.psum(loss_local, ('seq', 'head')) / token_total]
    all_gather x2 -> x0, waiting for transfers between devices: 72.4 us -> none  [entering(): gathered = lax.all_gather(part, axis)]
    ppermute x0 -> x17, waiting for transfers between devices: none -> 30.5 us  [swap(): return lax.ppermute(value, axis, [(i, i ^ step) for i in range(count)])]
    ppermute x0 -> x17, starting transfers between devices: none -> 21.8 us  [swap(): return lax.ppermute(value, axis, [(i, i ^ step) for i in range(count)])]
    dot_general x12 -> x0, matrix products: 17.5 us -> none  [the longest x1 2.67 us: shards(): jnp.einsum('the,thf->hef', key_heads, value_heads, precision=highest)]
    pallas_call x0 -> x10, Pallas kernels: none -> 10.5 us  [call(): pl.pallas_call(kernel, out_shape=outs, in_specs=[pl.BlockSpec(memory_spac...]
    add x7 -> x1, other arithmetic: 8.28 us -> 0.02 us  [scan_states(): total = total + other]
    slice x0 -> x4, local copies, waits for them, and re-layouts: none -> 3.63 us  [the longest x3 3.63 us: shards(): loss_value = loss_total[0, 0] / token_total[0, 0]]
  transfers between devices with their start and end apart: 2 -> 17, of which waited for: 2 -> 12; matrix products, arithmetic and copies ran while one was open for 6% -> 5% of each run, Pallas kernels for 0% -> 8%
where the time goes in v1:
time: 74.6 us; the launch traced here: 74.2 us
  waiting for transfers between devices  30.5 us (41%)
  starting transfers between devices  21.8 us (29%)
  Pallas kernels  10.5 us (14%)
  local copies, waits for them, and re-layouts  6.53 us (9%)
  between operations  3.87 us (5%)
  other arithmetic  0.94 us (1%)
    ppermute x17, waiting for transfers between devices, swap(): return lax.ppermute(value, axis, [(i, i ^ step) for i in range(count)])  30.5 us
    ppermute x17, starting transfers between devices, swap(): return lax.ppermute(value, axis, [(i, i ^ step) for i in range(count)])  21.8 us
    pallas_call x10, Pallas kernels, call(): pl.pallas_call(kernel, out_shape=outs, in_specs=[pl.BlockSpec(memory_spac...  10.5 us
    slice x3, local copies, waits for them, and re-layouts, shards(): loss_value = loss_total[0, 0] / token_total[0, 0]  3.63 us
    unnamed x24, local copies, waits for them, and re-layouts  2.9 us
  transfers between devices with their start and end apart: 17, of which 12 were waited for; matrix products, arithmetic and copies ran while one was open for 5% of the time, Pallas kernels for 8%

profile of v1, /device:TPU:0, one launch (start us, length us, event | category | flops | bytes accessed | tf_op | source)
XLA Modules:
  0.0 74.2 jit_solution(1064099083832878450)
XLA Ops:
  3.8 3.0 %collective-permute-start = (f32[264,128]{1,0:T(8,128)S(1)}, f32[264,128]{1,0:T(8,128)S(1)}, u32[]{:S(2)}, u32[]{:S(2)}) collective-permute-start(f32[264,128]{1,0:T(8,128)S(1)} %get-tuple-element.32), channel_id=1, source_target_pairs={{0,4},{4,0},{8,12},{12,8},{16,20},{20,16},{24,28},{28,24},{1,5},{5... | collective-permute-start | bytes 405512 | tf_op jit(solution)/shard_map/ppermute | solution.py:174
  6.8 1.6 %collective-permute-start.1 = (f32[264,128]{1,0:T(8,128)S(1)}, f32[264,128]{1,0:T(8,128)S(1)}, u32[]{:S(2)}, u32[]{:S(2)}) collective-permute-start(f32[264,128]{1,0:T(8,128)S(1)} %get-tuple-element.33), channel_id=1, source_target_pairs={{0,8},{4,12},{8,0},{12,4},{16,24},{20,28},{24,16},{28,20},{1,9},{5... | collective-permute-start | bytes 405512 | tf_op jit(solution)/shard_map/ppermute | solution.py:174
  8.4 2.0 %collective-permute-done.refs_1_ = f32[264,128]{1,0:T(8,128)S(1)} collective-permute-done((f32[264,128]{1,0:T(8,128)S(1)}, f32[264,128]{1,0:T(8,128)S(1)}, u32[]{:S(2)}, u32[]{:S(2)}) %collective-permute-start) | collective-permute-done | bytes 135200 | tf_op jit(solution)/shard_map/ppermute | solution.py:174
  10.4 2.9 %collective-permute-done.1.refs_2_ = f32[264,128]{1,0:T(8,128)S(1)} collective-permute-done((f32[264,128]{1,0:T(8,128)S(1)}, f32[264,128]{1,0:T(8,128)S(1)}, u32[]{:S(2)}, u32[]{:S(2)}) %collective-permute-start.1) | collective-permute-done | bytes 135200 | tf_op jit(solution)/shard_map/ppermute | solution.py:174
  13.3 1.2 %collective-permute-done.2.refs_3_ = f32[264,128]{1,0:T(8,128)S(1)} collective-permute-done((f32[264,128]{1,0:T(8,128)S(1)}, f32[264,128]{1,0:T(8,128)S(1)}, u32[]{:S(2)}, u32[]{:S(2)}) %collective-permute-start.2) | collective-permute-done | bytes 135200 | tf_op jit(solution)/shard_map/ppermute | solution.py:174
  14.6 2.8 %collective-permute-start.3 = (f32[264,128]{1,0:T(8,128)S(1)}, f32[264,128]{1,0:T(8,128)S(1)}, u32[]{:S(2)}, u32[]{:S(2)}) collective-permute-start(f32[264,128]{1,0:T(8,128)S(1)} %shard_map.95), channel_id=1, source_target_pairs={{0,16},{4,20},{8,24},{12,28},{16,0},{20,4},{24,8},{28,12},{1,17},{... | collective-permute-start | bytes 405512 | tf_op jit(solution)/shard_map/ppermute | solution.py:174
  17.4 5.6 %collective-permute-done.3 = f32[264,128]{1,0:T(8,128)S(1)} collective-permute-done((f32[264,128]{1,0:T(8,128)S(1)}, f32[264,128]{1,0:T(8,128)S(1)}, u32[]{:S(2)}, u32[]{:S(2)}) %collective-permute-start.3) | collective-permute-done | bytes 135200 | tf_op jit(solution)/shard_map/ppermute | solution.py:174
  24.9 1.9 %collective-permute-start.6 = (f32[256,128]{1,0:T(8,128)S(1)}, f32[256,128]{1,0:T(8,128)S(1)}, u32[]{:S(2)}, u32[]{:S(2)}) collective-permute-start(f32[256,128]{1,0:T(8,128)S(1)} %get-tuple-element.38), channel_id=1, source_target_pairs={{0,12},{4,8},{8,4},{12,0},{16,28},{20,24},{24,20},{28,16},{1,13},{... | collective-permute-start | bytes 393224 | tf_op jit(solution)/shard_map/ppermute | solution.py:174
  26.8 2.2 %shard_map.93 = (f32[8,128,128]{2,1,0:T(8,128)S(1)}, f32[128,1024]{1,0:T(8,128)S(1)}) custom-call(s32[1]{0:T(128)} %bitcast.place, f32[128,1024]{1,0:T(8,128)S(1)} %copy-done.4, f32[128,1024]{1,0:T(8,128)S(1)} %copy-done.1, f32[128,1024]{1,0:T(8,128)S(1)} %copy-done.3), custom_call_target="tpu_custom_call" | custom-call | flops 201326592 | bytes 2621444 | tf_op jit(solution)/shard_map/pallas_call | solution.py:42
  29.7 2.5 %collective-permute-done.6.refs_3_ = f32[256,128]{1,0:T(8,128)S(1)} collective-permute-done((f32[256,128]{1,0:T(8,128)S(1)}, f32[256,128]{1,0:T(8,128)S(1)}, u32[]{:S(2)}, u32[]{:S(2)}) %collective-permute-start.6) | collective-permute-done | bytes 131104 | tf_op jit(solution)/shard_map/ppermute | solution.py:174
  32.9 1.5 %collective-permute-start.8 = (f32[8,128]{1,0:T(8,128)S(1)}, f32[8,128]{1,0:T(8,128)S(1)}, u32[]{:S(2)}, u32[]{:S(2)}) collective-permute-start(f32[8,128]{1,0:T(8,128)S(1)} %get-tuple-element.40.refs_0_), channel_id=1, source_target_pairs={{0,2},{1,3},{2,0},{3,1},{4,6},{5,7},{6,4},{7,5},{8,10},{9,11},{10,... | collective-permute-start | bytes 12296 | tf_op jit(solution)/shard_map/ppermute | solution.py:174
  34.8 1.8 %collective-permute-done.8.refs_2_ = f32[8,128]{1,0:T(8,128)S(1)} collective-permute-done((f32[8,128]{1,0:T(8,128)S(1)}, f32[8,128]{1,0:T(8,128)S(1)}, u32[]{:S(2)}, u32[]{:S(2)}) %collective-permute-start.8) | collective-permute-done | bytes 4128 | tf_op jit(solution)/shard_map/ppermute | solution.py:174
  38.5 1.4 %collective-permute-start.11 = (f32[264,128]{1,0:T(8,128)S(1)}, f32[264,128]{1,0:T(8,128)S(1)}, u32[]{:S(2)}, u32[]{:S(2)}) collective-permute-start(f32[264,128]{1,0:T(8,128)S(1)} %get-tuple-element.48), channel_id=1, source_target_pairs={{0,8},{4,12},{8,0},{12,4},{16,24},{20,28},{24,16},{28,20},{1,9},{5... | collective-permute-start | bytes 405512 | tf_op jit(solution)/shard_map/ppermute | solution.py:174
  39.9 1.7 %collective-permute-start.12 = (f32[264,128]{1,0:T(8,128)S(1)}, f32[264,128]{1,0:T(8,128)S(1)}, u32[]{:S(2)}, u32[]{:S(2)}) collective-permute-start(f32[264,128]{1,0:T(8,128)S(1)} %get-tuple-element.49), channel_id=1, source_target_pairs={{0,12},{4,8},{8,4},{12,0},{16,28},{20,24},{24,20},{28,16},{1,13},{... | collective-permute-start | bytes 405512 | tf_op jit(solution)/shard_map/ppermute | solution.py:174
  41.6 2.2 %collective-permute-done.10.refs_1_ = f32[264,128]{1,0:T(8,128)S(1)} collective-permute-done((f32[264,128]{1,0:T(8,128)S(1)}, f32[264,128]{1,0:T(8,128)S(1)}, u32[]{:S(2)}, u32[]{:S(2)}) %collective-permute-start.10) | collective-permute-done | bytes 135200 | tf_op jit(solution)/shard_map/ppermute | solution.py:174
  44.9 3.0 %collective-permute-done.12.refs_3_ = f32[264,128]{1,0:T(8,128)S(1)} collective-permute-done((f32[264,128]{1,0:T(8,128)S(1)}, f32[264,128]{1,0:T(8,128)S(1)}, u32[]{:S(2)}, u32[]{:S(2)}) %collective-permute-start.12) | collective-permute-done | bytes 135200 | tf_op jit(solution)/shard_map/ppermute | solution.py:174
  48.6 1.9 %collective-permute-start.13 = (f32[264,128]{1,0:T(8,128)}, f32[264,128]{1,0:T(8,128)}, u32[]{:S(2)}, u32[]{:S(2)}) collective-permute-start(f32[264,128]{1,0:T(8,128)} %shard_map.100), channel_id=1, source_target_pairs={{0,16},{4,20},{8,24},{12,28},{16,0},{20,4},{24,8},{28,12},{1,17},{... | collective-permute-start | bytes 405512 | tf_op jit(solution)/shard_map/ppermute | solution.py:174
  50.5 6.6 %collective-permute-done.13 = f32[264,128]{1,0:T(8,128)} collective-permute-done((f32[264,128]{1,0:T(8,128)}, f32[264,128]{1,0:T(8,128)}, u32[]{:S(2)}, u32[]{:S(2)}) %collective-permute-start.13) | collective-permute-done | bytes 135200 | tf_op jit(solution)/shard_map/ppermute | solution.py:174
  59.2 2.4 %collective-permute-start.16 = (f32[256,128]{1,0:T(8,128)S(1)}, f32[256,128]{1,0:T(8,128)S(1)}, u32[]{:S(2)}, u32[]{:S(2)}) collective-permute-start(f32[256,128]{1,0:T(8,128)S(1)} %get-tuple-element.53), channel_id=1, source_target_pairs={{0,12},{4,8},{8,4},{12,0},{16,28},{20,24},{24,20},{28,16},{1,13},{... | collective-permute-start | bytes 393224 | tf_op jit(solution)/shard_map/ppermute | solution.py:174
  61.6 1.3 %slice.18 = f32[1,1]{1,0:T(1,128)} slice(f32[264,128]{1,0:T(8,128)} %copy-done.11), slice={[256:257], [0:1]} | slice | bytes 8 | tf_op jit(solution)/shard_map/slice | solution.py:293
  62.9 4.0 %shard_map.99 = (f32[128,1024]{1,0:T(8,128)}, f32[128,1024]{1,0:T(8,128)S(1)}, f32[128,1024]{1,0:T(8,128)S(1)}) custom-call(s32[1]{0:T(128)} %bitcast.place, f32[128,1024]{1,0:T(8,128)S(1)} %copy-done.4, f32[128,1024]{1,0:T(8,128)S(1)} %copy-done.1, f32[128,1024]{1,0:T(8,128)S(1)} %copy-done.3, f32[128,1024]{1,0:T(8,128)S(1)} %get-tuple-element.41.grad, ...), custom_call_target="tpu_custom_call" | custom-call | flops 503316480 | bytes 4718596 | tf_op jit(solution)/shard_map/pallas_call | solution.py:42
  66.9 1.2 %slice.16 = f32[1,1]{1,0:T(1,128)} slice(f32[264,128]{1,0:T(8,128)} %shard_map.100), slice={[256:257], [0:1]} | slice | bytes 8 | tf_op jit(solution)/shard_map/slice | solution.py:293
  68.1 1.2 %slice.17 = f32[1,1]{1,0:T(1,128)} slice(f32[264,128]{1,0:T(8,128)} %collective-permute-done.13), slice={[256:257], [0:1]} | slice | bytes 8 | tf_op jit(solution)/shard_map/slice | solution.py:293
  71.3 1.8 %shard_map.102 = (f32[128,1024]{1,0:T(8,128)}, f32[128,1024]{1,0:T(8,128)}) custom-call(s32[1]{0:T(128)} %bitcast.place, f32[128,1024]{1,0:T(8,128)S(1)} %copy-done.1, f32[128,1024]{1,0:T(8,128)S(1)} %copy-done.3, f32[128,1024]{1,0:T(8,128)S(1)} %get-tuple-element.44.part_k, f32[128,1024]{1,0:T(8,128)S(1)} %get-tuple-element.45.part_v, ...), custom_call_target="tpu_custom_call" | custom-call | flops 201326592 | bytes 3670020 | tf_op jit(solution)/shard_map/pallas_call | solution.py:42
  (50 shorter events, 12.6 us)
Async XLA Ops:
  3.8 6.6 %collective-permute-start = (f32[264,128]{1,0:T(8,128)S(1)}, f32[264,128]{1,0:T(8,128)S(1)}, u32[]{:S(2)}, u32[]{:S(2)}) collective-permute-start(f32[264,128]{1,0:T(8,128)S(1)} %get-tuple-element.32), channel_id=1, source_target_pairs={{0,4},{4,0},{8,12},{12,8},{16,20},{20,16},{24,28},{28,24},{1,5},{5... | collective-permute-start | bytes 405512 | tf_op jit(solution)/shard_map/ppermute | solution.py:174
  6.8 6.5 %collective-permute-start.1 = (f32[264,128]{1,0:T(8,128)S(1)}, f32[264,128]{1,0:T(8,128)S(1)}, u32[]{:S(2)}, u32[]{:S(2)}) collective-permute-start(f32[264,128]{1,0:T(8,128)S(1)} %get-tuple-element.33), channel_id=1, source_target_pairs={{0,8},{4,12},{8,0},{12,4},{16,24},{20,28},{24,16},{28,20},{1,9},{5... | collective-permute-start | bytes 405512 | tf_op jit(solution)/shard_map/ppermute | solution.py:174
  8.4 6.2 %collective-permute-start.2 = (f32[264,128]{1,0:T(8,128)S(1)}, f32[264,128]{1,0:T(8,128)S(1)}, u32[]{:S(2)}, u32[]{:S(2)}) collective-permute-start(f32[264,128]{1,0:T(8,128)S(1)} %get-tuple-element.34), channel_id=1, source_target_pairs={{0,12},{4,8},{8,4},{12,0},{16,28},{20,24},{24,20},{28,16},{1,13},{... | collective-permute-start | bytes 405512 | tf_op jit(solution)/shard_map/ppermute | solution.py:174
  14.6 12.2 %copy-start.4 = (f32[128,1024]{1,0:T(8,128)S(1)}, f32[128,1024]{1,0:T(8,128)}, u32[]{:S(2)}) copy-start(f32[128,1024]{1,0:T(8,128)} %q.7) | copy-start | bytes 1572868
  14.6 8.4 %collective-permute-start.3 = (f32[264,128]{1,0:T(8,128)S(1)}, f32[264,128]{1,0:T(8,128)S(1)}, u32[]{:S(2)}, u32[]{:S(2)}) collective-permute-start(f32[264,128]{1,0:T(8,128)S(1)} %shard_map.95), channel_id=1, source_target_pairs={{0,16},{4,20},{8,24},{12,28},{16,0},{20,4},{24,8},{28,12},{1,17},{... | collective-permute-start | bytes 405512 | tf_op jit(solution)/shard_map/ppermute | solution.py:174
  17.4 9.4 %copy-start.1 = (f32[128,1024]{1,0:T(8,128)S(1)}, f32[128,1024]{1,0:T(8,128)}, u32[]{:S(2)}) copy-start(f32[128,1024]{1,0:T(8,128)} %k.7) | copy-start | bytes 1572868
  17.4 9.4 %copy-start.3 = (f32[128,1024]{1,0:T(8,128)S(1)}, f32[128,1024]{1,0:T(8,128)}, u32[]{:S(2)}) copy-start(f32[128,1024]{1,0:T(8,128)} %v.7) | copy-start | bytes 1572868
  23.1 11.7 %copy-start.11 = (f32[264,128]{1,0:T(8,128)}, f32[264,128]{1,0:T(8,128)S(1)}, u32[]{:S(2)}) copy-start(f32[264,128]{1,0:T(8,128)S(1)} %get-tuple-element.56) | copy-start | bytes 405508
  23.2 5.8 %collective-permute-start.4 = (f32[256,128]{1,0:T(8,128)S(1)}, f32[256,128]{1,0:T(8,128)S(1)}, u32[]{:S(2)}, u32[]{:S(2)}) collective-permute-start(f32[256,128]{1,0:T(8,128)S(1)} %get-tuple-element.36), channel_id=1, source_target_pairs={{0,4},{4,0},{8,12},{12,8},{16,20},{20,16},{24,28},{28,24},{1,5},{5... | collective-permute-start | bytes 393224 | tf_op jit(solution)/shard_map/ppermute | solution.py:174
  24.2 5.5 %collective-permute-start.5 = (f32[256,128]{1,0:T(8,128)S(1)}, f32[256,128]{1,0:T(8,128)S(1)}, u32[]{:S(2)}, u32[]{:S(2)}) collective-permute-start(f32[256,128]{1,0:T(8,128)S(1)} %get-tuple-element.37), channel_id=1, source_target_pairs={{0,8},{4,12},{8,0},{12,4},{16,24},{20,28},{24,16},{28,20},{1,9},{5... | collective-permute-start | bytes 393224 | tf_op jit(solution)/shard_map/ppermute | solution.py:174
  24.9 7.4 %copy-start.5 = (f32[128,1024]{1,0:T(8,128)S(1)}, f32[128,1024]{1,0:T(8,128)}, u32[]{:S(2)}) copy-start(f32[128,1024]{1,0:T(8,128)} %target.3) | copy-start | bytes 1572868
  24.9 7.4 %collective-permute-start.6 = (f32[256,128]{1,0:T(8,128)S(1)}, f32[256,128]{1,0:T(8,128)S(1)}, u32[]{:S(2)}, u32[]{:S(2)}) collective-permute-start(f32[256,128]{1,0:T(8,128)S(1)} %get-tuple-element.38), channel_id=1, source_target_pairs={{0,12},{4,8},{8,4},{12,0},{16,28},{20,24},{24,20},{28,16},{1,13},{... | collective-permute-start | bytes 393224 | tf_op jit(solution)/shard_map/ppermute | solution.py:174
  29.0 3.2 %copy-start.8 = (f32[1024]{0:T(1024)S(1)}, f32[1024]{0:T(1024)}, u32[]{:S(2)}) copy-start(f32[1024]{0:T(1024)} %param.10) | copy-start | bytes 12292
  32.9 1.9 %collective-permute-start.7 = (f32[8,128]{1,0:T(8,128)S(1)}, f32[8,128]{1,0:T(8,128)S(1)}, u32[]{:S(2)}, u32[]{:S(2)}) collective-permute-start(f32[8,128]{1,0:T(8,128)S(1)} %get-tuple-element.40.refs_0_), channel_id=1, source_target_pairs={{0,1},{1,0},{2,3},{3,2},{4,5},{5,4},{6,7},{7,6},{8,9},{9,8},{10,11... | collective-permute-start | bytes 12296 | tf_op jit(solution)/shard_map/ppermute | solution.py:174
  32.9 3.6 %collective-permute-start.8 = (f32[8,128]{1,0:T(8,128)S(1)}, f32[8,128]{1,0:T(8,128)S(1)}, u32[]{:S(2)}, u32[]{:S(2)}) collective-permute-start(f32[8,128]{1,0:T(8,128)S(1)} %get-tuple-element.40.refs_0_), channel_id=1, source_target_pairs={{0,2},{1,3},{2,0},{3,1},{4,6},{5,7},{6,4},{7,5},{8,10},{9,11},{10,... | collective-permute-start | bytes 12296 | tf_op jit(solution)/shard_map/ppermute | solution.py:174
  34.4 3.0 %collective-permute-start.9 = (f32[8,128]{1,0:T(8,128)S(1)}, f32[8,128]{1,0:T(8,128)S(1)}, u32[]{:S(2)}, u32[]{:S(2)}) collective-permute-start(f32[8,128]{1,0:T(8,128)S(1)} %get-tuple-element.40.refs_0_), channel_id=1, source_target_pairs={{0,3},{1,2},{2,1},{3,0},{4,7},{5,6},{6,5},{7,4},{8,11},{9,10},{10,... | collective-permute-start | bytes 12296 | tf_op jit(solution)/shard_map/ppermute | solution.py:174
  38.0 5.8 %collective-permute-start.10 = (f32[264,128]{1,0:T(8,128)S(1)}, f32[264,128]{1,0:T(8,128)S(1)}, u32[]{:S(2)}, u32[]{:S(2)}) collective-permute-start(f32[264,128]{1,0:T(8,128)S(1)} %get-tuple-element.47), channel_id=1, source_target_pairs={{0,4},{4,0},{8,12},{12,8},{16,20},{20,16},{24,28},{28,24},{1,5},{5... | collective-permute-start | bytes 405512 | tf_op jit(solution)/shard_map/ppermute | solution.py:174
  38.5 6.5 %collective-permute-start.11 = (f32[264,128]{1,0:T(8,128)S(1)}, f32[264,128]{1,0:T(8,128)S(1)}, u32[]{:S(2)}, u32[]{:S(2)}) collective-permute-start(f32[264,128]{1,0:T(8,128)S(1)} %get-tuple-element.48), channel_id=1, source_target_pairs={{0,8},{4,12},{8,0},{12,4},{16,24},{20,28},{24,16},{28,20},{1,9},{5... | collective-permute-start | bytes 405512 | tf_op jit(solution)/shard_map/ppermute | solution.py:174
  39.9 8.0 %collective-permute-start.12 = (f32[264,128]{1,0:T(8,128)S(1)}, f32[264,128]{1,0:T(8,128)S(1)}, u32[]{:S(2)}, u32[]{:S(2)}) collective-permute-start(f32[264,128]{1,0:T(8,128)S(1)} %get-tuple-element.49), channel_id=1, source_target_pairs={{0,12},{4,8},{8,4},{12,0},{16,28},{20,24},{24,20},{28,16},{1,13},{... | collective-permute-start | bytes 405512 | tf_op jit(solution)/shard_map/ppermute | solution.py:174
  48.6 8.4 %collective-permute-start.13 = (f32[264,128]{1,0:T(8,128)}, f32[264,128]{1,0:T(8,128)}, u32[]{:S(2)}, u32[]{:S(2)}) collective-permute-start(f32[264,128]{1,0:T(8,128)} %shard_map.100), channel_id=1, source_target_pairs={{0,16},{4,20},{8,24},{12,28},{16,0},{20,4},{24,8},{28,12},{1,17},{... | collective-permute-start | bytes 405512 | tf_op jit(solution)/shard_map/ppermute | solution.py:174
  57.9 5.0 %copy-start.7 = (f32[256,128]{1,0:T(8,128)S(1)}, f32[256,128]{1,0:T(8,128)}, u32[]{:S(2)}) copy-start(f32[256,128]{1,0:T(8,128)} %copy-done.6) | copy-start | bytes 393220
  58.1 13.2 %collective-permute-start.14 = (f32[256,128]{1,0:T(8,128)S(1)}, f32[256,128]{1,0:T(8,128)S(1)}, u32[]{:S(2)}, u32[]{:S(2)}) collective-permute-start(f32[256,128]{1,0:T(8,128)S(1)} %get-tuple-element.51), channel_id=1, source_target_pairs={{0,4},{4,0},{8,12},{12,8},{16,20},{20,16},{24,28},{28,24},{1,5},{5... | collective-permute-start | bytes 393224 | tf_op jit(solution)/shard_map/ppermute | solution.py:174
  58.8 12.5 %collective-permute-start.15 = (f32[256,128]{1,0:T(8,128)S(1)}, f32[256,128]{1,0:T(8,128)S(1)}, u32[]{:S(2)}, u32[]{:S(2)}) collective-permute-start(f32[256,128]{1,0:T(8,128)S(1)} %get-tuple-element.52), channel_id=1, source_target_pairs={{0,8},{4,12},{8,0},{12,4},{16,24},{20,28},{24,16},{28,20},{1,9},{5... | collective-permute-start | bytes 393224 | tf_op jit(solution)/shard_map/ppermute | solution.py:174
  59.2 12.0 %collective-permute-start.16 = (f32[256,128]{1,0:T(8,128)S(1)}, f32[256,128]{1,0:T(8,128)S(1)}, u32[]{:S(2)}, u32[]{:S(2)}) collective-permute-start(f32[256,128]{1,0:T(8,128)S(1)} %get-tuple-element.53), channel_id=1, source_target_pairs={{0,12},{4,8},{8,4},{12,0},{16,28},{20,24},{24,20},{28,16},{1,13},{... | collective-permute-start | bytes 393224 | tf_op jit(solution)/shard_map/ppermute | solution.py:174
  (5 other events, 6.1 us)

commit v2 on v0

v2 whole, which is shorter than its diff:
```python
import functools

import jax
import jax.numpy as jnp
from jax import lax
from jax.experimental import pallas as pl
from jax.experimental.pallas import tpu as pltpu
from jax.sharding import PartitionSpec as P

HEAD_DIM = 128
TAIL = 8
epsilon = 1e-06
f32 = jnp.float32
bf16 = jnp.bfloat16
SMEM = pl.BlockSpec(memory_space=pltpu.SMEM)
VMEM = pl.BlockSpec(memory_space=pltpu.VMEM)
ANY = pl.BlockSpec(memory_space=pl.ANY)

NN = ((1,), (0,))
NT = ((1,), (1,))
TN = ((0,), (0,))


def split(x):
    high = x.astype(bf16)
    return high, (x - high.astype(f32)).astype(bf16)


def dot3(a, b, dims):
    d = functools.partial(lax.dot_general, dimension_numbers=(dims, ((), ())), preferred_element_type=f32)
    return d(a[0], b[0]) + (d(a[0], b[1]) + d(a[1], b[0]))


def head_cols(h):
    return pl.ds(pl.multiple_of(h * HEAD_DIM, HEAD_DIM), HEAD_DIM)


def rows_of(i):
    return slice(i * HEAD_DIM, (i + 1) * HEAD_DIM)


def in_hbm(x):
    return pltpu.with_memory_space_constraint(x, pltpu.HBM)


def shape(*s):
    return jax.ShapeDtypeStruct(s, f32)


def call(kernel, outs, flops, seat, *args, specs=None, out_specs=None, scratch=(), limit=24):
    specs = specs or [VMEM] * len(args)
    nbytes = sum(a.size * 4 for a in args) + sum(o.size * 4 for o in outs)
    return pl.pallas_call(
        kernel,
        out_shape=outs,
        in_specs=[SMEM] + specs,
        out_specs=out_specs or [VMEM] * len(outs),
        scratch_shapes=scratch,
        compiler_params=pltpu.CompilerParams(vmem_limit_bytes=limit * 1024 * 1024),
        cost_estimate=pl.CostEstimate(flops=flops, bytes_accessed=nbytes, transcendentals=0),
    )(seat, *args)


def causal_mask(n):
    return lax.broadcasted_iota(jnp.int32, (n, n), 0) >= lax.broadcasted_iota(jnp.int32, (n, n), 1)


def column(row, n):
    return jnp.broadcast_to(row, (n, n)).T


def pair_sum(parts):
    parts = list(parts)
    while len(parts) > 1:
        parts = [parts[i] + parts[i + 1] for i in range(0, len(parts), 2)]
    return parts[0]


class Plan:
    def __init__(self, length, heads, seq, head):
        group = 1
        while group < 4 and seq % (2 * group) == 0 and heads % (2 * group) == 0:
            group *= 2
        self.length, self.heads, self.head, self.group, self.own = length, heads, head, group, heads // group
        self.width, self.tokens = heads * HEAD_DIM * head, length * seq
        self.swaps = [group << i for i in range(30) if group << i < seq]
        self.state_rows = self.own * HEAD_DIM
        self.part_rows = self.own * length
        self.body = slice(0, self.state_rows)
        self.tail = slice(self.state_rows, self.state_rows + TAIL)

    def head_of(self, seat, x, i):
        return (seat % self.group ^ x) * self.own + i

    def piece(self, i):
        return slice(i * self.length, (i + 1) * self.length)


def outer_sum(plan, seat, reverse, totals):
    total = jnp.zeros((plan.state_rows, HEAD_DIM), f32)
    for step, other in zip(plan.swaps, totals):
        upper = (seat & step) != 0
        counts = jnp.logical_not(upper) if reverse else upper
        total = total + jnp.where(counts, other[plan.body, :], 0.0)
    return total


def state_at(plan, seat, reverse, x, outer, parts):
    here = seat % plan.group
    total = outer
    for y in range(plan.group):
        if y != x:
            ahead = (here ^ y) > (here ^ x) if reverse else (here ^ y) < (here ^ x)
            total = total + jnp.where(ahead, parts[y][plan.body, :], 0.0)
    return total


def full_count(plan, totals):
    count = totals[0][plan.tail, :]
    for other in totals[1:]:
        count = count + other[plan.tail, :]
    return count[0:1, :]


def state_kernel(plan, seat, k_hbm, v_hbm, mask, *refs):
    group, own = plan.group, plan.own
    out, (k, v, sems) = refs[:group], refs[group:]
    here = seat[0] % group
    order = [x for x in range(1, group)] + [0]
    copies = {}
    for x in order:
        cols = pl.ds(pl.multiple_of((here ^ x) * (own * HEAD_DIM), HEAD_DIM), own * HEAD_DIM)
        copies[x] = [
            pltpu.make_async_copy(src.at[:, cols], dst.at[x], sems.at[i, x])
            for i, (src, dst) in enumerate(((k_hbm, k), (v_hbm, v)))
        ]
        for copy in copies[x]:
            copy.start()
    count = jnp.sum(mask[...].astype(f32))
    for x in order:
        for copy in copies[x]:
            copy.wait()
        for i in range(own):
            out[x][rows_of(i), :] = dot3(split(k[x, :, rows_of(i)]), split(v[x, :, rows_of(i)]), TN)
        out[x][plan.tail, :] = jnp.full((TAIL, HEAD_DIM), count, f32)


def local_kernel(plan, seat, q, k, v, target, gain, mask, scores, local, aim):
    causal = causal_mask(plan.length)
    valid = column(mask[...].astype(f32), plan.length)
    for h in range(plan.heads):
        cols = head_cols(h)
        s = dot3(split(q[:, cols]), split(k[:, cols]), NT)
        s = jnp.where(causal, s, 0.0)
        scores[h] = s
        local[:, cols] = dot3(split(s), split(v[:, cols]), NN)
        aim[:, cols] = valid * (gain[:, cols] * target[:, cols])


def total_kernel(plan, seat, *refs):
    refs[-1][...] = pair_sum(r[...] for r in refs[: plan.group])


def prior_kernel(plan, seat, *refs):
    group = plan.group
    parts, totals, outs = refs[:group], refs[group : -group], refs[-group:]
    outer = outer_sum(plan, seat[0], False, totals)
    for x in range(group):
        outs[x][...] = state_at(plan, seat[0], False, x, outer, parts)


def attend_kernel(plan, seat, q, local, aim, *refs):
    priors, (attended, stats) = refs[: plan.group], refs[plan.group :]
    squares = jnp.zeros((plan.length, HEAD_DIM), f32)
    dots = jnp.zeros((plan.length, HEAD_DIM), f32)
    for x in range(plan.group):
        for i in range(plan.own):
            cols = head_cols(plan.head_of(seat[0], x, i))
            a = local[:, cols] + dot3(split(q[:, cols]), split(priors[x][rows_of(i), :]), NN)
            attended[:, cols] = a
            squares = squares + a * a
            dots = dots + aim[:, cols] * a
    stats[0:1, :] = jnp.sum(squares.T, axis=0, keepdims=True)
    stats[1:2, :] = jnp.sum(dots.T, axis=0, keepdims=True)
    stats[2:, :] = jnp.zeros((TAIL - 2, plan.length), f32)


def scales(plan, stats, row, count):
    squares, dots = stats[pl.ds(row, 1), :], stats[pl.ds(row + 1, 1), :]
    inverse_rms = lax.rsqrt(squares / plan.width + epsilon)
    left = (plan.tokens / count) * inverse_rms
    right = left * (inverse_rms * inverse_rms * dots / plan.width)
    return left, right, inverse_rms * dots


def grad_kernel(plan, seat, q, attended, aim, *refs):
    refs = list(refs)
    take = lambda n: [refs.pop(0) for _ in range(n)]
    totals, stat_parts, (grad,), out = take(1 + len(plan.swaps)), take(plan.head), take(1), take(plan.group)
    (stats,) = refs
    stats[...] = pair_sum(r[...] for r in stat_parts)
    left, right, losses = scales(plan, stats, 0, full_count(plan, totals))
    left, right = column(left, plan.length), column(right, plan.length)
    loss = jnp.sum(losses)
    for x in range(plan.group):
        for i in range(plan.own):
            cols = head_cols(plan.head_of(seat[0], x, i))
            g = left * aim[:, cols] - right * attended[:, cols]
            grad[:, cols] = g
            out[x][rows_of(i), :] = dot3(split(q[:, cols]), split(g), TN)
        out[x][plan.tail, :] = jnp.full((TAIL, HEAD_DIM), loss, f32)


def local_grad_kernel(plan, seat, q, k, v, grad, scores, *refs):
    priors, (grad_q, grad_k, grad_v) = refs[: plan.group], refs[plan.group :]
    causal = causal_mask(plan.length)
    for x in range(plan.group):
        for i in range(plan.own):
            h = plan.head_of(seat[0], x, i)
            cols = head_cols(h)
            g = split(grad[:, cols])
            gs = split(jnp.where(causal, dot3(g, split(v[:, cols]), NT), 0.0))
            prior = split(priors[x][rows_of(i), :])
            grad_q[:, cols] = dot3(gs, split(k[:, cols]), NN) + dot3(g, prior, NT)
            grad_k[:, cols] = dot3(gs, split(q[:, cols]), TN)
            grad_v[:, cols] = dot3(split(scores[h]), g, TN)


def later_kernel(plan, seat, *refs):
    group = plan.group
    refs = list(refs)
    take = lambda n: [refs.pop(0) for _ in range(n)]
    counts, states, totals = take(1 + len(plan.swaps)), take(group), take(1 + len(plan.swaps))
    take(1)
    outs, (loss,) = take(group), take(1)
    outer = outer_sum(plan, seat[0], True, totals[1:])
    for x in range(group):
        outs[x][...] = state_at(plan, seat[0], True, x, outer, states)
    loss[...] = (full_count(plan, totals) / full_count(plan, counts))[:, 0:1]


def final_kernel(plan, seat, k, v, part_k, part_v, *refs):
    later = refs[: plan.group]
    grad_k, grad_v = refs[plan.group :]
    for x in range(plan.group):
        for i in range(plan.own):
            cols = head_cols(plan.head_of(seat[0], x, i))
            state = split(later[x][rows_of(i), :])
            grad_k[:, cols] = part_k[:, cols] + dot3(split(v[:, cols]), state, NT)
            grad_v[:, cols] = part_v[:, cols] + dot3(split(k[:, cols]), state, NN)


def swap(value, axis, step):
    return lax.ppermute(value, axis, [(i, i ^ step) for i in range(lax.axis_size(axis))])


def swap_all(parts, axis):
    return [parts[0]] + [swap(part, axis, x) for x, part in enumerate(parts) if x]


def swap_totals(plan, total):
    totals = [total]
    for step in plan.swaps:
        totals.append(swap(total, "seq", step))
        if step != plan.swaps[-1]:
            total = total + totals[-1]
    return totals


def shards(queries, key_rows, value_rows, target, norm_gain, valid_mask):
    length, columns = queries.shape
    heads = columns // HEAD_DIM
    head_count = lax.axis_size("head")
    plan = Plan(length, heads, lax.axis_size("seq"), head_count)
    group, own = plan.group, plan.own
    product = 6 * HEAD_DIM**3 * heads
    seat = jnp.reshape(lax.axis_index("seq"), (1,)).astype(jnp.int32)
    gain = norm_gain.reshape(1, columns)
    mask = valid_mask.reshape(1, length)
    sum_shape = shape(plan.state_rows + TAIL, HEAD_DIM)
    state = shape(plan.state_rows, HEAD_DIM)
    piece = shape(plan.part_rows, HEAD_DIM)
    wide = shape(length, columns)
    bind = lambda kernel: functools.partial(kernel, plan)

    kv = call(
        bind(state_kernel),
        [sum_shape] * group,
        product,
        seat,
        in_hbm(key_rows),
        in_hbm(value_rows),
        in_hbm(mask),
        specs=[ANY, ANY, VMEM],
        scratch=[
            pltpu.VMEM((group, length, own * HEAD_DIM), f32),
            pltpu.VMEM((group, length, own * HEAD_DIM), f32),
            pltpu.SemaphoreType.DMA((2, group)),
        ],
    )
    scores, local, aim = call(
        bind(local_kernel),
        [shape(heads, length, length), wide, wide],
        2 * product,
        seat,
        queries,
        key_rows,
        value_rows,
        target,
        gain,
        mask,
    )
    kv = swap_all(kv, "seq")
    (total,) = call(bind(total_kernel), [sum_shape], 0, seat, *kv)
    totals = swap_totals(plan, total)
    priors = call(bind(prior_kernel), [state] * group, 0, seat, *kv, *totals[1:])
    priors = swap_all(priors, "seq")
    attended, stats = call(
        bind(attend_kernel),
        [wide, shape(TAIL, length)],
        product,
        seat,
        queries,
        local,
        aim,
        *priors,
    )
    stats = swap_all([stats] * head_count, "head")
    grad, *states = call(
        bind(grad_kernel),
        [wide] + [sum_shape] * group,
        product,
        seat,
        queries,
        attended,
        aim,
        *totals,
        *stats,
        scratch=[pltpu.VMEM((TAIL, length), f32)],
    )
    grad_query, part_key, part_value = call(
        bind(local_grad_kernel), [wide] * 3, 5 * product, seat, queries, key_rows, value_rows, grad, scores, *priors
    )
    states = swap_all(states, "seq")
    (grad_total,) = call(bind(total_kernel), [sum_shape], 0, seat, *states)
    grad_totals = swap_totals(plan, grad_total)
    *later, loss = call(
        bind(later_kernel),
        [state] * group + [shape(1, 1)],
        0,
        seat,
        *totals,
        *states,
        *grad_totals,
        part_key,
        specs=[VMEM] * (2 * len(totals) + group) + [ANY],
    )
    later = swap_all(later, "seq")
    grad_key, grad_value = call(
        bind(final_kernel), [wide] * 2, 2 * product, seat, key_rows, value_rows, part_key, part_value, *later
    )
    return (grad_query, grad_key, grad_value, loss[0, 0])


def solution(mesh):
    return jax.shard_map(
        shards,
        mesh=mesh,
        in_specs=(
            P("seq", "head"),
            P("seq", "head"),
            P("seq", "head"),
            P("seq", "head"),
            P("head"),
            P("seq"),
        ),
        out_specs=(P("seq", "head"), P("seq", "head"), P("seq", "head"), P()),
        check_vma=False,
    )
```

time: 211 us -> 67 us (0.32)
  blocking collectives: 82.7 us -> 0 us
  waiting for transfers between devices: 72.4 us -> 31.6 us
  starting transfers between devices: 0.08 us -> 21.9 us
  matrix products: 17.5 us -> 0 us
  between operations: 17.4 us -> 0.74 us
  Pallas kernels: 0 us -> 12.6 us
  other arithmetic: 12.1 us -> 0 us
  local copies, waits for them, and re-layouts: 8.04 us -> 0.03 us
    psum x4 -> x0, blocking collectives: 82.7 us -> none  [the longest x1 46.2 us: shards(): loss_value = lax.psum(loss_local, ('seq', 'head')) / token_total]
    all_gather x2 -> x0, waiting for transfers between devices: 72.4 us -> none  [entering(): gathered = lax.all_gather(part, axis)]
    ppermute x0 -> x17, waiting for transfers between devices: none -> 31.6 us  [swap(): lax.ppermute(value, axis, [(i, i ^ step) for i in range(lax.axis_size(axi...]
    ppermute x0 -> x17, starting transfers between devices: none -> 21.9 us  [swap(): lax.ppermute(value, axis, [(i, i ^ step) for i in range(lax.axis_size(axi...]
    dot_general x12 -> x0, matrix products: 17.5 us -> none  [the longest x1 2.67 us: shards(): jnp.einsum('the,thf->hef', key_heads, value_heads, precision=highest)]
    pallas_call x0 -> x10, Pallas kernels: none -> 12.6 us  [call(): pl.pallas_call(kernel, out_shape=outs, in_specs=[SMEM] + specs, out_specs...]
    add x7 -> x0, other arithmetic: 8.28 us -> none  [combine_sum(): return earlier + later]
    unnamed x22 -> x12, local copies, waits for them, and re-layouts: 6.36 us -> 0.03 us
  transfers between devices with their start and end apart: 2 -> 17, of which waited for: 2 -> 15; matrix products, arithmetic and copies ran while one was open for 6% -> 0% of each run, Pallas kernels for 0% -> 9%
where the time goes in v2:
time: 67 us; the launch traced here: 66.8 us
  waiting for transfers between devices  31.6 us (47%)
  starting transfers between devices  21.9 us (33%)
  Pallas kernels  12.6 us (19%)
  between operations  0.74 us (1%)
    ppermute x17, waiting for transfers between devices, swap(): lax.ppermute(value, axis, [(i, i ^ step) for i in range(lax.axis_size(axi...  31.6 us
    ppermute x17, starting transfers between devices, swap(): lax.ppermute(value, axis, [(i, i ^ step) for i in range(lax.axis_size(axi...  21.9 us
    pallas_call x10, Pallas kernels, call(): pl.pallas_call(kernel, out_shape=outs, in_specs=[SMEM] + specs, out_specs...  12.6 us
  transfers between devices with their start and end apart: 17, of which 15 were waited for; matrix products, arithmetic and copies ran while one was open for 0% of the time, Pallas kernels for 9%

profile of v2, /device:TPU:0, one launch (start us, length us, event | category | flops | bytes accessed | tf_op | source)
XLA Modules:
  0.0 66.8 jit_solution(1907821008881623794)
XLA Ops:
  0.7 2.8 %shard_map.94 = (f32[264,128]{1,0:T(8,128)S(1)}, f32[264,128]{1,0:T(8,128)S(1)}, f32[264,128]{1,0:T(8,128)S(1)}, f32[264,128]{1,0:T(8,128)S(1)}) custom-call(s32[1]{0:T(128)} %bitcast.seat, f32[128,1024]{1,0:T(8,128)} %k.5, f32[128,1024]{1,0:T(8,128)} %v.5, s32[1,128]{1,0:T(1,128)} %bitcast.5), custom_call_target="tpu_custom_call" | custom-call | flops 100663296 | bytes 1589760 | tf_op jit(solution)/shard_map/pallas_call | solution.py:53
  3.4 3.0 %collective-permute-start = (f32[264,128]{1,0:T(8,128)S(1)}, f32[264,128]{1,0:T(8,128)S(1)}, u32[]{:S(2)}, u32[]{:S(2)}) collective-permute-start(f32[264,128]{1,0:T(8,128)S(1)} %get-tuple-element.35), channel_id=1, source_target_pairs={{0,4},{4,0},{8,12},{12,8},{16,20},{20,16},{24,28},{28,24},{1,5},{5... | collective-permute-start | bytes 405512 | tf_op jit(solution)/shard_map/ppermute | solution.py:254
  6.5 1.6 %collective-permute-start.1 = (f32[264,128]{1,0:T(8,128)S(1)}, f32[264,128]{1,0:T(8,128)S(1)}, u32[]{:S(2)}, u32[]{:S(2)}) collective-permute-start(f32[264,128]{1,0:T(8,128)S(1)} %get-tuple-element.36), channel_id=1, source_target_pairs={{0,8},{4,12},{8,0},{12,4},{16,24},{20,28},{24,16},{28,20},{1,9},{5... | collective-permute-start | bytes 405512 | tf_op jit(solution)/shard_map/ppermute | solution.py:254
  8.0 2.0 %collective-permute-done.refs_1_ = f32[264,128]{1,0:T(8,128)S(1)} collective-permute-done((f32[264,128]{1,0:T(8,128)S(1)}, f32[264,128]{1,0:T(8,128)S(1)}, u32[]{:S(2)}, u32[]{:S(2)}) %collective-permute-start) | collective-permute-done | bytes 135200 | tf_op jit(solution)/shard_map/ppermute | solution.py:254
  10.0 2.9 %collective-permute-done.1.refs_2_ = f32[264,128]{1,0:T(8,128)S(1)} collective-permute-done((f32[264,128]{1,0:T(8,128)S(1)}, f32[264,128]{1,0:T(8,128)S(1)}, u32[]{:S(2)}, u32[]{:S(2)}) %collective-permute-start.1) | collective-permute-done | bytes 135200 | tf_op jit(solution)/shard_map/ppermute | solution.py:254
  12.9 1.2 %collective-permute-done.2.refs_3_ = f32[264,128]{1,0:T(8,128)S(1)} collective-permute-done((f32[264,128]{1,0:T(8,128)S(1)}, f32[264,128]{1,0:T(8,128)S(1)}, u32[]{:S(2)}, u32[]{:S(2)}) %collective-permute-start.2) | collective-permute-done | bytes 135200 | tf_op jit(solution)/shard_map/ppermute | solution.py:254
  14.2 2.8 %collective-permute-start.3 = (f32[264,128]{1,0:T(8,128)S(1)}, f32[264,128]{1,0:T(8,128)S(1)}, u32[]{:S(2)}, u32[]{:S(2)}) collective-permute-start(f32[264,128]{1,0:T(8,128)S(1)} %shard_map.95.refs_0_), channel_id=1, source_target_pairs={{0,16},{4,20},{8,24},{12,28},{16,0},{20,4},{24,8},{28,12},{1,17},{... | collective-permute-start | bytes 405512 | tf_op jit(solution)/shard_map/ppermute | solution.py:254
  17.0 5.6 %collective-permute-done.3.refs_4_.refs_1_ = f32[264,128]{1,0:T(8,128)S(1)} collective-permute-done((f32[264,128]{1,0:T(8,128)S(1)}, f32[264,128]{1,0:T(8,128)S(1)}, u32[]{:S(2)}, u32[]{:S(2)}) %collective-permute-start.3) | collective-permute-done | bytes 135200 | tf_op jit(solution)/shard_map/ppermute | solution.py:254
  24.5 1.9 %collective-permute-start.6 = (f32[256,128]{1,0:T(8,128)S(1)}, f32[256,128]{1,0:T(8,128)S(1)}, u32[]{:S(2)}, u32[]{:S(2)}) collective-permute-start(f32[256,128]{1,0:T(8,128)S(1)} %get-tuple-element.41), channel_id=1, source_target_pairs={{0,12},{4,8},{8,4},{12,0},{16,28},{20,24},{24,20},{28,16},{1,13},{... | collective-permute-start | bytes 393224 | tf_op jit(solution)/shard_map/ppermute | solution.py:254
  26.4 2.2 %shard_map.93 = (f32[8,128,128]{2,1,0:T(8,128)S(1)}, f32[128,1024]{1,0:T(8,128)S(1)}, f32[128,1024]{1,0:T(8,128)S(1)}) custom-call(s32[1]{0:T(128)} %bitcast.seat, f32[128,1024]{1,0:T(8,128)S(1)} %copy-done, f32[128,1024]{1,0:T(8,128)S(1)} %copy-done.1, f32[128,1024]{1,0:T(8,128)S(1)} %copy-done.2, f32[128,1024]{1,0:T(8,128)S(1)} %copy-done.3, ...), custom_call_target="tpu_custom_call" | custom-call | flops 201326592 | bytes 3674624 | tf_op jit(solution)/shard_map/pallas_call | solution.py:53
  29.3 2.5 %collective-permute-done.6.refs_3_ = f32[256,128]{1,0:T(8,128)S(1)} collective-permute-done((f32[256,128]{1,0:T(8,128)S(1)}, f32[256,128]{1,0:T(8,128)S(1)}, u32[]{:S(2)}, u32[]{:S(2)}) %collective-permute-start.6) | collective-permute-done | bytes 131104 | tf_op jit(solution)/shard_map/ppermute | solution.py:254
  32.4 1.6 %collective-permute-start.8 = (f32[8,128]{1,0:T(8,128)S(1)}, f32[8,128]{1,0:T(8,128)S(1)}, u32[]{:S(2)}, u32[]{:S(2)}) collective-permute-start(f32[8,128]{1,0:T(8,128)S(1)} %get-tuple-element.43.refs_2_), channel_id=1, source_target_pairs={{0,2},{1,3},{2,0},{3,1},{4,6},{5,7},{6,4},{7,5},{8,10},{9,11},{10,... | collective-permute-start | bytes 12296 | tf_op jit(solution)/shard_map/ppermute | solution.py:254
  37.1 1.4 %collective-permute-start.11 = (f32[264,128]{1,0:T(8,128)S(1)}, f32[264,128]{1,0:T(8,128)S(1)}, u32[]{:S(2)}, u32[]{:S(2)}) collective-permute-start(f32[264,128]{1,0:T(8,128)S(1)} %get-tuple-element.51), channel_id=1, source_target_pairs={{0,8},{4,12},{8,0},{12,4},{16,24},{20,28},{24,16},{28,20},{1,9},{5... | collective-permute-start | bytes 405512 | tf_op jit(solution)/shard_map/ppermute | solution.py:254
  38.5 1.7 %collective-permute-start.12 = (f32[264,128]{1,0:T(8,128)S(1)}, f32[264,128]{1,0:T(8,128)S(1)}, u32[]{:S(2)}, u32[]{:S(2)}) collective-permute-start(f32[264,128]{1,0:T(8,128)S(1)} %get-tuple-element.52), channel_id=1, source_target_pairs={{0,12},{4,8},{8,4},{12,0},{16,28},{20,24},{24,20},{28,16},{1,13},{... | collective-permute-start | bytes 405512 | tf_op jit(solution)/shard_map/ppermute | solution.py:254
  40.2 2.4 %collective-permute-done.10.refs_1_.refs_3_ = f32[264,128]{1,0:T(8,128)S(1)} collective-permute-done((f32[264,128]{1,0:T(8,128)S(1)}, f32[264,128]{1,0:T(8,128)S(1)}, u32[]{:S(2)}, u32[]{:S(2)}) %collective-permute-start.10) | collective-permute-done | bytes 135200 | tf_op jit(solution)/shard_map/ppermute | solution.py:254
  43.6 3.2 %collective-permute-done.12.refs_3_.refs_5_ = f32[264,128]{1,0:T(8,128)S(1)} collective-permute-done((f32[264,128]{1,0:T(8,128)S(1)}, f32[264,128]{1,0:T(8,128)S(1)}, u32[]{:S(2)}, u32[]{:S(2)}) %collective-permute-start.12) | collective-permute-done | bytes 135200 | tf_op jit(solution)/shard_map/ppermute | solution.py:254
  46.8 1.9 %collective-permute-start.13 = (f32[264,128]{1,0:T(8,128)S(1)}, f32[264,128]{1,0:T(8,128)S(1)}, u32[]{:S(2)}, u32[]{:S(2)}) collective-permute-start(f32[264,128]{1,0:T(8,128)S(1)} %shard_map.100.refs_6_), channel_id=1, source_target_pairs={{0,16},{4,20},{8,24},{12,28},{16,0},{20,4},{24,8},{28,12},{1,17},{... | collective-permute-start | bytes 405512 | tf_op jit(solution)/shard_map/ppermute | solution.py:254
  48.7 4.0 %shard_map.99 = (f32[128,1024]{1,0:T(8,128)}, f32[128,1024]{1,0:T(8,128)S(1)}, f32[128,1024]{1,0:T(8,128)S(1)}) custom-call(s32[1]{0:T(128)} %bitcast.seat, f32[128,1024]{1,0:T(8,128)S(1)} %copy-done, f32[128,1024]{1,0:T(8,128)S(1)} %copy-done.1, f32[128,1024]{1,0:T(8,128)S(1)} %copy-done.2, f32[128,1024]{1,0:T(8,128)S(1)} %get-tuple-element.44.grad, ...), custom_call_target="tpu_custom_call" | custom-call | flops 503316480 | bytes 4718592 | tf_op jit(solution)/shard_map/pallas_call | solution.py:53
  52.7 2.5 %collective-permute-done.13.refs_7_ = f32[264,128]{1,0:T(8,128)S(1)} collective-permute-done((f32[264,128]{1,0:T(8,128)S(1)}, f32[264,128]{1,0:T(8,128)S(1)}, u32[]{:S(2)}, u32[]{:S(2)}) %collective-permute-start.13) | collective-permute-done | bytes 135200 | tf_op jit(solution)/shard_map/ppermute | solution.py:254
  56.7 2.5 %collective-permute-start.16 = (f32[256,128]{1,0:T(8,128)S(1)}, f32[256,128]{1,0:T(8,128)S(1)}, u32[]{:S(2)}, u32[]{:S(2)}) collective-permute-start(f32[256,128]{1,0:T(8,128)S(1)} %get-tuple-element.56), channel_id=1, source_target_pairs={{0,12},{4,8},{8,4},{12,0},{16,28},{20,24},{24,20},{28,16},{1,13},{... | collective-permute-start | bytes 393224 | tf_op jit(solution)/shard_map/ppermute | solution.py:254
  59.2 2.0 %collective-permute-done.14.refs_1_ = f32[256,128]{1,0:T(8,128)S(1)} collective-permute-done((f32[256,128]{1,0:T(8,128)S(1)}, f32[256,128]{1,0:T(8,128)S(1)}, u32[]{:S(2)}, u32[]{:S(2)}) %collective-permute-start.14) | collective-permute-done | bytes 131104 | tf_op jit(solution)/shard_map/ppermute | solution.py:254
  61.2 1.2 %collective-permute-done.15.refs_2_ = f32[256,128]{1,0:T(8,128)S(1)} collective-permute-done((f32[256,128]{1,0:T(8,128)S(1)}, f32[256,128]{1,0:T(8,128)S(1)}, u32[]{:S(2)}, u32[]{:S(2)}) %collective-permute-start.15) | collective-permute-done | bytes 131104 | tf_op jit(solution)/shard_map/ppermute | solution.py:254
  62.5 2.6 %collective-permute-done.16.refs_3_ = f32[256,128]{1,0:T(8,128)S(1)} collective-permute-done((f32[256,128]{1,0:T(8,128)S(1)}, f32[256,128]{1,0:T(8,128)S(1)}, u32[]{:S(2)}, u32[]{:S(2)}) %collective-permute-start.16) | collective-permute-done | bytes 131104 | tf_op jit(solution)/shard_map/ppermute | solution.py:254
  65.0 1.8 %shard_map.102 = (f32[128,1024]{1,0:T(8,128)}, f32[128,1024]{1,0:T(8,128)}) custom-call(s32[1]{0:T(128)} %bitcast.seat, f32[128,1024]{1,0:T(8,128)S(1)} %copy-done.1, f32[128,1024]{1,0:T(8,128)S(1)} %copy-done.2, f32[128,1024]{1,0:T(8,128)S(1)} %get-tuple-element.47.refs_8_.part_k, f32[128,1024]{1,0:T(8,128)S(1)} %get-tuple-element.48.part_v, ...), custom_call_target="tpu_custom_call" | custom-call | flops 201326592 | bytes 3670016 | tf_op jit(solution)/shard_map/pallas_call | solution.py:53
  (32 shorter events, 8.7 us)
Async XLA Ops:
  0.6 25.7 %copy-start.2 = (f32[128,1024]{1,0:T(8,128)S(1)}, f32[128,1024]{1,0:T(8,128)}, u32[]{:S(2)}) copy-start(f32[128,1024]{1,0:T(8,128)} %v.5) | copy-start | bytes 1572868
  0.6 25.7 %copy-start.3 = (f32[128,1024]{1,0:T(8,128)S(1)}, f32[128,1024]{1,0:T(8,128)}, u32[]{:S(2)}) copy-start(f32[128,1024]{1,0:T(8,128)} %target.1) | copy-start | bytes 1572868
  3.4 6.6 %collective-permute-start = (f32[264,128]{1,0:T(8,128)S(1)}, f32[264,128]{1,0:T(8,128)S(1)}, u32[]{:S(2)}, u32[]{:S(2)}) collective-permute-start(f32[264,128]{1,0:T(8,128)S(1)} %get-tuple-element.35), channel_id=1, source_target_pairs={{0,4},{4,0},{8,12},{12,8},{16,20},{20,16},{24,28},{28,24},{1,5},{5... | collective-permute-start | bytes 405512 | tf_op jit(solution)/shard_map/ppermute | solution.py:254
  6.5 6.5 %collective-permute-start.1 = (f32[264,128]{1,0:T(8,128)S(1)}, f32[264,128]{1,0:T(8,128)S(1)}, u32[]{:S(2)}, u32[]{:S(2)}) collective-permute-start(f32[264,128]{1,0:T(8,128)S(1)} %get-tuple-element.36), channel_id=1, source_target_pairs={{0,8},{4,12},{8,0},{12,4},{16,24},{20,28},{24,16},{28,20},{1,9},{5... | collective-permute-start | bytes 405512 | tf_op jit(solution)/shard_map/ppermute | solution.py:254
  8.0 6.2 %collective-permute-start.2 = (f32[264,128]{1,0:T(8,128)S(1)}, f32[264,128]{1,0:T(8,128)S(1)}, u32[]{:S(2)}, u32[]{:S(2)}) collective-permute-start(f32[264,128]{1,0:T(8,128)S(1)} %get-tuple-element.37), channel_id=1, source_target_pairs={{0,12},{4,8},{8,4},{12,0},{16,28},{20,24},{24,20},{28,16},{1,13},{... | collective-permute-start | bytes 405512 | tf_op jit(solution)/shard_map/ppermute | solution.py:254
  14.2 12.2 %copy-start = (f32[128,1024]{1,0:T(8,128)S(1)}, f32[128,1024]{1,0:T(8,128)}, u32[]{:S(2)}) copy-start(f32[128,1024]{1,0:T(8,128)} %q.7) | copy-start | bytes 1572868
  14.2 12.2 %copy-start.1 = (f32[128,1024]{1,0:T(8,128)S(1)}, f32[128,1024]{1,0:T(8,128)}, u32[]{:S(2)}) copy-start(f32[128,1024]{1,0:T(8,128)} %k.5) | copy-start | bytes 1572868
  14.2 8.4 %collective-permute-start.3 = (f32[264,128]{1,0:T(8,128)S(1)}, f32[264,128]{1,0:T(8,128)S(1)}, u32[]{:S(2)}, u32[]{:S(2)}) collective-permute-start(f32[264,128]{1,0:T(8,128)S(1)} %shard_map.95.refs_0_), channel_id=1, source_target_pairs={{0,16},{4,20},{8,24},{12,28},{16,0},{20,4},{24,8},{28,12},{1,17},{... | collective-permute-start | bytes 405512 | tf_op jit(solution)/shard_map/ppermute | solution.py:254
  22.8 3.6 %copy-start.4 = (f32[1024]{0:T(1024)S(1)}, f32[1024]{0:T(1024)}, u32[]{:S(2)}) copy-start(f32[1024]{0:T(1024)} %param.10) | copy-start | bytes 12292
  22.8 5.8 %collective-permute-start.4 = (f32[256,128]{1,0:T(8,128)S(1)}, f32[256,128]{1,0:T(8,128)S(1)}, u32[]{:S(2)}, u32[]{:S(2)}) collective-permute-start(f32[256,128]{1,0:T(8,128)S(1)} %get-tuple-element.39), channel_id=1, source_target_pairs={{0,4},{4,0},{8,12},{12,8},{16,20},{20,16},{24,28},{28,24},{1,5},{5... | collective-permute-start | bytes 393224 | tf_op jit(solution)/shard_map/ppermute | solution.py:254
  23.8 5.5 %collective-permute-start.5 = (f32[256,128]{1,0:T(8,128)S(1)}, f32[256,128]{1,0:T(8,128)S(1)}, u32[]{:S(2)}, u32[]{:S(2)}) collective-permute-start(f32[256,128]{1,0:T(8,128)S(1)} %get-tuple-element.40), channel_id=1, source_target_pairs={{0,8},{4,12},{8,0},{12,4},{16,24},{20,28},{24,16},{28,20},{1,9},{5... | collective-permute-start | bytes 393224 | tf_op jit(solution)/shard_map/ppermute | solution.py:254
  24.5 1.9 %copy-start.5 = (s32[128]{0:T(128)S(1)}, s32[128]{0:T(128)}, u32[]{:S(2)}) copy-start(s32[128]{0:T(128)} %param.11) | copy-start | bytes 1540
  24.5 7.3 %collective-permute-start.6 = (f32[256,128]{1,0:T(8,128)S(1)}, f32[256,128]{1,0:T(8,128)S(1)}, u32[]{:S(2)}, u32[]{:S(2)}) collective-permute-start(f32[256,128]{1,0:T(8,128)S(1)} %get-tuple-element.41), channel_id=1, source_target_pairs={{0,12},{4,8},{8,4},{12,0},{16,28},{20,24},{24,20},{28,16},{1,13},{... | collective-permute-start | bytes 393224 | tf_op jit(solution)/shard_map/ppermute | solution.py:254
  32.3 3.1 %collective-permute-start.9 = (f32[8,128]{1,0:T(8,128)S(1)}, f32[8,128]{1,0:T(8,128)S(1)}, u32[]{:S(2)}, u32[]{:S(2)}) collective-permute-start(f32[8,128]{1,0:T(8,128)S(1)} %get-tuple-element.43.refs_2_), channel_id=1, source_target_pairs={{0,3},{1,2},{2,1},{3,0},{4,7},{5,6},{6,5},{7,4},{8,11},{9,10},{10,... | collective-permute-start | bytes 12296 | tf_op jit(solution)/shard_map/ppermute | solution.py:254
  32.4 3.7 %collective-permute-start.8 = (f32[8,128]{1,0:T(8,128)S(1)}, f32[8,128]{1,0:T(8,128)S(1)}, u32[]{:S(2)}, u32[]{:S(2)}) collective-permute-start(f32[8,128]{1,0:T(8,128)S(1)} %get-tuple-element.43.refs_2_), channel_id=1, source_target_pairs={{0,2},{1,3},{2,0},{3,1},{4,6},{5,7},{6,4},{7,5},{8,10},{9,11},{10,... | collective-permute-start | bytes 12296 | tf_op jit(solution)/shard_map/ppermute | solution.py:254
  34.0 2.1 %collective-permute-start.7 = (f32[8,128]{1,0:T(8,128)S(1)}, f32[8,128]{1,0:T(8,128)S(1)}, u32[]{:S(2)}, u32[]{:S(2)}) collective-permute-start(f32[8,128]{1,0:T(8,128)S(1)} %get-tuple-element.43.refs_2_), channel_id=1, source_target_pairs={{0,1},{1,0},{2,3},{3,2},{4,5},{5,4},{6,7},{7,6},{8,9},{9,8},{10,11... | collective-permute-start | bytes 12296 | tf_op jit(solution)/shard_map/ppermute | solution.py:254
  36.7 6.0 %collective-permute-start.10 = (f32[264,128]{1,0:T(8,128)S(1)}, f32[264,128]{1,0:T(8,128)S(1)}, u32[]{:S(2)}, u32[]{:S(2)}) collective-permute-start(f32[264,128]{1,0:T(8,128)S(1)} %get-tuple-element.50), channel_id=1, source_target_pairs={{0,4},{4,0},{8,12},{12,8},{16,20},{20,16},{24,28},{28,24},{1,5},{5... | collective-permute-start | bytes 405512 | tf_op jit(solution)/shard_map/ppermute | solution.py:254
  37.1 6.4 %collective-permute-start.11 = (f32[264,128]{1,0:T(8,128)S(1)}, f32[264,128]{1,0:T(8,128)S(1)}, u32[]{:S(2)}, u32[]{:S(2)}) collective-permute-start(f32[264,128]{1,0:T(8,128)S(1)} %get-tuple-element.51), channel_id=1, source_target_pairs={{0,8},{4,12},{8,0},{12,4},{16,24},{20,28},{24,16},{28,20},{1,9},{5... | collective-permute-start | bytes 405512 | tf_op jit(solution)/shard_map/ppermute | solution.py:254
  38.5 8.2 %collective-permute-start.12 = (f32[264,128]{1,0:T(8,128)S(1)}, f32[264,128]{1,0:T(8,128)S(1)}, u32[]{:S(2)}, u32[]{:S(2)}) collective-permute-start(f32[264,128]{1,0:T(8,128)S(1)} %get-tuple-element.52), channel_id=1, source_target_pairs={{0,12},{4,8},{8,4},{12,0},{16,28},{20,24},{24,20},{28,16},{1,13},{... | collective-permute-start | bytes 405512 | tf_op jit(solution)/shard_map/ppermute | solution.py:254
  46.8 8.4 %collective-permute-start.13 = (f32[264,128]{1,0:T(8,128)S(1)}, f32[264,128]{1,0:T(8,128)S(1)}, u32[]{:S(2)}, u32[]{:S(2)}) collective-permute-start(f32[264,128]{1,0:T(8,128)S(1)} %shard_map.100.refs_6_), channel_id=1, source_target_pairs={{0,16},{4,20},{8,24},{12,28},{16,0},{20,4},{24,8},{28,12},{1,17},{... | collective-permute-start | bytes 405512 | tf_op jit(solution)/shard_map/ppermute | solution.py:254
  55.7 5.5 %collective-permute-start.14 = (f32[256,128]{1,0:T(8,128)S(1)}, f32[256,128]{1,0:T(8,128)S(1)}, u32[]{:S(2)}, u32[]{:S(2)}) collective-permute-start(f32[256,128]{1,0:T(8,128)S(1)} %get-tuple-element.54), channel_id=1, source_target_pairs={{0,4},{4,0},{8,12},{12,8},{16,20},{20,16},{24,28},{28,24},{1,5},{5... | collective-permute-start | bytes 393224 | tf_op jit(solution)/shard_map/ppermute | solution.py:254
  56.4 6.1 %collective-permute-start.15 = (f32[256,128]{1,0:T(8,128)S(1)}, f32[256,128]{1,0:T(8,128)S(1)}, u32[]{:S(2)}, u32[]{:S(2)}) collective-permute-start(f32[256,128]{1,0:T(8,128)S(1)} %get-tuple-element.55), channel_id=1, source_target_pairs={{0,8},{4,12},{8,0},{12,4},{16,24},{20,28},{24,16},{28,20},{1,9},{5... | collective-permute-start | bytes 393224 | tf_op jit(solution)/shard_map/ppermute | solution.py:254
  56.7 8.3 %collective-permute-start.16 = (f32[256,128]{1,0:T(8,128)S(1)}, f32[256,128]{1,0:T(8,128)S(1)}, u32[]{:S(2)}, u32[]{:S(2)}) collective-permute-start(f32[256,128]{1,0:T(8,128)S(1)} %get-tuple-element.56), channel_id=1, source_target_pairs={{0,12},{4,8},{8,4},{12,0},{16,28},{20,24},{24,20},{28,16},{1,13},{... | collective-permute-start | bytes 393224 | tf_op jit(solution)/shard_map/ppermute | solution.py:254

commit v3 on v2

v3 whole, which is shorter than its diff:
```python
import functools

import jax
import jax.numpy as jnp
from jax import lax
from jax.experimental import pallas as pl
from jax.experimental.pallas import tpu as pltpu
from jax.sharding import PartitionSpec as P

HEAD_DIM = 128
TAIL = 8
epsilon = 1e-06
f32 = jnp.float32
bf16 = jnp.bfloat16
SMEM = pl.BlockSpec(memory_space=pltpu.SMEM)
VMEM = pl.BlockSpec(memory_space=pltpu.VMEM)
ANY = pl.BlockSpec(memory_space=pl.ANY)

NN = ((1,), (0,))
NT = ((1,), (1,))
TN = ((0,), (0,))


def split(x):
    high = x.astype(bf16)
    return high, (x - high.astype(f32)).astype(bf16)


def dot(a, b, dims):
    ca, cb = dims[0][0], dims[1][0]
    left = jnp.concatenate(a, axis=ca)
    both = jnp.concatenate(b, axis=1 - cb)
    right = jnp.concatenate([both, both], axis=cb)
    out = lax.dot_general(left, right, (dims, ((), ())), preferred_element_type=f32)
    n = out.shape[1] // 2
    return out[:, :n] + out[:, n:]


def head_cols(h):
    return pl.ds(pl.multiple_of(h * HEAD_DIM, HEAD_DIM), HEAD_DIM)


def rows_of(i):
    return slice(i * HEAD_DIM, (i + 1) * HEAD_DIM)


def in_hbm(x):
    return pltpu.with_memory_space_constraint(x, pltpu.HBM)


def shape(*s):
    return jax.ShapeDtypeStruct(s, f32)


def call(kernel, outs, flops, seat, *args, specs=None, out_specs=None, scratch=(), aliases=None, limit=24):
    specs = specs or [VMEM] * len(args)
    place = [] if seat is None else [seat]
    nbytes = sum(a.size * 4 for a in args) + sum(o.size * 4 for o in outs)
    return pl.pallas_call(
        kernel,
        out_shape=outs,
        in_specs=[SMEM] * len(place) + specs,
        out_specs=out_specs or [VMEM] * len(outs),
        scratch_shapes=scratch,
        input_output_aliases=aliases or {},
        compiler_params=pltpu.CompilerParams(vmem_limit_bytes=limit * 1024 * 1024),
        cost_estimate=pl.CostEstimate(flops=flops, bytes_accessed=nbytes, transcendentals=0),
    )(*place, *args)


def causal_mask(n):
    return lax.broadcasted_iota(jnp.int32, (n, n), 0) >= lax.broadcasted_iota(jnp.int32, (n, n), 1)


def column(row, n):
    return jnp.broadcast_to(row, (n, n)).T


def pair_sum(parts):
    parts = list(parts)
    while len(parts) > 1:
        parts = [parts[i] + parts[i + 1] for i in range(0, len(parts), 2)]
    return parts[0]


class Plan:
    def __init__(self, length, heads, seq, head):
        group = 1
        while group < 4 and seq % (2 * group) == 0 and heads % (2 * group) == 0:
            group *= 2
        self.length, self.heads, self.head, self.group, self.own = length, heads, head, group, heads // group
        self.width, self.tokens = heads * HEAD_DIM * head, length * seq
        self.bits = [group << i for i in range(30) if group << i < seq]
        self.swaps = [bit | (bit // 2 if bit == group else 0) for bit in self.bits]
        self.state_rows = self.own * HEAD_DIM
        self.body = slice(0, self.state_rows)
        self.tail = slice(self.state_rows, self.state_rows + TAIL)

    def owned(self, seat, x):
        return (seat % self.group) ^ ((seat & self.group) // 2) ^ x

    def head_of(self, seat, x, i):
        return self.owned(seat, x) * self.own + i

    def share(self, seat, x, count=1):
        start = self.owned(seat, x) // count * (count * self.state_rows)
        return pl.ds(pl.multiple_of(start, HEAD_DIM), count * self.state_rows)


def outer_sum(plan, seat, reverse, totals):
    total = jnp.zeros((plan.state_rows, HEAD_DIM), f32)
    for bit, other in zip(plan.bits, totals):
        upper = (seat & bit) != 0
        counts = jnp.logical_not(upper) if reverse else upper
        total = total + jnp.where(counts, other[plan.body, :], 0.0)
    return total


def state_at(plan, seat, reverse, x, outer, parts):
    here = seat % plan.group
    total = outer
    for y in range(plan.group):
        if y != x:
            ahead = (here ^ y) > (here ^ x) if reverse else (here ^ y) < (here ^ x)
            total = total + jnp.where(ahead, parts[y][plan.body, :], 0.0)
    return total


def full_count(plan, totals):
    count = totals[0][plan.tail, :]
    for other in totals[1:]:
        count = count + other[plan.tail, :]
    return count[0:1, :]


def state_kernel(plan, k_hbm, v_hbm, mask_hbm, *refs):
    group = plan.group
    out, (k, v, mask, sems) = refs[:group], refs[group:]
    seat = [lax.axis_index("seq")]
    pair = min(group, 2)
    copies = {}
    for x in range(0, group, pair):
        cols = plan.share(seat[0], x, pair)
        copies[x] = [
            pltpu.make_async_copy(src.at[:, cols], dst.at[:, cols], sems.at[i, x])
            for i, (src, dst) in enumerate(((k_hbm, k), (v_hbm, v)))
        ]
        for copy in copies[x]:
            copy.start()
    mask_copy = pltpu.make_async_copy(mask_hbm, mask, sems.at[0, group])
    mask_copy.start()
    for x in range(group):
        for copy in copies.get(x, ()):
            copy.wait()
        for i in range(plan.own):
            cols = head_cols(plan.head_of(seat[0], x, i))
            out[x][rows_of(i), :] = dot(split(k[:, cols]), split(v[:, cols]), TN)
    mask_copy.wait()
    count = jnp.sum(mask[...].astype(f32))
    for x in range(group):
        out[x][plan.tail, :] = jnp.full((TAIL, HEAD_DIM), count, f32)


def local_kernel(plan, seat, q_hbm, k, v, target_hbm, gain, mask, q, scores, local, aim, target, sems):
    copies = [
        pltpu.make_async_copy(src, dst, sems.at[i]) for i, (src, dst) in enumerate(((q_hbm, q), (target_hbm, target)))
    ]
    for copy in copies:
        copy.start()
    causal = causal_mask(plan.length)
    valid = column(mask[...].astype(f32), plan.length)
    for copy in copies:
        copy.wait()
    for h in range(plan.heads):
        cols = head_cols(h)
        s = dot(split(q[:, cols]), split(k[:, cols]), NT)
        s = jnp.where(causal, s, 0.0)
        scores[h] = s
        local[:, cols] = dot(split(s), split(v[:, cols]), NN)
        aim[:, cols] = valid * (gain[:, cols] * target[:, cols])


def total_kernel(plan, seat, *refs):
    refs[-1][...] = pair_sum(r[...] for r in refs[: plan.group])


def prior_kernel(plan, seat, *refs):
    group = plan.group
    parts, totals, outs = refs[:group], refs[group : -group], refs[-group:]
    outer = outer_sum(plan, seat[0], False, totals)
    for x in range(group):
        outs[x][...] = state_at(plan, seat[0], False, x, outer, parts)


def attend_kernel(plan, which, last, seat, q, local, aim, *refs):
    n = len(which)
    priors, refs = refs[:n], refs[n:]
    if last:
        squares, dots = refs[0][...], refs[1][...]
        refs = refs[2:]
    else:
        squares = jnp.zeros((plan.length, HEAD_DIM), f32)
        dots = jnp.zeros((plan.length, HEAD_DIM), f32)
    attended, sums = refs[:n], refs[n:]
    for x, prior, out in zip(which, priors, attended):
        for i in range(plan.own):
            cols = head_cols(plan.head_of(seat[0], x, i))
            a = local[:, cols] + dot(split(q[:, cols]), split(prior[rows_of(i), :]), NN)
            out[:, rows_of(i)] = a
            squares = squares + a * a
            dots = dots + aim[:, cols] * a
    if last:
        (stats,) = sums
        stats[0:1, :] = jnp.sum(squares.T, axis=0, keepdims=True)
        stats[1:2, :] = jnp.sum(dots.T, axis=0, keepdims=True)
        stats[2:, :] = jnp.zeros((TAIL - 2, plan.length), f32)
    else:
        sums[0][...] = squares
        sums[1][...] = dots


def scales(plan, stats, row, count):
    squares, dots = stats[pl.ds(row, 1), :], stats[pl.ds(row + 1, 1), :]
    inverse_rms = lax.rsqrt(squares / plan.width + epsilon)
    left = (plan.tokens / count) * inverse_rms
    right = left * (inverse_rms * inverse_rms * dots / plan.width)
    return left, right, inverse_rms * dots


def grad_kernel(plan, seat, q, aim, *refs):
    refs = list(refs)
    take = lambda n: [refs.pop(0) for _ in range(n)]
    attended, totals, stat_parts = take(plan.group), take(1 + len(plan.swaps)), take(plan.head)
    (grad,), out = take(1), take(plan.group)
    (stats,) = refs
    stats[...] = pair_sum(r[...] for r in stat_parts)
    left, right, losses = scales(plan, stats, 0, full_count(plan, totals))
    left, right = column(left, plan.length), column(right, plan.length)
    loss = jnp.sum(losses)
    for x in range(plan.group):
        for i in range(plan.own):
            cols = head_cols(plan.head_of(seat[0], x, i))
            g = left * aim[:, cols] - right * attended[x][:, rows_of(i)]
            grad[:, cols] = g
            out[x][rows_of(i), :] = dot(split(q[:, cols]), split(g), TN)
        out[x][plan.tail, :] = jnp.full((TAIL, HEAD_DIM), loss, f32)


def local_grad_kernel(plan, seat, q, k, v, grad, scores, *refs):
    priors, (grad_q, grad_k, grad_v) = refs[: plan.group], refs[plan.group :]
    causal = causal_mask(plan.length)
    for x in range(plan.group):
        for i in range(plan.own):
            h = plan.head_of(seat[0], x, i)
            cols = head_cols(h)
            g = split(grad[:, cols])
            gs = split(jnp.where(causal, dot(g, split(v[:, cols]), NT), 0.0))
            prior = split(priors[x][rows_of(i), :])
            grad_q[:, cols] = dot(gs, split(k[:, cols]), NN) + dot(g, prior, NT)
            grad_k[:, cols] = dot(gs, split(q[:, cols]), TN)
            grad_v[:, cols] = dot(split(scores[h]), g, TN)


def later_kernel(plan, seat, *refs):
    group = plan.group
    states, totals, outs = refs[:group], refs[group : -group - 1], refs[-group:]
    outer = outer_sum(plan, seat[0], True, totals)
    for x in range(group):
        outs[x][...] = state_at(plan, seat[0], True, x, outer, states)


def loss_kernel(plan, seat, *refs):
    n = 1 + len(plan.swaps)
    refs[-1][...] = (full_count(plan, refs[n : 2 * n]) / full_count(plan, refs[:n]))[:, 0:1]


def final_kernel(plan, which, seat, k, v, part_k, part_v, *refs):
    n = len(which)
    later = refs[:n]
    grad_k, grad_v, block_k, block_v, sems = refs[-5:]
    copies = []
    for j, x in enumerate(which):
        for i in range(plan.own):
            cols = head_cols(plan.head_of(seat[0], x, i))
            state = split(later[j][rows_of(i), :])
            block_k[j, :, rows_of(i)] = part_k[:, cols] + dot(split(v[:, cols]), state, NT)
            block_v[j, :, rows_of(i)] = part_v[:, cols] + dot(split(k[:, cols]), state, NN)
        for m, (block, out) in enumerate(((block_k, grad_k), (block_v, grad_v))):
            copies.append(pltpu.make_async_copy(block.at[j], out.at[:, plan.share(seat[0], x)], sems.at[m, j]))
            copies[-1].start()
    for copy in copies:
        copy.wait()


def swap(value, axis, step):
    return lax.ppermute(value, axis, [(i, i ^ step) for i in range(lax.axis_size(axis))])


def swap_all(parts, axis):
    return [parts[0]] + [swap(part, axis, x) for x, part in enumerate(parts) if x]


def swap_totals(plan, total):
    totals = [total]
    for step in plan.swaps:
        totals.append(swap(total, "seq", step))
        if step != plan.swaps[-1]:
            total = total + totals[-1]
    return totals


def shards(queries, key_rows, value_rows, target, norm_gain, valid_mask):
    length, columns = queries.shape
    heads = columns // HEAD_DIM
    head_count = lax.axis_size("head")
    plan = Plan(length, heads, lax.axis_size("seq"), head_count)
    group, own = plan.group, plan.own
    product = 6 * HEAD_DIM**3 * heads
    seat = jnp.reshape(lax.axis_index("seq"), (1,)).astype(jnp.int32)
    gain = norm_gain.reshape(1, columns)
    mask = valid_mask.reshape(1, length)
    sum_shape = shape(plan.state_rows + TAIL, HEAD_DIM)
    state = shape(plan.state_rows, HEAD_DIM)
    piece = shape(length, plan.state_rows)
    wide = shape(length, columns)
    bind = lambda kernel: functools.partial(kernel, plan)

    *kv, key_rows, value_rows = call(
        bind(state_kernel),
        [sum_shape] * group + [wide] * 2,
        product,
        None,
        in_hbm(key_rows),
        in_hbm(value_rows),
        in_hbm(mask),
        specs=[ANY] * 3,
        scratch=[pltpu.VMEM((1, length), jnp.int32), pltpu.SemaphoreType.DMA((2, group + 1))],
    )
    queries, scores, local, aim = call(
        bind(local_kernel),
        [wide, shape(heads, length, length), wide, wide],
        2 * product,
        seat,
        in_hbm(queries),
        key_rows,
        value_rows,
        in_hbm(target),
        in_hbm(gain),
        in_hbm(mask),
        specs=[ANY, VMEM, VMEM, ANY, VMEM, VMEM],
        scratch=[pltpu.VMEM((length, columns), f32), pltpu.SemaphoreType.DMA((2,))],
    )
    kv = swap_all(kv, "seq")
    (total,) = call(bind(total_kernel), [sum_shape], 0, seat, *kv)
    totals = swap_totals(plan, total)
    priors = call(bind(prior_kernel), [state] * group, 0, seat, *kv, *totals[1:])
    priors = swap_all(priors, "seq")
    early, late = list(range(group - 1)), [group - 1]
    column_sum = shape(length, HEAD_DIM)
    *attended, squares, dots = call(
        functools.partial(attend_kernel, plan, early, False),
        [piece] * len(early) + [column_sum] * 2,
        product,
        seat,
        queries,
        local,
        aim,
        *priors[:-1],
    )
    last, stats = call(
        functools.partial(attend_kernel, plan, late, True),
        [piece, shape(TAIL, length)],
        product // group,
        seat,
        queries,
        local,
        aim,
        priors[-1],
        squares,
        dots,
    )
    attended.append(last)
    stats = swap_all([stats] * head_count, "head")
    grad, *states = call(
        bind(grad_kernel),
        [wide] + [sum_shape] * group,
        product,
        seat,
        queries,
        aim,
        *attended,
        *totals,
        *stats,
        scratch=[pltpu.VMEM((TAIL, length), f32)],
    )
    grad_query, part_key, part_value = call(
        bind(local_grad_kernel), [wide] * 3, 5 * product, seat, queries, key_rows, value_rows, grad, scores, *priors
    )
    states = swap_all(states, "seq")
    (grad_total,) = call(bind(total_kernel), [sum_shape], 0, seat, *states)
    grad_totals = swap_totals(plan, grad_total)
    later = call(
        bind(later_kernel),
        [state] * group,
        0,
        seat,
        *states,
        *grad_totals[1:],
        part_key,
        specs=[VMEM] * (group + len(plan.swaps)) + [ANY],
    )
    (loss,) = call(bind(loss_kernel), [shape(1, 1)], 0, seat, *totals, *grad_totals)
    later = swap_all(later, "seq")
    grads = []
    for which in [early[:2], *([x] for x in early[2:]), late]:
        block = pltpu.VMEM((len(which), length, plan.state_rows), f32)
        inputs = [key_rows, value_rows, part_key, part_value, *(later[x] for x in which)]
        grads = call(
            functools.partial(final_kernel, plan, which),
            [wide] * 2,
            2 * product * len(which) // group,
            seat,
            *inputs,
            *grads,
            specs=[VMEM] * len(inputs) + [ANY] * len(grads),
            out_specs=[ANY] * 2,
            scratch=[block, block, pltpu.SemaphoreType.DMA((2, len(which)))],
            aliases={1 + len(inputs) + i: i for i in range(len(grads))},
        )
    grad_key, grad_value = grads
    return (grad_query, grad_key, grad_value, loss[0, 0])


def solution(mesh):
    return jax.shard_map(
        shards,
        mesh=mesh,
        in_specs=(
            P("seq", "head"),
            P("seq", "head"),
            P("seq", "head"),
            P("seq", "head"),
            P("head"),
            P("seq"),
        ),
        out_specs=(P("seq", "head"), P("seq", "head"), P("seq", "head"), P()),
        check_vma=False,
    )
```

time: 67 us -> 62 us (0.925)
  waiting for transfers between devices: 31.6 us -> 23.3 us
  starting transfers between devices: 21.9 us -> 24.2 us
  Pallas kernels: 12.6 us -> 13.6 us
    ppermute x17, waiting for transfers between devices: 31.6 us -> 23.3 us  [swap(): lax.ppermute(value, axis, [(i, i ^ step) for i in range(lax.axis_size(axi...]
    ppermute x17, starting transfers between devices: 21.9 us -> 24.2 us  [swap(): lax.ppermute(value, axis, [(i, i ^ step) for i in range(lax.axis_size(axi...]
    pallas_call x10 -> x14, Pallas kernels: 12.6 us -> 13.6 us  [call(): pl.pallas_call(kernel, out_shape=outs, in_specs=[SMEM] * len(place) + spe...]
  transfers between devices with their start and end apart: 17 -> 17, of which waited for: 15 -> 15; matrix products, arithmetic and copies ran while one was open for 0% -> 0% of each run, Pallas kernels for 9% -> 16%
where the time goes in v3:
time: 62 us; the launch traced here: 61.8 us
  starting transfers between devices  24.2 us (39%)
  waiting for transfers between devices  23.3 us (38%)
  Pallas kernels  13.6 us (22%)
  between operations  0.72 us (1%)
    ppermute x17, starting transfers between devices, swap(): lax.ppermute(value, axis, [(i, i ^ step) for i in range(lax.axis_size(axi...  24.2 us
    ppermute x17, waiting for transfers between devices, swap(): lax.ppermute(value, axis, [(i, i ^ step) for i in range(lax.axis_size(axi...  23.3 us
    pallas_call x14, Pallas kernels, call(): pl.pallas_call(kernel, out_shape=outs, in_specs=[SMEM] * len(place) + spe...  13.6 us
  transfers between devices with their start and end apart: 17, of which 15 were waited for; matrix products, arithmetic and copies ran while one was open for 0% of the time, Pallas kernels for 16%

profile of v3, /device:TPU:0, one launch (start us, length us, event | category | flops | bytes accessed | tf_op | source)
XLA Modules:
  0.0 61.8 jit_solution(6483160573807385960)
XLA Ops:
  0.6 1.8 %shard_map.93 = (f32[264,128]{1,0:T(8,128)S(1)}, f32[264,128]{1,0:T(8,128)S(1)}, f32[264,128]{1,0:T(8,128)S(1)}, f32[264,128]{1,0:T(8,128)S(1)}, f32[128,1024]{1,0:T(8,128)S(1)}, /*index=5*/f32[128,1024]{1,0:T(8,128)S(1)}) custom-call(f32[128,1024]{1,0:T(8,128)} %k_hbm.1, f32[128,1024]{1,0:T(8,128)} %v_hbm.1, s32[1,128]{1,0:T(1,128)} %bitcast.5), custom_call_target="tpu_custom_call" | custom-call | flops 100663296 | bytes 2638336 | tf_op jit(solution)/shard_map/pallas_call | solution.py:59
  2.5 3.0 %collective-permute-start = (f32[264,128]{1,0:T(8,128)S(1)}, f32[264,128]{1,0:T(8,128)S(1)}, u32[]{:S(2)}, u32[]{:S(2)}) collective-permute-start(f32[264,128]{1,0:T(8,128)S(1)} %get-tuple-element.49), channel_id=1, source_target_pairs={{0,4},{4,0},{8,12},{12,8},{16,20},{20,16},{24,28},{28,24},{1,5},{5... | collective-permute-start | bytes 405512 | tf_op jit(solution)/shard_map/ppermute | solution.py:296
  5.5 1.6 %collective-permute-start.1 = (f32[264,128]{1,0:T(8,128)S(1)}, f32[264,128]{1,0:T(8,128)S(1)}, u32[]{:S(2)}, u32[]{:S(2)}) collective-permute-start(f32[264,128]{1,0:T(8,128)S(1)} %get-tuple-element.50), channel_id=1, source_target_pairs={{0,8},{4,12},{8,0},{12,4},{16,24},{20,28},{24,16},{28,20},{1,9},{5... | collective-permute-start | bytes 405512 | tf_op jit(solution)/shard_map/ppermute | solution.py:296
  7.1 2.0 %collective-permute-done.refs_1_ = f32[264,128]{1,0:T(8,128)S(1)} collective-permute-done((f32[264,128]{1,0:T(8,128)S(1)}, f32[264,128]{1,0:T(8,128)S(1)}, u32[]{:S(2)}, u32[]{:S(2)}) %collective-permute-start) | collective-permute-done | bytes 135200 | tf_op jit(solution)/shard_map/ppermute | solution.py:296
  9.1 2.9 %collective-permute-done.1.refs_2_ = f32[264,128]{1,0:T(8,128)S(1)} collective-permute-done((f32[264,128]{1,0:T(8,128)S(1)}, f32[264,128]{1,0:T(8,128)S(1)}, u32[]{:S(2)}, u32[]{:S(2)}) %collective-permute-start.1) | collective-permute-done | bytes 135200 | tf_op jit(solution)/shard_map/ppermute | solution.py:296
  12.0 1.2 %collective-permute-done.2.refs_3_ = f32[264,128]{1,0:T(8,128)S(1)} collective-permute-done((f32[264,128]{1,0:T(8,128)S(1)}, f32[264,128]{1,0:T(8,128)S(1)}, u32[]{:S(2)}, u32[]{:S(2)}) %collective-permute-start.2) | collective-permute-done | bytes 135200 | tf_op jit(solution)/shard_map/ppermute | solution.py:296
  13.3 3.8 %collective-permute-start.3 = (f32[264,128]{1,0:T(8,128)S(1)}, f32[264,128]{1,0:T(8,128)S(1)}, u32[]{:S(2)}, u32[]{:S(2)}) collective-permute-start(f32[264,128]{1,0:T(8,128)S(1)} %shard_map.95.refs_4_.refs_0_), channel_id=1, source_target_pairs={{0,24},{4,28},{8,16},{12,20},{16,8},{20,12},{24,0},{28,4},{1,25},{... | collective-permute-start | bytes 405512 | tf_op jit(solution)/shard_map/ppermute | solution.py:296
  17.1 3.2 %collective-permute-done.3.refs_4_.refs_5_.refs_1_ = f32[264,128]{1,0:T(8,128)S(1)} collective-permute-done((f32[264,128]{1,0:T(8,128)S(1)}, f32[264,128]{1,0:T(8,128)S(1)}, u32[]{:S(2)}, u32[]{:S(2)}) %collective-permute-start.3) | collective-permute-done | bytes 135200 | tf_op jit(solution)/shard_map/ppermute | solution.py:296
  20.4 1.7 %collective-permute-start.4 = (f32[256,128]{1,0:T(8,128)S(1)}, f32[256,128]{1,0:T(8,128)S(1)}, u32[]{:S(2)}, u32[]{:S(2)}) collective-permute-start(f32[256,128]{1,0:T(8,128)S(1)} %get-tuple-element.53), channel_id=1, source_target_pairs={{0,4},{4,0},{8,12},{12,8},{16,20},{20,16},{24,28},{28,24},{1,5},{5... | collective-permute-start | bytes 393224 | tf_op jit(solution)/shard_map/ppermute | solution.py:296
  22.1 1.4 %collective-permute-start.5 = (f32[256,128]{1,0:T(8,128)S(1)}, f32[256,128]{1,0:T(8,128)S(1)}, u32[]{:S(2)}, u32[]{:S(2)}) collective-permute-start(f32[256,128]{1,0:T(8,128)S(1)} %get-tuple-element.54), channel_id=1, source_target_pairs={{0,8},{4,12},{8,0},{12,4},{16,24},{20,28},{24,16},{28,20},{1,9},{5... | collective-permute-start | bytes 393224 | tf_op jit(solution)/shard_map/ppermute | solution.py:296
  24.0 3.7 %shard_map.94 = (f32[128,1024]{1,0:T(8,128)S(1)}, f32[8,128,128]{2,1,0:T(8,128)S(1)}, f32[128,1024]{1,0:T(8,128)S(1)}, f32[128,1024]{1,0:T(8,128)S(1)}) custom-call(s32[1]{0:T(128)} %bitcast.seat, f32[128,1024]{1,0:T(8,128)} %q_hbm.1, f32[128,1024]{1,0:T(8,128)S(1)} %get-tuple-element.43.k, f32[128,1024]{1,0:T(8,128)S(1)} %get-tuple-element.44.v, ...), custom_call_target="tpu_custom_call" | custom-call | flops 201326592 | bytes 4198912 | tf_op jit(solution)/shard_map/pallas_call | solution.py:59
  29.8 1.5 %collective-permute-start.8 = (f32[8,128]{1,0:T(8,128)S(1)}, f32[8,128]{1,0:T(8,128)S(1)}, u32[]{:S(2)}, u32[]{:S(2)}) collective-permute-start(f32[8,128]{1,0:T(8,128)S(1)} %get-tuple-element.62.refs_6_), channel_id=1, source_target_pairs={{0,2},{1,3},{2,0},{3,1},{4,6},{5,7},{6,4},{7,5},{8,10},{9,11},{10,... | collective-permute-start | bytes 12296 | tf_op jit(solution)/shard_map/ppermute | solution.py:296
  31.7 1.8 %collective-permute-done.8.refs_8_ = f32[8,128]{1,0:T(8,128)S(1)} collective-permute-done((f32[8,128]{1,0:T(8,128)S(1)}, f32[8,128]{1,0:T(8,128)S(1)}, u32[]{:S(2)}, u32[]{:S(2)}) %collective-permute-start.8) | collective-permute-done | bytes 4128 | tf_op jit(solution)/shard_map/ppermute | solution.py:296
  34.9 1.3 %collective-permute-start.10 = (f32[264,128]{1,0:T(8,128)S(1)}, f32[264,128]{1,0:T(8,128)S(1)}, u32[]{:S(2)}, u32[]{:S(2)}) collective-permute-start(f32[264,128]{1,0:T(8,128)S(1)} %get-tuple-element.69), channel_id=1, source_target_pairs={{0,4},{4,0},{8,12},{12,8},{16,20},{20,16},{24,28},{28,24},{1,5},{5... | collective-permute-start | bytes 405512 | tf_op jit(solution)/shard_map/ppermute | solution.py:296
  36.9 1.5 %collective-permute-start.12 = (f32[264,128]{1,0:T(8,128)S(1)}, f32[264,128]{1,0:T(8,128)S(1)}, u32[]{:S(2)}, u32[]{:S(2)}) collective-permute-start(f32[264,128]{1,0:T(8,128)S(1)} %get-tuple-element.71), channel_id=1, source_target_pairs={{0,12},{4,8},{8,4},{12,0},{16,28},{20,24},{24,20},{28,16},{1,13},{... | collective-permute-start | bytes 405512 | tf_op jit(solution)/shard_map/ppermute | solution.py:296
  38.4 2.2 %collective-permute-done.10.refs_1_ = f32[264,128]{1,0:T(8,128)S(1)} collective-permute-done((f32[264,128]{1,0:T(8,128)S(1)}, f32[264,128]{1,0:T(8,128)S(1)}, u32[]{:S(2)}, u32[]{:S(2)}) %collective-permute-start.10) | collective-permute-done | bytes 135200 | tf_op jit(solution)/shard_map/ppermute | solution.py:296
  40.6 2.1 %collective-permute-done.11.refs_2_ = f32[264,128]{1,0:T(8,128)S(1)} collective-permute-done((f32[264,128]{1,0:T(8,128)S(1)}, f32[264,128]{1,0:T(8,128)S(1)}, u32[]{:S(2)}, u32[]{:S(2)}) %collective-permute-start.11) | collective-permute-done | bytes 135200 | tf_op jit(solution)/shard_map/ppermute | solution.py:296
  42.7 2.0 %collective-permute-done.12.refs_3_ = f32[264,128]{1,0:T(8,128)S(1)} collective-permute-done((f32[264,128]{1,0:T(8,128)S(1)}, f32[264,128]{1,0:T(8,128)S(1)}, u32[]{:S(2)}, u32[]{:S(2)}) %collective-permute-start.12) | collective-permute-done | bytes 135200 | tf_op jit(solution)/shard_map/ppermute | solution.py:296
  44.7 3.0 %collective-permute-start.13 = (f32[264,128]{1,0:T(8,128)S(1)}, f32[264,128]{1,0:T(8,128)S(1)}, u32[]{:S(2)}, u32[]{:S(2)}) collective-permute-start(f32[264,128]{1,0:T(8,128)S(1)} %shard_map.101.refs_2_), channel_id=1, source_target_pairs={{0,24},{4,28},{8,16},{12,20},{16,8},{20,12},{24,0},{28,4},{1,25},{... | collective-permute-start | bytes 405512 | tf_op jit(solution)/shard_map/ppermute | solution.py:296
  47.7 3.1 %shard_map.100 = (f32[128,1024]{1,0:T(8,128)}, f32[128,1024]{1,0:T(8,128)S(1)}, f32[128,1024]{1,0:T(8,128)S(1)}) custom-call(s32[1]{0:T(128)} %bitcast.seat, f32[128,1024]{1,0:T(8,128)S(1)} %get-tuple-element.45.q, f32[128,1024]{1,0:T(8,128)S(1)} %get-tuple-element.43.k, f32[128,1024]{1,0:T(8,128)S(1)} %get-tuple-element.44.v, ...), custom_call_target="tpu_custom_call" | custom-call | flops 503316480 | bytes 4718592 | tf_op jit(solution)/shard_map/pallas_call | solution.py:59
  51.8 1.3 %collective-permute-start.16 = (f32[256,128]{1,0:T(8,128)S(1)}, f32[256,128]{1,0:T(8,128)S(1)}, u32[]{:S(2)}, u32[]{:S(2)}) collective-permute-start(f32[256,128]{1,0:T(8,128)S(1)} %get-tuple-element.75), channel_id=1, source_target_pairs={{0,4},{4,0},{8,12},{12,8},{16,20},{20,16},{24,28},{28,24},{1,5},{5... | collective-permute-start | bytes 393224 | tf_op jit(solution)/shard_map/ppermute | solution.py:296
  53.1 1.5 %collective-permute-start.15 = (f32[256,128]{1,0:T(8,128)S(1)}, f32[256,128]{1,0:T(8,128)S(1)}, u32[]{:S(2)}, u32[]{:S(2)}) collective-permute-start(f32[256,128]{1,0:T(8,128)S(1)} %get-tuple-element.73), channel_id=1, source_target_pairs={{0,8},{4,12},{8,0},{12,4},{16,24},{20,28},{24,16},{28,20},{1,9},{5... | collective-permute-start | bytes 393224 | tf_op jit(solution)/shard_map/ppermute | solution.py:296
  56.0 1.5 %collective-permute-done.16.refs_1_ = f32[256,128]{1,0:T(8,128)S(1)} collective-permute-done((f32[256,128]{1,0:T(8,128)S(1)}, f32[256,128]{1,0:T(8,128)S(1)}, u32[]{:S(2)}, u32[]{:S(2)}) %collective-permute-start.16) | collective-permute-done | bytes 131104 | tf_op jit(solution)/shard_map/ppermute | solution.py:296
  57.4 1.1 %shard_map.103 = (f32[128,1024]{1,0:T(8,128)}, f32[128,1024]{1,0:T(8,128)}) custom-call(s32[1]{0:T(128)} %bitcast.seat, f32[128,1024]{1,0:T(8,128)S(1)} %get-tuple-element.43.k, f32[128,1024]{1,0:T(8,128)S(1)} %get-tuple-element.44.v, f32[128,1024]{1,0:T(8,128)S(1)} %get-tuple-element.66.refs_5_.part_k, f32[128,1024]{1,0:T(8,128)S(1)} %get-tuple-element.67.part_v, ...), custom_call_target="tpu_custom_call" | custom-call | flops 100663296 | bytes 3407872 | tf_op jit(solution)/shard_map/pallas_call | solution.py:59
  (24 shorter events, 10.7 us)
Async XLA Ops:
  2.5 6.6 %collective-permute-start = (f32[264,128]{1,0:T(8,128)S(1)}, f32[264,128]{1,0:T(8,128)S(1)}, u32[]{:S(2)}, u32[]{:S(2)}) collective-permute-start(f32[264,128]{1,0:T(8,128)S(1)} %get-tuple-element.49), channel_id=1, source_target_pairs={{0,4},{4,0},{8,12},{12,8},{16,20},{20,16},{24,28},{28,24},{1,5},{5... | collective-permute-start | bytes 405512 | tf_op jit(solution)/shard_map/ppermute | solution.py:296
  5.5 6.5 %collective-permute-start.1 = (f32[264,128]{1,0:T(8,128)S(1)}, f32[264,128]{1,0:T(8,128)S(1)}, u32[]{:S(2)}, u32[]{:S(2)}) collective-permute-start(f32[264,128]{1,0:T(8,128)S(1)} %get-tuple-element.50), channel_id=1, source_target_pairs={{0,8},{4,12},{8,0},{12,4},{16,24},{20,28},{24,16},{28,20},{1,9},{5... | collective-permute-start | bytes 405512 | tf_op jit(solution)/shard_map/ppermute | solution.py:296
  7.1 6.2 %collective-permute-start.2 = (f32[264,128]{1,0:T(8,128)S(1)}, f32[264,128]{1,0:T(8,128)S(1)}, u32[]{:S(2)}, u32[]{:S(2)}) collective-permute-start(f32[264,128]{1,0:T(8,128)S(1)} %get-tuple-element.51), channel_id=1, source_target_pairs={{0,12},{4,8},{8,4},{12,0},{16,28},{20,24},{24,20},{28,16},{1,13},{... | collective-permute-start | bytes 405512 | tf_op jit(solution)/shard_map/ppermute | solution.py:296
  13.3 7.0 %collective-permute-start.3 = (f32[264,128]{1,0:T(8,128)S(1)}, f32[264,128]{1,0:T(8,128)S(1)}, u32[]{:S(2)}, u32[]{:S(2)}) collective-permute-start(f32[264,128]{1,0:T(8,128)S(1)} %shard_map.95.refs_4_.refs_0_), channel_id=1, source_target_pairs={{0,24},{4,28},{8,16},{12,20},{16,8},{20,12},{24,0},{28,4},{1,25},{... | collective-permute-start | bytes 405512 | tf_op jit(solution)/shard_map/ppermute | solution.py:296
  20.4 7.3 %collective-permute-start.4 = (f32[256,128]{1,0:T(8,128)S(1)}, f32[256,128]{1,0:T(8,128)S(1)}, u32[]{:S(2)}, u32[]{:S(2)}) collective-permute-start(f32[256,128]{1,0:T(8,128)S(1)} %get-tuple-element.53), channel_id=1, source_target_pairs={{0,4},{4,0},{8,12},{12,8},{16,20},{20,16},{24,28},{28,24},{1,5},{5... | collective-permute-start | bytes 393224 | tf_op jit(solution)/shard_map/ppermute | solution.py:296
  22.1 6.0 %collective-permute-start.5 = (f32[256,128]{1,0:T(8,128)S(1)}, f32[256,128]{1,0:T(8,128)S(1)}, u32[]{:S(2)}, u32[]{:S(2)}) collective-permute-start(f32[256,128]{1,0:T(8,128)S(1)} %get-tuple-element.54), channel_id=1, source_target_pairs={{0,8},{4,12},{8,0},{12,4},{16,24},{20,28},{24,16},{28,20},{1,9},{5... | collective-permute-start | bytes 393224 | tf_op jit(solution)/shard_map/ppermute | solution.py:296
  23.5 5.9 %collective-permute-start.6 = (f32[256,128]{1,0:T(8,128)S(1)}, f32[256,128]{1,0:T(8,128)S(1)}, u32[]{:S(2)}, u32[]{:S(2)}) collective-permute-start(f32[256,128]{1,0:T(8,128)S(1)} %get-tuple-element.58), channel_id=1, source_target_pairs={{0,12},{4,8},{8,4},{12,0},{16,28},{20,24},{24,20},{28,16},{1,13},{... | collective-permute-start | bytes 393224 | tf_op jit(solution)/shard_map/ppermute | solution.py:296
  29.7 1.9 %collective-permute-start.7 = (f32[8,128]{1,0:T(8,128)S(1)}, f32[8,128]{1,0:T(8,128)S(1)}, u32[]{:S(2)}, u32[]{:S(2)}) collective-permute-start(f32[8,128]{1,0:T(8,128)S(1)} %get-tuple-element.62.refs_6_), channel_id=1, source_target_pairs={{0,1},{1,0},{2,3},{3,2},{4,5},{5,4},{6,7},{7,6},{8,9},{9,8},{10,11... | collective-permute-start | bytes 12296 | tf_op jit(solution)/shard_map/ppermute | solution.py:296
  29.8 3.7 %collective-permute-start.8 = (f32[8,128]{1,0:T(8,128)S(1)}, f32[8,128]{1,0:T(8,128)S(1)}, u32[]{:S(2)}, u32[]{:S(2)}) collective-permute-start(f32[8,128]{1,0:T(8,128)S(1)} %get-tuple-element.62.refs_6_), channel_id=1, source_target_pairs={{0,2},{1,3},{2,0},{3,1},{4,6},{5,7},{6,4},{7,5},{8,10},{9,11},{10,... | collective-permute-start | bytes 12296 | tf_op jit(solution)/shard_map/ppermute | solution.py:296
  31.3 3.0 %collective-permute-start.9 = (f32[8,128]{1,0:T(8,128)S(1)}, f32[8,128]{1,0:T(8,128)S(1)}, u32[]{:S(2)}, u32[]{:S(2)}) collective-permute-start(f32[8,128]{1,0:T(8,128)S(1)} %get-tuple-element.62.refs_6_), channel_id=1, source_target_pairs={{0,3},{1,2},{2,1},{3,0},{4,7},{5,6},{6,5},{7,4},{8,11},{9,10},{10,... | collective-permute-start | bytes 12296 | tf_op jit(solution)/shard_map/ppermute | solution.py:296
  34.9 5.7 %collective-permute-start.10 = (f32[264,128]{1,0:T(8,128)S(1)}, f32[264,128]{1,0:T(8,128)S(1)}, u32[]{:S(2)}, u32[]{:S(2)}) collective-permute-start(f32[264,128]{1,0:T(8,128)S(1)} %get-tuple-element.69), channel_id=1, source_target_pairs={{0,4},{4,0},{8,12},{12,8},{16,20},{20,16},{24,28},{28,24},{1,5},{5... | collective-permute-start | bytes 405512 | tf_op jit(solution)/shard_map/ppermute | solution.py:296
  36.2 6.5 %collective-permute-start.11 = (f32[264,128]{1,0:T(8,128)S(1)}, f32[264,128]{1,0:T(8,128)S(1)}, u32[]{:S(2)}, u32[]{:S(2)}) collective-permute-start(f32[264,128]{1,0:T(8,128)S(1)} %get-tuple-element.70), channel_id=1, source_target_pairs={{0,8},{4,12},{8,0},{12,4},{16,24},{20,28},{24,16},{28,20},{1,9},{5... | collective-permute-start | bytes 405512 | tf_op jit(solution)/shard_map/ppermute | solution.py:296
  36.9 7.8 %collective-permute-start.12 = (f32[264,128]{1,0:T(8,128)S(1)}, f32[264,128]{1,0:T(8,128)S(1)}, u32[]{:S(2)}, u32[]{:S(2)}) collective-permute-start(f32[264,128]{1,0:T(8,128)S(1)} %get-tuple-element.71), channel_id=1, source_target_pairs={{0,12},{4,8},{8,4},{12,0},{16,28},{20,24},{24,20},{28,16},{1,13},{... | collective-permute-start | bytes 405512 | tf_op jit(solution)/shard_map/ppermute | solution.py:296
  44.7 6.9 %collective-permute-start.13 = (f32[264,128]{1,0:T(8,128)S(1)}, f32[264,128]{1,0:T(8,128)S(1)}, u32[]{:S(2)}, u32[]{:S(2)}) collective-permute-start(f32[264,128]{1,0:T(8,128)S(1)} %shard_map.101.refs_2_), channel_id=1, source_target_pairs={{0,24},{4,28},{8,16},{12,20},{16,8},{20,12},{24,0},{28,4},{1,25},{... | collective-permute-start | bytes 405512 | tf_op jit(solution)/shard_map/ppermute | solution.py:296
  51.8 5.7 %collective-permute-start.16 = (f32[256,128]{1,0:T(8,128)S(1)}, f32[256,128]{1,0:T(8,128)S(1)}, u32[]{:S(2)}, u32[]{:S(2)}) collective-permute-start(f32[256,128]{1,0:T(8,128)S(1)} %get-tuple-element.75), channel_id=1, source_target_pairs={{0,4},{4,0},{8,12},{12,8},{16,20},{20,16},{24,28},{28,24},{1,5},{5... | collective-permute-start | bytes 393224 | tf_op jit(solution)/shard_map/ppermute | solution.py:296
  53.1 6.4 %collective-permute-start.15 = (f32[256,128]{1,0:T(8,128)S(1)}, f32[256,128]{1,0:T(8,128)S(1)}, u32[]{:S(2)}, u32[]{:S(2)}) collective-permute-start(f32[256,128]{1,0:T(8,128)S(1)} %get-tuple-element.73), channel_id=1, source_target_pairs={{0,8},{4,12},{8,0},{12,4},{16,24},{20,28},{24,16},{28,20},{1,9},{5... | collective-permute-start | bytes 393224 | tf_op jit(solution)/shard_map/ppermute | solution.py:296
  54.6 6.2 %collective-permute-start.14 = (f32[256,128]{1,0:T(8,128)S(1)}, f32[256,128]{1,0:T(8,128)S(1)}, u32[]{:S(2)}, u32[]{:S(2)}) collective-permute-start(f32[256,128]{1,0:T(8,128)S(1)} %get-tuple-element.72), channel_id=1, source_target_pairs={{0,12},{4,8},{8,4},{12,0},{16,28},{20,24},{24,20},{28,16},{1,13},{... | collective-permute-start | bytes 393224 | tf_op jit(solution)/shard_map/ppermute | solution.py:296

commit v4 on v3

--- a/solution.py
+++ b/solution.py
@@ -93,6 +93,7 @@
         self.bits = [group << i for i in range(30) if group << i < seq]
         self.swaps = [bit | (bit // 2 if bit == group else 0) for bit in self.bits]
         self.state_rows = self.own * HEAD_DIM
+        self.last = group // 2
         self.body = slice(0, self.state_rows)
         self.tail = slice(self.state_rows, self.state_rows + TAIL)
 
@@ -126,53 +127,43 @@
     return total
 
 
-def full_count(plan, totals):
-    count = totals[0][plan.tail, :]
-    for other in totals[1:]:
-        count = count + other[plan.tail, :]
-    return count[0:1, :]
-
-
-def state_kernel(plan, k_hbm, v_hbm, mask_hbm, *refs):
+def state_kernel(plan, k_hbm, v_hbm, *refs):
     group = plan.group
-    out, (k, v, mask, sems) = refs[:group], refs[group:]
-    seat = [lax.axis_index("seq")]
+    out, (k, v, sems) = refs[:group], refs[group:]
+    seat = lax.axis_index("seq")
     pair = min(group, 2)
     copies = {}
     for x in range(0, group, pair):
-        cols = plan.share(seat[0], x, pair)
+        cols = plan.share(seat, x, pair)
         copies[x] = [
             pltpu.make_async_copy(src.at[:, cols], dst.at[:, cols], sems.at[i, x])
             for i, (src, dst) in enumerate(((k_hbm, k), (v_hbm, v)))
         ]
         for copy in copies[x]:
             copy.start()
-    mask_copy = pltpu.make_async_copy(mask_hbm, mask, sems.at[0, group])
-    mask_copy.start()
     for x in range(group):
         for copy in copies.get(x, ()):
             copy.wait()
         for i in range(plan.own):
-            cols = head_cols(plan.head_of(seat[0], x, i))
+            cols = head_cols(plan.head_of(seat, x, i))
             out[x][rows_of(i), :] = dot(split(k[:, cols]), split(v[:, cols]), TN)
-    mask_copy.wait()
-    count = jnp.sum(mask[...].astype(f32))
-    for x in range(group):
-        out[x][plan.tail, :] = jnp.full((TAIL, HEAD_DIM), count, f32)
-
-
-def local_kernel(plan, seat, q_hbm, k, v, target_hbm, gain, mask, q, scores, local, aim, target, sems):
+
+
+def local_kernel(plan, seat, q_hbm, k, v, target_hbm, gain, mask, q, flipped, scores, local, aim, count, target, sems):
     copies = [
         pltpu.make_async_copy(src, dst, sems.at[i]) for i, (src, dst) in enumerate(((q_hbm, q), (target_hbm, target)))
     ]
     for copy in copies:
         copy.start()
     causal = causal_mask(plan.length)
-    valid = column(mask[...].astype(f32), plan.length)
+    valid = mask[...].astype(f32)
+    count[...] = jnp.full((TAIL, HEAD_DIM), jnp.sum(valid), f32)
+    valid = column(valid, plan.length)
     for copy in copies:
         copy.wait()
     for h in range(plan.heads):
         cols = head_cols(h)
+        flipped[h] = q[:, cols].T
         s = dot(split(q[:, cols]), split(k[:, cols]), NT)
         s = jnp.where(causal, s, 0.0)
         scores[h] = s
@@ -181,7 +172,10 @@
 
 
 def total_kernel(plan, seat, *refs):
-    refs[-1][...] = pair_sum(r[...] for r in refs[: plan.group])
+    parts, out = refs[:-1], refs[-1]
+    out[plan.body, :] = pair_sum(r[plan.body, :] for r in parts)
+    if out.shape[0] > plan.state_rows:
+        out[plan.tail, :] = parts[0][plan.tail, :] + parts[plan.last][plan.tail, :]
 
 
 def prior_kernel(plan, seat, *refs):
@@ -219,31 +213,30 @@
         sums[1][...] = dots
 
 
-def scales(plan, stats, row, count):
-    squares, dots = stats[pl.ds(row, 1), :], stats[pl.ds(row + 1, 1), :]
+def scales(plan, stats):
+    squares, dots = stats[0:1, :], stats[1:2, :]
     inverse_rms = lax.rsqrt(squares / plan.width + epsilon)
-    left = (plan.tokens / count) * inverse_rms
-    right = left * (inverse_rms * inverse_rms * dots / plan.width)
-    return left, right, inverse_rms * dots
-
-
-def grad_kernel(plan, seat, q, aim, *refs):
+    loss = inverse_rms * dots
+    return inverse_rms, inverse_rms * inverse_rms * loss / plan.width, loss
+
+
+def grad_kernel(plan, seat, flipped, aim, count, *refs):
     refs = list(refs)
     take = lambda n: [refs.pop(0) for _ in range(n)]
-    attended, totals, stat_parts = take(plan.group), take(1 + len(plan.swaps)), take(plan.head)
-    (grad,), out = take(1), take(plan.group)
-    (stats,) = refs
-    stats[...] = pair_sum(r[...] for r in stat_parts)
-    left, right, losses = scales(plan, stats, 0, full_count(plan, totals))
+    attended, stat_parts, (grad,), out = take(plan.group), take(plan.head), take(1), take(plan.group)
+    left, right, losses = scales(plan, pair_sum(r[...] for r in stat_parts))
     left, right = column(left, plan.length), column(right, plan.length)
-    loss = jnp.sum(losses)
+    row = lax.broadcasted_iota(jnp.int32, (TAIL, HEAD_DIM), 0)
+    tail = jnp.where(row == 0, jnp.sum(losses), count[...])
     for x in range(plan.group):
         for i in range(plan.own):
-            cols = head_cols(plan.head_of(seat[0], x, i))
+            h = plan.head_of(seat[0], x, i)
+            cols = head_cols(h)
             g = left * aim[:, cols] - right * attended[x][:, rows_of(i)]
             grad[:, cols] = g
-            out[x][rows_of(i), :] = dot(split(q[:, cols]), split(g), TN)
-        out[x][plan.tail, :] = jnp.full((TAIL, HEAD_DIM), loss, f32)
+            out[x][rows_of(i), :] = dot(split(flipped[h]), split(g), NN)
+        if x in (0, plan.last):
+            out[x][plan.tail, :] = tail
 
 
 def local_grad_kernel(plan, seat, q, k, v, grad, scores, *refs):
@@ -264,30 +257,44 @@
 def later_kernel(plan, seat, *refs):
     group = plan.group
     states, totals, outs = refs[:group], refs[group : -group - 1], refs[-group:]
-    outer = outer_sum(plan, seat[0], True, totals)
+    outer = outer_sum(plan, seat[0], True, totals[1:])
+    tail = totals[0][plan.tail, :]
+    for other in totals[1:]:
+        tail = tail + other[plan.tail, :]
     for x in range(group):
-        outs[x][...] = state_at(plan, seat[0], True, x, outer, states)
-
-
-def loss_kernel(plan, seat, *refs):
-    n = 1 + len(plan.swaps)
-    refs[-1][...] = (full_count(plan, refs[n : 2 * n]) / full_count(plan, refs[:n]))[:, 0:1]
-
-
-def final_kernel(plan, which, seat, k, v, part_k, part_v, *refs):
+        outs[x][plan.body, :] = state_at(plan, seat[0], True, x, outer, states)
+        if x == min(1, group - 1):
+            outs[x][plan.tail, :] = tail
+
+
+def final_kernel(plan, which, seat, k, v, part_k, part_v, sent, *refs):
     n = len(which)
-    later = refs[:n]
-    grad_k, grad_v, block_k, block_v, sems = refs[-5:]
+    first = which[0] == 0
+    later, refs = list(refs[:n]), refs[n:]
+    if first:
+        (part_q, loss, grad_q, grad_k, grad_v, block_k, block_v, block_q, sems) = refs
+        tail = later[-1][plan.tail, :]
+    else:
+        (tail_ref, _, _, grad_k, grad_v, block_k, block_v, sems) = refs
+        tail = tail_ref[plan.tail, :]
+    if plan.group > 1:
+        tail = sent[plan.tail, :] + tail
+    factor = plan.tokens / tail[1:2, 0:1]
     copies = []
     for j, x in enumerate(which):
         for i in range(plan.own):
             cols = head_cols(plan.head_of(seat[0], x, i))
             state = split(later[j][rows_of(i), :])
-            block_k[j, :, rows_of(i)] = part_k[:, cols] + dot(split(v[:, cols]), state, NT)
-            block_v[j, :, rows_of(i)] = part_v[:, cols] + dot(split(k[:, cols]), state, NN)
+            block_k[j, :, rows_of(i)] = factor * (part_k[:, cols] + dot(split(v[:, cols]), state, NT))
+            block_v[j, :, rows_of(i)] = factor * (part_v[:, cols] + dot(split(k[:, cols]), state, NN))
         for m, (block, out) in enumerate(((block_k, grad_k), (block_v, grad_v))):
             copies.append(pltpu.make_async_copy(block.at[j], out.at[:, plan.share(seat[0], x)], sems.at[m, j]))
             copies[-1].start()
+    if first:
+        block_q[...] = factor * part_q[...]
+        copies.append(pltpu.make_async_copy(block_q, grad_q, sems.at[2, 0]))
+        copies[-1].start()
+        loss[...] = tail[0:1, 0:1] / tail[1:2, 0:1]
     for copy in copies:
         copy.wait()
 
@@ -327,18 +334,17 @@
 
     *kv, key_rows, value_rows = call(
         bind(state_kernel),
-        [sum_shape] * group + [wide] * 2,
+        [state] * group + [wide] * 2,
         product,
         None,
         in_hbm(key_rows),
         in_hbm(value_rows),
-        in_hbm(mask),
-        specs=[ANY] * 3,
-        scratch=[pltpu.VMEM((1, length), jnp.int32), pltpu.SemaphoreType.DMA((2, group + 1))],
-    )
-    queries, scores, local, aim = call(
+        specs=[ANY] * 2,
+        scratch=[pltpu.SemaphoreType.DMA((2, group))],
+    )
+    queries, flipped, scores, local, aim, count = call(
         bind(local_kernel),
-        [wide, shape(heads, length, length), wide, wide],
+        [wide, shape(heads, HEAD_DIM, length), shape(heads, length, length), wide, wide, shape(TAIL, HEAD_DIM)],
         2 * product,
         seat,
         in_hbm(queries),
@@ -351,7 +357,7 @@
         scratch=[pltpu.VMEM((length, columns), f32), pltpu.SemaphoreType.DMA((2,))],
     )
     kv = swap_all(kv, "seq")
-    (total,) = call(bind(total_kernel), [sum_shape], 0, seat, *kv)
+    (total,) = call(bind(total_kernel), [state], 0, seat, *kv)
     totals = swap_totals(plan, total)
     priors = call(bind(prior_kernel), [state] * group, 0, seat, *kv, *totals[1:])
     priors = swap_all(priors, "seq")
@@ -383,17 +389,16 @@
     stats = swap_all([stats] * head_count, "head")
     grad, *states = call(
         bind(grad_kernel),
-        [wide] + [sum_shape] * group,
+        [wide] + [sum_shape if x in (0, plan.last) else state for x in range(group)],
         product,
         seat,
-        queries,
+        flipped,
         aim,
+        count,
         *attended,
-        *totals,
         *stats,
-        scratch=[pltpu.VMEM((TAIL, length), f32)],
-    )
-    grad_query, part_key, part_value = call(
+    )
+    part_query, part_key, part_value = call(
         bind(local_grad_kernel), [wide] * 3, 5 * product, seat, queries, key_rows, value_rows, grad, scores, *priors
     )
     states = swap_all(states, "seq")
@@ -401,20 +406,33 @@
     grad_totals = swap_totals(plan, grad_total)
     later = call(
         bind(later_kernel),
-        [state] * group,
+        [sum_shape if x == min(1, group - 1) else state for x in range(group)],
         0,
         seat,
         *states,
-        *grad_totals[1:],
+        *grad_totals,
         part_key,
-        specs=[VMEM] * (group + len(plan.swaps)) + [ANY],
-    )
-    (loss,) = call(bind(loss_kernel), [shape(1, 1)], 0, seat, *totals, *grad_totals)
+        specs=[VMEM] * (group + len(grad_totals)) + [ANY],
+    )
+    sent = later[min(1, group - 1)]
     later = swap_all(later, "seq")
     grads = []
     for which in [early[:2], *([x] for x in early[2:]), late]:
         block = pltpu.VMEM((len(which), length, plan.state_rows), f32)
-        inputs = [key_rows, value_rows, part_key, part_value, *(later[x] for x in which)]
+        inputs = [key_rows, value_rows, part_key, part_value, sent, *(later[x] for x in which)]
+        if not grads:
+            loss, grad_query, *grads = call(
+                functools.partial(final_kernel, plan, which),
+                [shape(1, 1), wide, wide, wide],
+                2 * product * len(which) // group,
+                seat,
+                *inputs,
+                part_query,
+                out_specs=[VMEM] + [ANY] * 3,
+                scratch=[block, block, pltpu.VMEM((length, columns), f32), pltpu.SemaphoreType.DMA((3, len(which)))],
+            )
+            continue
+        inputs.append(later[1])
         grads = call(
             functools.partial(final_kernel, plan, which),
             [wide] * 2,
@@ -422,10 +440,10 @@
             seat,
             *inputs,
             *grads,
-            specs=[VMEM] * len(inputs) + [ANY] * len(grads),
+            specs=[VMEM] * len(inputs) + [ANY] * 2,
             out_specs=[ANY] * 2,
             scratch=[block, block, pltpu.SemaphoreType.DMA((2, len(which)))],
-            aliases={1 + len(inputs) + i: i for i in range(len(grads))},
+            aliases={1 + len(inputs) + i: i for i in range(2)},
         )
     grad_key, grad_value = grads
     return (grad_query, grad_key, grad_value, loss[0, 0])

time: 62 us -> 60.7 us (0.979)
  waiting for transfers between devices: 23.3 us -> 22.5 us
  Pallas kernels: 13.6 us -> 12.8 us
    ppermute x17, waiting for transfers between devices: 23.3 us -> 22.5 us  [swap(): lax.ppermute(value, axis, [(i, i ^ step) for i in range(lax.axis_size(axi...]
    pallas_call x14 -> x13, Pallas kernels: 13.6 us -> 12.8 us  [call(): pl.pallas_call(kernel, out_shape=outs, in_specs=[SMEM] * len(place) + spe...]
  transfers between devices with their start and end apart: 17 -> 17, of which waited for: 15 -> 13; matrix products, arithmetic and copies ran while one was open for 0% -> 0% of each run, Pallas kernels for 16% -> 15%
where the time goes in v4:
time: 60.7 us; the launch traced here: 60.5 us
  starting transfers between devices  24.4 us (40%)
  waiting for transfers between devices  22.5 us (37%)
  Pallas kernels  12.8 us (21%)
  between operations  0.72 us (1%)
    ppermute x17, starting transfers between devices, swap(): lax.ppermute(value, axis, [(i, i ^ step) for i in range(lax.axis_size(axi...  24.4 us
    ppermute x17, waiting for transfers between devices, swap(): lax.ppermute(value, axis, [(i, i ^ step) for i in range(lax.axis_size(axi...  22.5 us
    pallas_call x13, Pallas kernels, call(): pl.pallas_call(kernel, out_shape=outs, in_specs=[SMEM] * len(place) + spe...  12.8 us
  transfers between devices with their start and end apart: 17, of which 13 were waited for; matrix products, arithmetic and copies ran while one was open for 0% of the time, Pallas kernels for 15%

profile of v4, /device:TPU:0, one launch (start us, length us, event | category | flops | bytes accessed | tf_op | source)
XLA Modules:
  0.0 60.5 jit_solution(17540330753377347504)
XLA Ops:
  0.6 1.7 %shard_map.93 = (f32[256,128]{1,0:T(8,128)S(1)}, f32[256,128]{1,0:T(8,128)S(1)}, f32[256,128]{1,0:T(8,128)S(1)}, f32[256,128]{1,0:T(8,128)S(1)}, f32[128,1024]{1,0:T(8,128)S(1)}, /*index=5*/f32[128,1024]{1,0:T(8,128)S(1)}) custom-call(f32[128,1024]{1,0:T(8,128)} %k_hbm.1, f32[128,1024]{1,0:T(8,128)} %v_hbm.1), custom_call_target="tpu_custom_call" | custom-call | flops 100663296 | bytes 2621440 | tf_op jit(solution)/shard_map/pallas_call | solution.py:59
  2.3 3.0 %collective-permute-start = (f32[256,128]{1,0:T(8,128)S(1)}, f32[256,128]{1,0:T(8,128)S(1)}, u32[]{:S(2)}, u32[]{:S(2)}) collective-permute-start(f32[256,128]{1,0:T(8,128)S(1)} %get-tuple-element.55), channel_id=1, source_target_pairs={{0,4},{4,0},{8,12},{12,8},{16,20},{20,16},{24,28},{28,24},{1,5},{5... | collective-permute-start | bytes 393224 | tf_op jit(solution)/shard_map/ppermute | solution.py:303
  5.4 1.6 %collective-permute-start.1 = (f32[256,128]{1,0:T(8,128)S(1)}, f32[256,128]{1,0:T(8,128)S(1)}, u32[]{:S(2)}, u32[]{:S(2)}) collective-permute-start(f32[256,128]{1,0:T(8,128)S(1)} %get-tuple-element.56), channel_id=1, source_target_pairs={{0,8},{4,12},{8,0},{12,4},{16,24},{20,28},{24,16},{28,20},{1,9},{5... | collective-permute-start | bytes 393224 | tf_op jit(solution)/shard_map/ppermute | solution.py:303
  7.0 1.9 %collective-permute-done.refs_1_ = f32[256,128]{1,0:T(8,128)S(1)} collective-permute-done((f32[256,128]{1,0:T(8,128)S(1)}, f32[256,128]{1,0:T(8,128)S(1)}, u32[]{:S(2)}, u32[]{:S(2)}) %collective-permute-start) | collective-permute-done | bytes 131104 | tf_op jit(solution)/shard_map/ppermute | solution.py:303
  8.9 2.9 %collective-permute-done.1.refs_2_ = f32[256,128]{1,0:T(8,128)S(1)} collective-permute-done((f32[256,128]{1,0:T(8,128)S(1)}, f32[256,128]{1,0:T(8,128)S(1)}, u32[]{:S(2)}, u32[]{:S(2)}) %collective-permute-start.1) | collective-permute-done | bytes 131104 | tf_op jit(solution)/shard_map/ppermute | solution.py:303
  11.7 1.2 %collective-permute-done.2.refs_3_ = f32[256,128]{1,0:T(8,128)S(1)} collective-permute-done((f32[256,128]{1,0:T(8,128)S(1)}, f32[256,128]{1,0:T(8,128)S(1)}, u32[]{:S(2)}, u32[]{:S(2)}) %collective-permute-start.2) | collective-permute-done | bytes 131104 | tf_op jit(solution)/shard_map/ppermute | solution.py:303
  13.0 3.8 %collective-permute-start.3 = (f32[256,128]{1,0:T(8,128)S(1)}, f32[256,128]{1,0:T(8,128)S(1)}, u32[]{:S(2)}, u32[]{:S(2)}) collective-permute-start(f32[256,128]{1,0:T(8,128)S(1)} %shard_map.95), channel_id=1, source_target_pairs={{0,24},{4,28},{8,16},{12,20},{16,8},{20,12},{24,0},{28,4},{1,25},{... | collective-permute-start | bytes 393224 | tf_op jit(solution)/shard_map/ppermute | solution.py:303
  16.8 3.1 %collective-permute-done.3.refs_4_ = f32[256,128]{1,0:T(8,128)S(1)} collective-permute-done((f32[256,128]{1,0:T(8,128)S(1)}, f32[256,128]{1,0:T(8,128)S(1)}, u32[]{:S(2)}, u32[]{:S(2)}) %collective-permute-start.3) | collective-permute-done | bytes 131104 | tf_op jit(solution)/shard_map/ppermute | solution.py:303
  20.0 1.7 %collective-permute-start.4 = (f32[256,128]{1,0:T(8,128)S(1)}, f32[256,128]{1,0:T(8,128)S(1)}, u32[]{:S(2)}, u32[]{:S(2)}) collective-permute-start(f32[256,128]{1,0:T(8,128)S(1)} %get-tuple-element.59), channel_id=1, source_target_pairs={{0,4},{4,0},{8,12},{12,8},{16,20},{20,16},{24,28},{28,24},{1,5},{5... | collective-permute-start | bytes 393224 | tf_op jit(solution)/shard_map/ppermute | solution.py:303
  21.8 1.3 %collective-permute-start.5 = (f32[256,128]{1,0:T(8,128)S(1)}, f32[256,128]{1,0:T(8,128)S(1)}, u32[]{:S(2)}, u32[]{:S(2)}) collective-permute-start(f32[256,128]{1,0:T(8,128)S(1)} %get-tuple-element.60), channel_id=1, source_target_pairs={{0,8},{4,12},{8,0},{12,4},{16,24},{20,28},{24,16},{28,20},{1,9},{5... | collective-permute-start | bytes 393224 | tf_op jit(solution)/shard_map/ppermute | solution.py:303
  23.6 3.7 %shard_map.94 = (f32[128,1024]{1,0:T(8,128)S(1)}, f32[8,128,128]{2,1,0:T(8,128)S(1)}, f32[8,128,128]{2,1,0:T(8,128)S(1)}, f32[128,1024]{1,0:T(8,128)S(1)}, f32[1...) custom-call(s32[1]{0:T(128)} %bitcast.seat, f32[128,1024]{1,0:T(8,128)} %q_hbm.1, f32[128,1024]{1,0:T(8,128)S(1)} %get-tuple-element.47.k, ...), custom_call_target="tpu_custom_call" | custom-call | flops 201326592 | bytes 4727296 | tf_op jit(solution)/shard_map/pallas_call | solution.py:59
  27.8 1.1 %collective-permute-done.6.refs_0_.refs_3_ = f32[256,128]{1,0:T(8,128)S(1)} collective-permute-done((f32[256,128]{1,0:T(8,128)S(1)}, f32[256,128]{1,0:T(8,128)S(1)}, u32[]{:S(2)}, u32[]{:S(2)}) %collective-permute-start.6) | collective-permute-done | bytes 131104 | tf_op jit(solution)/shard_map/ppermute | solution.py:303
  29.2 1.6 %collective-permute-start.8 = (f32[8,128]{1,0:T(8,128)S(1)}, f32[8,128]{1,0:T(8,128)S(1)}, u32[]{:S(2)}, u32[]{:S(2)}) collective-permute-start(f32[8,128]{1,0:T(8,128)S(1)} %get-tuple-element.68.refs_4_), channel_id=1, source_target_pairs={{0,2},{1,3},{2,0},{3,1},{4,6},{5,7},{6,4},{7,5},{8,10},{9,11},{10,... | collective-permute-start | bytes 12296 | tf_op jit(solution)/shard_map/ppermute | solution.py:303
  31.1 1.2 %collective-permute-done.9.refs_7_ = f32[8,128]{1,0:T(8,128)S(1)} collective-permute-done((f32[8,128]{1,0:T(8,128)S(1)}, f32[8,128]{1,0:T(8,128)S(1)}, u32[]{:S(2)}, u32[]{:S(2)}) %collective-permute-start.9) | collective-permute-done | bytes 4128 | tf_op jit(solution)/shard_map/ppermute | solution.py:303
  33.4 1.7 %collective-permute-start.11 = (f32[264,128]{1,0:T(8,128)S(1)}, f32[264,128]{1,0:T(8,128)S(1)}, u32[]{:S(2)}, u32[]{:S(2)}) collective-permute-start(f32[264,128]{1,0:T(8,128)S(1)} %get-tuple-element.75), channel_id=1, source_target_pairs={{0,8},{4,12},{8,0},{12,4},{16,24},{20,28},{24,16},{28,20},{1,9},{5... | collective-permute-start | bytes 405512 | tf_op jit(solution)/shard_map/ppermute | solution.py:303
  35.5 1.4 %collective-permute-start.12 = (f32[256,128]{1,0:T(8,128)S(1)}, f32[256,128]{1,0:T(8,128)S(1)}, u32[]{:S(2)}, u32[]{:S(2)}) collective-permute-start(f32[256,128]{1,0:T(8,128)S(1)} %get-tuple-element.76), channel_id=1, source_target_pairs={{0,12},{4,8},{8,4},{12,0},{16,28},{20,24},{24,20},{28,16},{1,13},{... | collective-permute-start | bytes 393224 | tf_op jit(solution)/shard_map/ppermute | solution.py:303
  37.0 5.9 %collective-permute-done.10.refs_1_ = f32[256,128]{1,0:T(8,128)S(1)} collective-permute-done((f32[256,128]{1,0:T(8,128)S(1)}, f32[256,128]{1,0:T(8,128)S(1)}, u32[]{:S(2)}, u32[]{:S(2)}) %collective-permute-start.10) | collective-permute-done | bytes 131104 | tf_op jit(solution)/shard_map/ppermute | solution.py:303
  43.0 3.3 %collective-permute-start.13 = (f32[264,128]{1,0:T(8,128)S(1)}, f32[264,128]{1,0:T(8,128)S(1)}, u32[]{:S(2)}, u32[]{:S(2)}) collective-permute-start(f32[264,128]{1,0:T(8,128)S(1)} %shard_map.101.refs_4_), channel_id=1, source_target_pairs={{0,24},{4,28},{8,16},{12,20},{16,8},{20,12},{24,0},{28,4},{1,25},{... | collective-permute-start | bytes 405512 | tf_op jit(solution)/shard_map/ppermute | solution.py:303
  46.2 2.3 %shard_map.100 = (f32[128,1024]{1,0:T(8,128)S(1)}, f32[128,1024]{1,0:T(8,128)S(1)}, f32[128,1024]{1,0:T(8,128)S(1)}) custom-call(s32[1]{0:T(128)} %bitcast.seat, f32[128,1024]{1,0:T(8,128)S(1)} %get-tuple-element.49.q, f32[128,1024]{1,0:T(8,128)S(1)} %get-tuple-element.47.k, f32[128,1024]{1,0:T(8,128)S(1)} %get-tuple-element.48.v, ...), custom_call_target="tpu_custom_call" | custom-call | flops 503316480 | bytes 4718592 | tf_op jit(solution)/shard_map/pallas_call | solution.py:59
  48.6 1.3 %collective-permute-done.13.refs_5_ = f32[264,128]{1,0:T(8,128)S(1)} collective-permute-done((f32[264,128]{1,0:T(8,128)S(1)}, f32[264,128]{1,0:T(8,128)S(1)}, u32[]{:S(2)}, u32[]{:S(2)}) %collective-permute-start.13) | collective-permute-done | bytes 135200 | tf_op jit(solution)/shard_map/ppermute | solution.py:303
  50.9 2.7 %collective-permute-start.16 = (f32[256,128]{1,0:T(8,128)S(1)}, f32[256,128]{1,0:T(8,128)S(1)}, u32[]{:S(2)}, u32[]{:S(2)}) collective-permute-start(f32[256,128]{1,0:T(8,128)S(1)} %get-tuple-element.82), channel_id=1, source_target_pairs={{0,8},{4,12},{8,0},{12,4},{16,24},{20,28},{24,16},{28,20},{1,9},{5... | collective-permute-start | bytes 393224 | tf_op jit(solution)/shard_map/ppermute | solution.py:303
  53.6 1.5 %collective-permute-done.14.refs_1_ = f32[264,128]{1,0:T(8,128)S(1)} collective-permute-done((f32[264,128]{1,0:T(8,128)S(1)}, f32[264,128]{1,0:T(8,128)S(1)}, u32[]{:S(2)}, u32[]{:S(2)}) %collective-permute-start.14) | collective-permute-done | bytes 135200 | tf_op jit(solution)/shard_map/ppermute | solution.py:303
  55.1 1.8 %shard_map.103 = (f32[1,1]{1,0:T(1,128)}, f32[128,1024]{1,0:T(8,128)}, f32[128,1024]{1,0:T(8,128)}, f32[128,1024]{1,0:T(8,128)}) custom-call(s32[1]{0:T(128)} %bitcast.seat, f32[128,1024]{1,0:T(8,128)S(1)} %get-tuple-element.47.k, f32[128,1024]{1,0:T(8,128)S(1)} %get-tuple-element.48.v, f32[128,1024]{1,0:T(8,128)S(1)} %get-tuple-element.71.refs_6_.part_k, ...), custom_call_target="tpu_custom_call" | custom-call | flops 100663296 | bytes 4595716 | tf_op jit(solution)/shard_map/pallas_call | solution.py:59
  56.9 1.1 %collective-permute-done.16.refs_0_ = f32[256,128]{1,0:T(8,128)S(1)} collective-permute-done((f32[256,128]{1,0:T(8,128)S(1)}, f32[256,128]{1,0:T(8,128)S(1)}, u32[]{:S(2)}, u32[]{:S(2)}) %collective-permute-start.16) | collective-permute-done | bytes 131104 | tf_op jit(solution)/shard_map/ppermute | solution.py:303
  (23 shorter events, 6.9 us)
Async XLA Ops:
  2.3 6.5 %collective-permute-start = (f32[256,128]{1,0:T(8,128)S(1)}, f32[256,128]{1,0:T(8,128)S(1)}, u32[]{:S(2)}, u32[]{:S(2)}) collective-permute-start(f32[256,128]{1,0:T(8,128)S(1)} %get-tuple-element.55), channel_id=1, source_target_pairs={{0,4},{4,0},{8,12},{12,8},{16,20},{20,16},{24,28},{28,24},{1,5},{5... | collective-permute-start | bytes 393224 | tf_op jit(solution)/shard_map/ppermute | solution.py:303
  5.4 6.4 %collective-permute-start.1 = (f32[256,128]{1,0:T(8,128)S(1)}, f32[256,128]{1,0:T(8,128)S(1)}, u32[]{:S(2)}, u32[]{:S(2)}) collective-permute-start(f32[256,128]{1,0:T(8,128)S(1)} %get-tuple-element.56), channel_id=1, source_target_pairs={{0,8},{4,12},{8,0},{12,4},{16,24},{20,28},{24,16},{28,20},{1,9},{5... | collective-permute-start | bytes 393224 | tf_op jit(solution)/shard_map/ppermute | solution.py:303
  7.0 6.0 %collective-permute-start.2 = (f32[256,128]{1,0:T(8,128)S(1)}, f32[256,128]{1,0:T(8,128)S(1)}, u32[]{:S(2)}, u32[]{:S(2)}) collective-permute-start(f32[256,128]{1,0:T(8,128)S(1)} %get-tuple-element.57), channel_id=1, source_target_pairs={{0,12},{4,8},{8,4},{12,0},{16,28},{20,24},{24,20},{28,16},{1,13},{... | collective-permute-start | bytes 393224 | tf_op jit(solution)/shard_map/ppermute | solution.py:303
  13.0 6.9 %collective-permute-start.3 = (f32[256,128]{1,0:T(8,128)S(1)}, f32[256,128]{1,0:T(8,128)S(1)}, u32[]{:S(2)}, u32[]{:S(2)}) collective-permute-start(f32[256,128]{1,0:T(8,128)S(1)} %shard_map.95), channel_id=1, source_target_pairs={{0,24},{4,28},{8,16},{12,20},{16,8},{20,12},{24,0},{28,4},{1,25},{... | collective-permute-start | bytes 393224 | tf_op jit(solution)/shard_map/ppermute | solution.py:303
  20.0 7.3 %collective-permute-start.4 = (f32[256,128]{1,0:T(8,128)S(1)}, f32[256,128]{1,0:T(8,128)S(1)}, u32[]{:S(2)}, u32[]{:S(2)}) collective-permute-start(f32[256,128]{1,0:T(8,128)S(1)} %get-tuple-element.59), channel_id=1, source_target_pairs={{0,4},{4,0},{8,12},{12,8},{16,20},{20,16},{24,28},{28,24},{1,5},{5... | collective-permute-start | bytes 393224 | tf_op jit(solution)/shard_map/ppermute | solution.py:303
  21.8 5.7 %collective-permute-start.5 = (f32[256,128]{1,0:T(8,128)S(1)}, f32[256,128]{1,0:T(8,128)S(1)}, u32[]{:S(2)}, u32[]{:S(2)}) collective-permute-start(f32[256,128]{1,0:T(8,128)S(1)} %get-tuple-element.60), channel_id=1, source_target_pairs={{0,8},{4,12},{8,0},{12,4},{16,24},{20,28},{24,16},{28,20},{1,9},{5... | collective-permute-start | bytes 393224 | tf_op jit(solution)/shard_map/ppermute | solution.py:303
  23.0 5.9 %collective-permute-start.6 = (f32[256,128]{1,0:T(8,128)S(1)}, f32[256,128]{1,0:T(8,128)S(1)}, u32[]{:S(2)}, u32[]{:S(2)}) collective-permute-start(f32[256,128]{1,0:T(8,128)S(1)} %get-tuple-element.64), channel_id=1, source_target_pairs={{0,12},{4,8},{8,4},{12,0},{16,28},{20,24},{24,20},{28,16},{1,13},{... | collective-permute-start | bytes 393224 | tf_op jit(solution)/shard_map/ppermute | solution.py:303
  29.2 3.1 %collective-permute-start.9 = (f32[8,128]{1,0:T(8,128)S(1)}, f32[8,128]{1,0:T(8,128)S(1)}, u32[]{:S(2)}, u32[]{:S(2)}) collective-permute-start(f32[8,128]{1,0:T(8,128)S(1)} %get-tuple-element.68.refs_4_), channel_id=1, source_target_pairs={{0,3},{1,2},{2,1},{3,0},{4,7},{5,6},{6,5},{7,4},{8,11},{9,10},{10,... | collective-permute-start | bytes 12296 | tf_op jit(solution)/shard_map/ppermute | solution.py:303
  29.2 3.7 %collective-permute-start.8 = (f32[8,128]{1,0:T(8,128)S(1)}, f32[8,128]{1,0:T(8,128)S(1)}, u32[]{:S(2)}, u32[]{:S(2)}) collective-permute-start(f32[8,128]{1,0:T(8,128)S(1)} %get-tuple-element.68.refs_4_), channel_id=1, source_target_pairs={{0,2},{1,3},{2,0},{3,1},{4,6},{5,7},{6,4},{7,5},{8,10},{9,11},{10,... | collective-permute-start | bytes 12296 | tf_op jit(solution)/shard_map/ppermute | solution.py:303
  30.8 2.1 %collective-permute-start.7 = (f32[8,128]{1,0:T(8,128)S(1)}, f32[8,128]{1,0:T(8,128)S(1)}, u32[]{:S(2)}, u32[]{:S(2)}) collective-permute-start(f32[8,128]{1,0:T(8,128)S(1)} %get-tuple-element.68.refs_4_), channel_id=1, source_target_pairs={{0,1},{1,0},{2,3},{3,2},{4,5},{5,4},{6,7},{7,6},{8,9},{9,8},{10,11... | collective-permute-start | bytes 12296 | tf_op jit(solution)/shard_map/ppermute | solution.py:303
  33.4 9.5 %collective-permute-start.11 = (f32[264,128]{1,0:T(8,128)S(1)}, f32[264,128]{1,0:T(8,128)S(1)}, u32[]{:S(2)}, u32[]{:S(2)}) collective-permute-start(f32[264,128]{1,0:T(8,128)S(1)} %get-tuple-element.75), channel_id=1, source_target_pairs={{0,8},{4,12},{8,0},{12,4},{16,24},{20,28},{24,16},{28,20},{1,9},{5... | collective-permute-start | bytes 405512 | tf_op jit(solution)/shard_map/ppermute | solution.py:303
  35.1 7.8 %collective-permute-start.10 = (f32[256,128]{1,0:T(8,128)S(1)}, f32[256,128]{1,0:T(8,128)S(1)}, u32[]{:S(2)}, u32[]{:S(2)}) collective-permute-start(f32[256,128]{1,0:T(8,128)S(1)} %get-tuple-element.74), channel_id=1, source_target_pairs={{0,4},{4,0},{8,12},{12,8},{16,20},{20,16},{24,28},{28,24},{1,5},{5... | collective-permute-start | bytes 393224 | tf_op jit(solution)/shard_map/ppermute | solution.py:303
  35.5 7.4 %collective-permute-start.12 = (f32[256,128]{1,0:T(8,128)S(1)}, f32[256,128]{1,0:T(8,128)S(1)}, u32[]{:S(2)}, u32[]{:S(2)}) collective-permute-start(f32[256,128]{1,0:T(8,128)S(1)} %get-tuple-element.76), channel_id=1, source_target_pairs={{0,12},{4,8},{8,4},{12,0},{16,28},{20,24},{24,20},{28,16},{1,13},{... | collective-permute-start | bytes 393224 | tf_op jit(solution)/shard_map/ppermute | solution.py:303
  43.0 6.9 %collective-permute-start.13 = (f32[264,128]{1,0:T(8,128)S(1)}, f32[264,128]{1,0:T(8,128)S(1)}, u32[]{:S(2)}, u32[]{:S(2)}) collective-permute-start(f32[264,128]{1,0:T(8,128)S(1)} %shard_map.101.refs_4_), channel_id=1, source_target_pairs={{0,24},{4,28},{8,16},{12,20},{16,8},{20,12},{24,0},{28,4},{1,25},{... | collective-permute-start | bytes 405512 | tf_op jit(solution)/shard_map/ppermute | solution.py:303
  50.0 5.1 %collective-permute-start.14 = (f32[264,128]{1,0:T(8,128)S(1)}, f32[264,128]{1,0:T(8,128)S(1)}, u32[]{:S(2)}, u32[]{:S(2)}) collective-permute-start(f32[264,128]{1,0:T(8,128)S(1)} %get-tuple-element.77.sent), channel_id=1, source_target_pairs={{0,4},{4,0},{8,12},{12,8},{16,20},{20,16},{24,28},{28,24},{1,5},{5... | collective-permute-start | bytes 405512 | tf_op jit(solution)/shard_map/ppermute | solution.py:303
  50.9 7.1 %collective-permute-start.16 = (f32[256,128]{1,0:T(8,128)S(1)}, f32[256,128]{1,0:T(8,128)S(1)}, u32[]{:S(2)}, u32[]{:S(2)}) collective-permute-start(f32[256,128]{1,0:T(8,128)S(1)} %get-tuple-element.82), channel_id=1, source_target_pairs={{0,8},{4,12},{8,0},{12,4},{16,24},{20,28},{24,16},{28,20},{1,9},{5... | collective-permute-start | bytes 393224 | tf_op jit(solution)/shard_map/ppermute | solution.py:303
  53.6 5.9 %collective-permute-start.15 = (f32[256,128]{1,0:T(8,128)S(1)}, f32[256,128]{1,0:T(8,128)S(1)}, u32[]{:S(2)}, u32[]{:S(2)}) collective-permute-start(f32[256,128]{1,0:T(8,128)S(1)} %get-tuple-element.81), channel_id=1, source_target_pairs={{0,12},{4,8},{8,4},{12,0},{16,28},{20,24},{24,20},{28,16},{1,13},{... | collective-permute-start | bytes 393224 | tf_op jit(solution)/shard_map/ppermute | solution.py:303

commit v5 on v4

--- a/solution.py
+++ b/solution.py
@@ -73,7 +73,7 @@
 
 
 def column(row, n):
-    return jnp.broadcast_to(row, (n, n)).T
+    return jnp.broadcast_to(row, (HEAD_DIM, n)).T
 
 
 def pair_sum(parts):

time: 60.7 us -> 60.7 us (level)
  no operation moved by 1% of the time
where the time goes in v5:
time: 60.7 us; the launch traced here: 60.5 us
  starting transfers between devices  24.4 us (40%)
  waiting for transfers between devices  22.5 us (37%)
  Pallas kernels  12.8 us (21%)
  between operations  0.72 us (1%)
    ppermute x17, starting transfers between devices, swap(): lax.ppermute(value, axis, [(i, i ^ step) for i in range(lax.axis_size(axi...  24.4 us
    ppermute x17, waiting for transfers between devices, swap(): lax.ppermute(value, axis, [(i, i ^ step) for i in range(lax.axis_size(axi...  22.5 us
    pallas_call x13, Pallas kernels, call(): pl.pallas_call(kernel, out_shape=outs, in_specs=[SMEM] * len(place) + spe...  12.8 us
  transfers between devices with their start and end apart: 17, of which 13 were waited for; matrix products, arithmetic and copies ran while one was open for 0% of the time, Pallas kernels for 15%

profile of v5, /device:TPU:0, one launch (start us, length us, event | category | flops | bytes accessed | tf_op | source)
XLA Modules:
  0.0 60.5 jit_solution(17540330753377347504)
XLA Ops:
  0.6 1.7 %shard_map.93 = (f32[256,128]{1,0:T(8,128)S(1)}, f32[256,128]{1,0:T(8,128)S(1)}, f32[256,128]{1,0:T(8,128)S(1)}, f32[256,128]{1,0:T(8,128)S(1)}, f32[128,1024]{1,0:T(8,128)S(1)}, /*index=5*/f32[128,1024]{1,0:T(8,128)S(1)}) custom-call(f32[128,1024]{1,0:T(8,128)} %k_hbm.1, f32[128,1024]{1,0:T(8,128)} %v_hbm.1), custom_call_target="tpu_custom_call" | custom-call | flops 100663296 | bytes 2621440 | tf_op jit(solution)/shard_map/pallas_call | solution.py:59
  2.3 3.0 %collective-permute-start = (f32[256,128]{1,0:T(8,128)S(1)}, f32[256,128]{1,0:T(8,128)S(1)}, u32[]{:S(2)}, u32[]{:S(2)}) collective-permute-start(f32[256,128]{1,0:T(8,128)S(1)} %get-tuple-element.55), channel_id=1, source_target_pairs={{0,4},{4,0},{8,12},{12,8},{16,20},{20,16},{24,28},{28,24},{1,5},{5... | collective-permute-start | bytes 393224 | tf_op jit(solution)/shard_map/ppermute | solution.py:303
  5.4 1.6 %collective-permute-start.1 = (f32[256,128]{1,0:T(8,128)S(1)}, f32[256,128]{1,0:T(8,128)S(1)}, u32[]{:S(2)}, u32[]{:S(2)}) collective-permute-start(f32[256,128]{1,0:T(8,128)S(1)} %get-tuple-element.56), channel_id=1, source_target_pairs={{0,8},{4,12},{8,0},{12,4},{16,24},{20,28},{24,16},{28,20},{1,9},{5... | collective-permute-start | bytes 393224 | tf_op jit(solution)/shard_map/ppermute | solution.py:303
  7.0 1.9 %collective-permute-done.refs_1_ = f32[256,128]{1,0:T(8,128)S(1)} collective-permute-done((f32[256,128]{1,0:T(8,128)S(1)}, f32[256,128]{1,0:T(8,128)S(1)}, u32[]{:S(2)}, u32[]{:S(2)}) %collective-permute-start) | collective-permute-done | bytes 131104 | tf_op jit(solution)/shard_map/ppermute | solution.py:303
  8.9 2.9 %collective-permute-done.1.refs_2_ = f32[256,128]{1,0:T(8,128)S(1)} collective-permute-done((f32[256,128]{1,0:T(8,128)S(1)}, f32[256,128]{1,0:T(8,128)S(1)}, u32[]{:S(2)}, u32[]{:S(2)}) %collective-permute-start.1) | collective-permute-done | bytes 131104 | tf_op jit(solution)/shard_map/ppermute | solution.py:303
  11.7 1.2 %collective-permute-done.2.refs_3_ = f32[256,128]{1,0:T(8,128)S(1)} collective-permute-done((f32[256,128]{1,0:T(8,128)S(1)}, f32[256,128]{1,0:T(8,128)S(1)}, u32[]{:S(2)}, u32[]{:S(2)}) %collective-permute-start.2) | collective-permute-done | bytes 131104 | tf_op jit(solution)/shard_map/ppermute | solution.py:303
  13.0 3.8 %collective-permute-start.3 = (f32[256,128]{1,0:T(8,128)S(1)}, f32[256,128]{1,0:T(8,128)S(1)}, u32[]{:S(2)}, u32[]{:S(2)}) collective-permute-start(f32[256,128]{1,0:T(8,128)S(1)} %shard_map.95), channel_id=1, source_target_pairs={{0,24},{4,28},{8,16},{12,20},{16,8},{20,12},{24,0},{28,4},{1,25},{... | collective-permute-start | bytes 393224 | tf_op jit(solution)/shard_map/ppermute | solution.py:303
  16.8 3.1 %collective-permute-done.3.refs_4_ = f32[256,128]{1,0:T(8,128)S(1)} collective-permute-done((f32[256,128]{1,0:T(8,128)S(1)}, f32[256,128]{1,0:T(8,128)S(1)}, u32[]{:S(2)}, u32[]{:S(2)}) %collective-permute-start.3) | collective-permute-done | bytes 131104 | tf_op jit(solution)/shard_map/ppermute | solution.py:303
  20.0 1.7 %collective-permute-start.4 = (f32[256,128]{1,0:T(8,128)S(1)}, f32[256,128]{1,0:T(8,128)S(1)}, u32[]{:S(2)}, u32[]{:S(2)}) collective-permute-start(f32[256,128]{1,0:T(8,128)S(1)} %get-tuple-element.59), channel_id=1, source_target_pairs={{0,4},{4,0},{8,12},{12,8},{16,20},{20,16},{24,28},{28,24},{1,5},{5... | collective-permute-start | bytes 393224 | tf_op jit(solution)/shard_map/ppermute | solution.py:303
  21.8 1.3 %collective-permute-start.5 = (f32[256,128]{1,0:T(8,128)S(1)}, f32[256,128]{1,0:T(8,128)S(1)}, u32[]{:S(2)}, u32[]{:S(2)}) collective-permute-start(f32[256,128]{1,0:T(8,128)S(1)} %get-tuple-element.60), channel_id=1, source_target_pairs={{0,8},{4,12},{8,0},{12,4},{16,24},{20,28},{24,16},{28,20},{1,9},{5... | collective-permute-start | bytes 393224 | tf_op jit(solution)/shard_map/ppermute | solution.py:303
  23.6 3.7 %shard_map.94 = (f32[128,1024]{1,0:T(8,128)S(1)}, f32[8,128,128]{2,1,0:T(8,128)S(1)}, f32[8,128,128]{2,1,0:T(8,128)S(1)}, f32[128,1024]{1,0:T(8,128)S(1)}, f32[1...) custom-call(s32[1]{0:T(128)} %bitcast.seat, f32[128,1024]{1,0:T(8,128)} %q_hbm.1, f32[128,1024]{1,0:T(8,128)S(1)} %get-tuple-element.47.k, ...), custom_call_target="tpu_custom_call" | custom-call | flops 201326592 | bytes 4727296 | tf_op jit(solution)/shard_map/pallas_call | solution.py:59
  27.8 1.1 %collective-permute-done.6.refs_0_.refs_3_ = f32[256,128]{1,0:T(8,128)S(1)} collective-permute-done((f32[256,128]{1,0:T(8,128)S(1)}, f32[256,128]{1,0:T(8,128)S(1)}, u32[]{:S(2)}, u32[]{:S(2)}) %collective-permute-start.6) | collective-permute-done | bytes 131104 | tf_op jit(solution)/shard_map/ppermute | solution.py:303
  29.2 1.6 %collective-permute-start.8 = (f32[8,128]{1,0:T(8,128)S(1)}, f32[8,128]{1,0:T(8,128)S(1)}, u32[]{:S(2)}, u32[]{:S(2)}) collective-permute-start(f32[8,128]{1,0:T(8,128)S(1)} %get-tuple-element.68.refs_4_), channel_id=1, source_target_pairs={{0,2},{1,3},{2,0},{3,1},{4,6},{5,7},{6,4},{7,5},{8,10},{9,11},{10,... | collective-permute-start | bytes 12296 | tf_op jit(solution)/shard_map/ppermute | solution.py:303
  31.1 1.2 %collective-permute-done.9.refs_7_ = f32[8,128]{1,0:T(8,128)S(1)} collective-permute-done((f32[8,128]{1,0:T(8,128)S(1)}, f32[8,128]{1,0:T(8,128)S(1)}, u32[]{:S(2)}, u32[]{:S(2)}) %collective-permute-start.9) | collective-permute-done | bytes 4128 | tf_op jit(solution)/shard_map/ppermute | solution.py:303
  33.4 1.7 %collective-permute-start.11 = (f32[264,128]{1,0:T(8,128)S(1)}, f32[264,128]{1,0:T(8,128)S(1)}, u32[]{:S(2)}, u32[]{:S(2)}) collective-permute-start(f32[264,128]{1,0:T(8,128)S(1)} %get-tuple-element.75), channel_id=1, source_target_pairs={{0,8},{4,12},{8,0},{12,4},{16,24},{20,28},{24,16},{28,20},{1,9},{5... | collective-permute-start | bytes 405512 | tf_op jit(solution)/shard_map/ppermute | solution.py:303
  35.5 1.4 %collective-permute-start.12 = (f32[256,128]{1,0:T(8,128)S(1)}, f32[256,128]{1,0:T(8,128)S(1)}, u32[]{:S(2)}, u32[]{:S(2)}) collective-permute-start(f32[256,128]{1,0:T(8,128)S(1)} %get-tuple-element.76), channel_id=1, source_target_pairs={{0,12},{4,8},{8,4},{12,0},{16,28},{20,24},{24,20},{28,16},{1,13},{... | collective-permute-start | bytes 393224 | tf_op jit(solution)/shard_map/ppermute | solution.py:303
  37.0 5.9 %collective-permute-done.10.refs_1_ = f32[256,128]{1,0:T(8,128)S(1)} collective-permute-done((f32[256,128]{1,0:T(8,128)S(1)}, f32[256,128]{1,0:T(8,128)S(1)}, u32[]{:S(2)}, u32[]{:S(2)}) %collective-permute-start.10) | collective-permute-done | bytes 131104 | tf_op jit(solution)/shard_map/ppermute | solution.py:303
  43.0 3.3 %collective-permute-start.13 = (f32[264,128]{1,0:T(8,128)S(1)}, f32[264,128]{1,0:T(8,128)S(1)}, u32[]{:S(2)}, u32[]{:S(2)}) collective-permute-start(f32[264,128]{1,0:T(8,128)S(1)} %shard_map.101.refs_4_), channel_id=1, source_target_pairs={{0,24},{4,28},{8,16},{12,20},{16,8},{20,12},{24,0},{28,4},{1,25},{... | collective-permute-start | bytes 405512 | tf_op jit(solution)/shard_map/ppermute | solution.py:303
  46.2 2.3 %shard_map.100 = (f32[128,1024]{1,0:T(8,128)S(1)}, f32[128,1024]{1,0:T(8,128)S(1)}, f32[128,1024]{1,0:T(8,128)S(1)}) custom-call(s32[1]{0:T(128)} %bitcast.seat, f32[128,1024]{1,0:T(8,128)S(1)} %get-tuple-element.49.q, f32[128,1024]{1,0:T(8,128)S(1)} %get-tuple-element.47.k, f32[128,1024]{1,0:T(8,128)S(1)} %get-tuple-element.48.v, ...), custom_call_target="tpu_custom_call" | custom-call | flops 503316480 | bytes 4718592 | tf_op jit(solution)/shard_map/pallas_call | solution.py:59
  48.6 1.3 %collective-permute-done.13.refs_5_ = f32[264,128]{1,0:T(8,128)S(1)} collective-permute-done((f32[264,128]{1,0:T(8,128)S(1)}, f32[264,128]{1,0:T(8,128)S(1)}, u32[]{:S(2)}, u32[]{:S(2)}) %collective-permute-start.13) | collective-permute-done | bytes 135200 | tf_op jit(solution)/shard_map/ppermute | solution.py:303
  50.9 2.7 %collective-permute-start.16 = (f32[256,128]{1,0:T(8,128)S(1)}, f32[256,128]{1,0:T(8,128)S(1)}, u32[]{:S(2)}, u32[]{:S(2)}) collective-permute-start(f32[256,128]{1,0:T(8,128)S(1)} %get-tuple-element.82), channel_id=1, source_target_pairs={{0,8},{4,12},{8,0},{12,4},{16,24},{20,28},{24,16},{28,20},{1,9},{5... | collective-permute-start | bytes 393224 | tf_op jit(solution)/shard_map/ppermute | solution.py:303
  53.6 1.5 %collective-permute-done.14.refs_1_ = f32[264,128]{1,0:T(8,128)S(1)} collective-permute-done((f32[264,128]{1,0:T(8,128)S(1)}, f32[264,128]{1,0:T(8,128)S(1)}, u32[]{:S(2)}, u32[]{:S(2)}) %collective-permute-start.14) | collective-permute-done | bytes 135200 | tf_op jit(solution)/shard_map/ppermute | solution.py:303
  55.1 1.8 %shard_map.103 = (f32[1,1]{1,0:T(1,128)}, f32[128,1024]{1,0:T(8,128)}, f32[128,1024]{1,0:T(8,128)}, f32[128,1024]{1,0:T(8,128)}) custom-call(s32[1]{0:T(128)} %bitcast.seat, f32[128,1024]{1,0:T(8,128)S(1)} %get-tuple-element.47.k, f32[128,1024]{1,0:T(8,128)S(1)} %get-tuple-element.48.v, f32[128,1024]{1,0:T(8,128)S(1)} %get-tuple-element.71.refs_6_.part_k, ...), custom_call_target="tpu_custom_call" | custom-call | flops 100663296 | bytes 4595716 | tf_op jit(solution)/shard_map/pallas_call | solution.py:59
  56.9 1.1 %collective-permute-done.16.refs_0_ = f32[256,128]{1,0:T(8,128)S(1)} collective-permute-done((f32[256,128]{1,0:T(8,128)S(1)}, f32[256,128]{1,0:T(8,128)S(1)}, u32[]{:S(2)}, u32[]{:S(2)}) %collective-permute-start.16) | collective-permute-done | bytes 131104 | tf_op jit(solution)/shard_map/ppermute | solution.py:303
  (23 shorter events, 6.9 us)
Async XLA Ops:
  2.3 6.5 %collective-permute-start = (f32[256,128]{1,0:T(8,128)S(1)}, f32[256,128]{1,0:T(8,128)S(1)}, u32[]{:S(2)}, u32[]{:S(2)}) collective-permute-start(f32[256,128]{1,0:T(8,128)S(1)} %get-tuple-element.55), channel_id=1, source_target_pairs={{0,4},{4,0},{8,12},{12,8},{16,20},{20,16},{24,28},{28,24},{1,5},{5... | collective-permute-start | bytes 393224 | tf_op jit(solution)/shard_map/ppermute | solution.py:303
  5.4 6.4 %collective-permute-start.1 = (f32[256,128]{1,0:T(8,128)S(1)}, f32[256,128]{1,0:T(8,128)S(1)}, u32[]{:S(2)}, u32[]{:S(2)}) collective-permute-start(f32[256,128]{1,0:T(8,128)S(1)} %get-tuple-element.56), channel_id=1, source_target_pairs={{0,8},{4,12},{8,0},{12,4},{16,24},{20,28},{24,16},{28,20},{1,9},{5... | collective-permute-start | bytes 393224 | tf_op jit(solution)/shard_map/ppermute | solution.py:303
  7.0 6.0 %collective-permute-start.2 = (f32[256,128]{1,0:T(8,128)S(1)}, f32[256,128]{1,0:T(8,128)S(1)}, u32[]{:S(2)}, u32[]{:S(2)}) collective-permute-start(f32[256,128]{1,0:T(8,128)S(1)} %get-tuple-element.57), channel_id=1, source_target_pairs={{0,12},{4,8},{8,4},{12,0},{16,28},{20,24},{24,20},{28,16},{1,13},{... | collective-permute-start | bytes 393224 | tf_op jit(solution)/shard_map/ppermute | solution.py:303
  13.0 6.9 %collective-permute-start.3 = (f32[256,128]{1,0:T(8,128)S(1)}, f32[256,128]{1,0:T(8,128)S(1)}, u32[]{:S(2)}, u32[]{:S(2)}) collective-permute-start(f32[256,128]{1,0:T(8,128)S(1)} %shard_map.95), channel_id=1, source_target_pairs={{0,24},{4,28},{8,16},{12,20},{16,8},{20,12},{24,0},{28,4},{1,25},{... | collective-permute-start | bytes 393224 | tf_op jit(solution)/shard_map/ppermute | solution.py:303
  20.0 7.3 %collective-permute-start.4 = (f32[256,128]{1,0:T(8,128)S(1)}, f32[256,128]{1,0:T(8,128)S(1)}, u32[]{:S(2)}, u32[]{:S(2)}) collective-permute-start(f32[256,128]{1,0:T(8,128)S(1)} %get-tuple-element.59), channel_id=1, source_target_pairs={{0,4},{4,0},{8,12},{12,8},{16,20},{20,16},{24,28},{28,24},{1,5},{5... | collective-permute-start | bytes 393224 | tf_op jit(solution)/shard_map/ppermute | solution.py:303
  21.8 5.7 %collective-permute-start.5 = (f32[256,128]{1,0:T(8,128)S(1)}, f32[256,128]{1,0:T(8,128)S(1)}, u32[]{:S(2)}, u32[]{:S(2)}) collective-permute-start(f32[256,128]{1,0:T(8,128)S(1)} %get-tuple-element.60), channel_id=1, source_target_pairs={{0,8},{4,12},{8,0},{12,4},{16,24},{20,28},{24,16},{28,20},{1,9},{5... | collective-permute-start | bytes 393224 | tf_op jit(solution)/shard_map/ppermute | solution.py:303
  23.0 5.9 %collective-permute-start.6 = (f32[256,128]{1,0:T(8,128)S(1)}, f32[256,128]{1,0:T(8,128)S(1)}, u32[]{:S(2)}, u32[]{:S(2)}) collective-permute-start(f32[256,128]{1,0:T(8,128)S(1)} %get-tuple-element.64), channel_id=1, source_target_pairs={{0,12},{4,8},{8,4},{12,0},{16,28},{20,24},{24,20},{28,16},{1,13},{... | collective-permute-start | bytes 393224 | tf_op jit(solution)/shard_map/ppermute | solution.py:303
  29.2 3.1 %collective-permute-start.9 = (f32[8,128]{1,0:T(8,128)S(1)}, f32[8,128]{1,0:T(8,128)S(1)}, u32[]{:S(2)}, u32[]{:S(2)}) collective-permute-start(f32[8,128]{1,0:T(8,128)S(1)} %get-tuple-element.68.refs_4_), channel_id=1, source_target_pairs={{0,3},{1,2},{2,1},{3,0},{4,7},{5,6},{6,5},{7,4},{8,11},{9,10},{10,... | collective-permute-start | bytes 12296 | tf_op jit(solution)/shard_map/ppermute | solution.py:303
  29.2 3.7 %collective-permute-start.8 = (f32[8,128]{1,0:T(8,128)S(1)}, f32[8,128]{1,0:T(8,128)S(1)}, u32[]{:S(2)}, u32[]{:S(2)}) collective-permute-start(f32[8,128]{1,0:T(8,128)S(1)} %get-tuple-element.68.refs_4_), channel_id=1, source_target_pairs={{0,2},{1,3},{2,0},{3,1},{4,6},{5,7},{6,4},{7,5},{8,10},{9,11},{10,... | collective-permute-start | bytes 12296 | tf_op jit(solution)/shard_map/ppermute | solution.py:303
  30.8 2.1 %collective-permute-start.7 = (f32[8,128]{1,0:T(8,128)S(1)}, f32[8,128]{1,0:T(8,128)S(1)}, u32[]{:S(2)}, u32[]{:S(2)}) collective-permute-start(f32[8,128]{1,0:T(8,128)S(1)} %get-tuple-element.68.refs_4_), channel_id=1, source_target_pairs={{0,1},{1,0},{2,3},{3,2},{4,5},{5,4},{6,7},{7,6},{8,9},{9,8},{10,11... | collective-permute-start | bytes 12296 | tf_op jit(solution)/shard_map/ppermute | solution.py:303
  33.4 9.5 %collective-permute-start.11 = (f32[264,128]{1,0:T(8,128)S(1)}, f32[264,128]{1,0:T(8,128)S(1)}, u32[]{:S(2)}, u32[]{:S(2)}) collective-permute-start(f32[264,128]{1,0:T(8,128)S(1)} %get-tuple-element.75), channel_id=1, source_target_pairs={{0,8},{4,12},{8,0},{12,4},{16,24},{20,28},{24,16},{28,20},{1,9},{5... | collective-permute-start | bytes 405512 | tf_op jit(solution)/shard_map/ppermute | solution.py:303
  35.1 7.8 %collective-permute-start.10 = (f32[256,128]{1,0:T(8,128)S(1)}, f32[256,128]{1,0:T(8,128)S(1)}, u32[]{:S(2)}, u32[]{:S(2)}) collective-permute-start(f32[256,128]{1,0:T(8,128)S(1)} %get-tuple-element.74), channel_id=1, source_target_pairs={{0,4},{4,0},{8,12},{12,8},{16,20},{20,16},{24,28},{28,24},{1,5},{5... | collective-permute-start | bytes 393224 | tf_op jit(solution)/shard_map/ppermute | solution.py:303
  35.5 7.4 %collective-permute-start.12 = (f32[256,128]{1,0:T(8,128)S(1)}, f32[256,128]{1,0:T(8,128)S(1)}, u32[]{:S(2)}, u32[]{:S(2)}) collective-permute-start(f32[256,128]{1,0:T(8,128)S(1)} %get-tuple-element.76), channel_id=1, source_target_pairs={{0,12},{4,8},{8,4},{12,0},{16,28},{20,24},{24,20},{28,16},{1,13},{... | collective-permute-start | bytes 393224 | tf_op jit(solution)/shard_map/ppermute | solution.py:303
  43.0 6.9 %collective-permute-start.13 = (f32[264,128]{1,0:T(8,128)S(1)}, f32[264,128]{1,0:T(8,128)S(1)}, u32[]{:S(2)}, u32[]{:S(2)}) collective-permute-start(f32[264,128]{1,0:T(8,128)S(1)} %shard_map.101.refs_4_), channel_id=1, source_target_pairs={{0,24},{4,28},{8,16},{12,20},{16,8},{20,12},{24,0},{28,4},{1,25},{... | collective-permute-start | bytes 405512 | tf_op jit(solution)/shard_map/ppermute | solution.py:303
  50.0 5.1 %collective-permute-start.14 = (f32[264,128]{1,0:T(8,128)S(1)}, f32[264,128]{1,0:T(8,128)S(1)}, u32[]{:S(2)}, u32[]{:S(2)}) collective-permute-start(f32[264,128]{1,0:T(8,128)S(1)} %get-tuple-element.77.sent), channel_id=1, source_target_pairs={{0,4},{4,0},{8,12},{12,8},{16,20},{20,16},{24,28},{28,24},{1,5},{5... | collective-permute-start | bytes 405512 | tf_op jit(solution)/shard_map/ppermute | solution.py:303
  50.9 7.1 %collective-permute-start.16 = (f32[256,128]{1,0:T(8,128)S(1)}, f32[256,128]{1,0:T(8,128)S(1)}, u32[]{:S(2)}, u32[]{:S(2)}) collective-permute-start(f32[256,128]{1,0:T(8,128)S(1)} %get-tuple-element.82), channel_id=1, source_target_pairs={{0,8},{4,12},{8,0},{12,4},{16,24},{20,28},{24,16},{28,20},{1,9},{5... | collective-permute-start | bytes 393224 | tf_op jit(solution)/shard_map/ppermute | solution.py:303
  53.6 5.9 %collective-permute-start.15 = (f32[256,128]{1,0:T(8,128)S(1)}, f32[256,128]{1,0:T(8,128)S(1)}, u32[]{:S(2)}, u32[]{:S(2)}) collective-permute-start(f32[256,128]{1,0:T(8,128)S(1)} %get-tuple-element.81), channel_id=1, source_target_pairs={{0,12},{4,8},{8,4},{12,0},{16,28},{20,24},{24,20},{28,16},{1,13},{... | collective-permute-start | bytes 393224 | tf_op jit(solution)/shard_map/ppermute | solution.py:303

commit v6 on v5

--- a/solution.py
+++ b/solution.py
@@ -223,8 +223,10 @@
 def grad_kernel(plan, seat, flipped, aim, count, *refs):
     refs = list(refs)
     take = lambda n: [refs.pop(0) for _ in range(n)]
-    attended, stat_parts, (grad,), out = take(plan.group), take(plan.head), take(1), take(plan.group)
+    attended, stat_parts, (factors,), out = take(plan.group), take(plan.head), take(1), take(plan.group)
     left, right, losses = scales(plan, pair_sum(r[...] for r in stat_parts))
+    factors[0:1, :] = left
+    factors[1:2, :] = right
     left, right = column(left, plan.length), column(right, plan.length)
     row = lax.broadcasted_iota(jnp.int32, (TAIL, HEAD_DIM), 0)
     tail = jnp.where(row == 0, jnp.sum(losses), count[...])
@@ -233,20 +235,21 @@
             h = plan.head_of(seat[0], x, i)
             cols = head_cols(h)
             g = left * aim[:, cols] - right * attended[x][:, rows_of(i)]
-            grad[:, cols] = g
             out[x][rows_of(i), :] = dot(split(flipped[h]), split(g), NN)
         if x in (0, plan.last):
             out[x][plan.tail, :] = tail
 
 
-def local_grad_kernel(plan, seat, q, k, v, grad, scores, *refs):
-    priors, (grad_q, grad_k, grad_v) = refs[: plan.group], refs[plan.group :]
+def local_grad_kernel(plan, seat, q, k, v, aim, factors, scores, *refs):
+    group = plan.group
+    attended, priors, (grad_q, grad_k, grad_v) = refs[:group], refs[group : 2 * group], refs[2 * group :]
+    left, right = column(factors[0:1, :], plan.length), column(factors[1:2, :], plan.length)
     causal = causal_mask(plan.length)
     for x in range(plan.group):
         for i in range(plan.own):
             h = plan.head_of(seat[0], x, i)
             cols = head_cols(h)
-            g = split(grad[:, cols])
+            g = split(left * aim[:, cols] - right * attended[x][:, rows_of(i)])
             gs = split(jnp.where(causal, dot(g, split(v[:, cols]), NT), 0.0))
             prior = split(priors[x][rows_of(i), :])
             grad_q[:, cols] = dot(gs, split(k[:, cols]), NN) + dot(g, prior, NT)
@@ -387,9 +390,9 @@
     )
     attended.append(last)
     stats = swap_all([stats] * head_count, "head")
-    grad, *states = call(
+    factors, *states = call(
         bind(grad_kernel),
-        [wide] + [sum_shape if x in (0, plan.last) else state for x in range(group)],
+        [shape(TAIL, length)] + [sum_shape if x in (0, plan.last) else state for x in range(group)],
         product,
         seat,
         flipped,
@@ -399,7 +402,7 @@
         *stats,
     )
     part_query, part_key, part_value = call(
-        bind(local_grad_kernel), [wide] * 3, 5 * product, seat, queries, key_rows, value_rows, grad, scores, *priors
+        bind(local_grad_kernel), [wide] * 3, 5 * product, seat, queries, key_rows, value_rows, aim, factors, scores, *attended, *priors
     )
     states = swap_all(states, "seq")
     (grad_total,) = call(bind(total_kernel), [sum_shape], 0, seat, *states)

time: 60.7 us -> 60.6 us (level)
  no operation moved by 1% of the time
where the time goes in v6:
time: 60.6 us; the launch traced here: 60.5 us
  starting transfers between devices  24.4 us (40%)
  waiting for transfers between devices  22.4 us (37%)
  Pallas kernels  12.9 us (21%)
  between operations  0.73 us (1%)
    ppermute x17, starting transfers between devices, swap(): lax.ppermute(value, axis, [(i, i ^ step) for i in range(lax.axis_size(axi...  24.4 us
    ppermute x17, waiting for transfers between devices, swap(): lax.ppermute(value, axis, [(i, i ^ step) for i in range(lax.axis_size(axi...  22.4 us
    pallas_call x13, Pallas kernels, call(): pl.pallas_call(kernel, out_shape=outs, in_specs=[SMEM] * len(place) + spe...  12.9 us
  transfers between devices with their start and end apart: 17, of which 13 were waited for; matrix products, arithmetic and copies ran while one was open for 0% of the time, Pallas kernels for 15%

profile of v6, /device:TPU:0, one launch (start us, length us, event | category | flops | bytes accessed | tf_op | source)
XLA Modules:
  0.0 60.5 jit_solution(2582114966210180995)
XLA Ops:
  0.6 1.7 %shard_map.93 = (f32[256,128]{1,0:T(8,128)S(1)}, f32[256,128]{1,0:T(8,128)S(1)}, f32[256,128]{1,0:T(8,128)S(1)}, f32[256,128]{1,0:T(8,128)S(1)}, f32[128,1024]{1,0:T(8,128)S(1)}, /*index=5*/f32[128,1024]{1,0:T(8,128)S(1)}) custom-call(f32[128,1024]{1,0:T(8,128)} %k_hbm.1, f32[128,1024]{1,0:T(8,128)} %v_hbm.1), custom_call_target="tpu_custom_call" | custom-call | flops 100663296 | bytes 2621440 | tf_op jit(solution)/shard_map/pallas_call | solution.py:59
  2.3 3.0 %collective-permute-start = (f32[256,128]{1,0:T(8,128)S(1)}, f32[256,128]{1,0:T(8,128)S(1)}, u32[]{:S(2)}, u32[]{:S(2)}) collective-permute-start(f32[256,128]{1,0:T(8,128)S(1)} %get-tuple-element.55), channel_id=1, source_target_pairs={{0,4},{4,0},{8,12},{12,8},{16,20},{20,16},{24,28},{28,24},{1,5},{5... | collective-permute-start | bytes 393224 | tf_op jit(solution)/shard_map/ppermute | solution.py:306
  5.4 1.6 %collective-permute-start.1 = (f32[256,128]{1,0:T(8,128)S(1)}, f32[256,128]{1,0:T(8,128)S(1)}, u32[]{:S(2)}, u32[]{:S(2)}) collective-permute-start(f32[256,128]{1,0:T(8,128)S(1)} %get-tuple-element.56), channel_id=1, source_target_pairs={{0,8},{4,12},{8,0},{12,4},{16,24},{20,28},{24,16},{28,20},{1,9},{5... | collective-permute-start | bytes 393224 | tf_op jit(solution)/shard_map/ppermute | solution.py:306
  7.0 1.9 %collective-permute-done.refs_1_ = f32[256,128]{1,0:T(8,128)S(1)} collective-permute-done((f32[256,128]{1,0:T(8,128)S(1)}, f32[256,128]{1,0:T(8,128)S(1)}, u32[]{:S(2)}, u32[]{:S(2)}) %collective-permute-start) | collective-permute-done | bytes 131104 | tf_op jit(solution)/shard_map/ppermute | solution.py:306
  8.9 2.9 %collective-permute-done.1.refs_2_ = f32[256,128]{1,0:T(8,128)S(1)} collective-permute-done((f32[256,128]{1,0:T(8,128)S(1)}, f32[256,128]{1,0:T(8,128)S(1)}, u32[]{:S(2)}, u32[]{:S(2)}) %collective-permute-start.1) | collective-permute-done | bytes 131104 | tf_op jit(solution)/shard_map/ppermute | solution.py:306
  11.7 1.2 %collective-permute-done.2.refs_3_ = f32[256,128]{1,0:T(8,128)S(1)} collective-permute-done((f32[256,128]{1,0:T(8,128)S(1)}, f32[256,128]{1,0:T(8,128)S(1)}, u32[]{:S(2)}, u32[]{:S(2)}) %collective-permute-start.2) | collective-permute-done | bytes 131104 | tf_op jit(solution)/shard_map/ppermute | solution.py:306
  13.0 3.8 %collective-permute-start.3 = (f32[256,128]{1,0:T(8,128)S(1)}, f32[256,128]{1,0:T(8,128)S(1)}, u32[]{:S(2)}, u32[]{:S(2)}) collective-permute-start(f32[256,128]{1,0:T(8,128)S(1)} %shard_map.95), channel_id=1, source_target_pairs={{0,24},{4,28},{8,16},{12,20},{16,8},{20,12},{24,0},{28,4},{1,25},{... | collective-permute-start | bytes 393224 | tf_op jit(solution)/shard_map/ppermute | solution.py:306
  16.8 3.1 %collective-permute-done.3.refs_4_ = f32[256,128]{1,0:T(8,128)S(1)} collective-permute-done((f32[256,128]{1,0:T(8,128)S(1)}, f32[256,128]{1,0:T(8,128)S(1)}, u32[]{:S(2)}, u32[]{:S(2)}) %collective-permute-start.3) | collective-permute-done | bytes 131104 | tf_op jit(solution)/shard_map/ppermute | solution.py:306
  20.0 1.7 %collective-permute-start.4 = (f32[256,128]{1,0:T(8,128)S(1)}, f32[256,128]{1,0:T(8,128)S(1)}, u32[]{:S(2)}, u32[]{:S(2)}) collective-permute-start(f32[256,128]{1,0:T(8,128)S(1)} %get-tuple-element.59), channel_id=1, source_target_pairs={{0,4},{4,0},{8,12},{12,8},{16,20},{20,16},{24,28},{28,24},{1,5},{5... | collective-permute-start | bytes 393224 | tf_op jit(solution)/shard_map/ppermute | solution.py:306
  21.8 1.3 %collective-permute-start.5 = (f32[256,128]{1,0:T(8,128)S(1)}, f32[256,128]{1,0:T(8,128)S(1)}, u32[]{:S(2)}, u32[]{:S(2)}) collective-permute-start(f32[256,128]{1,0:T(8,128)S(1)} %get-tuple-element.60), channel_id=1, source_target_pairs={{0,8},{4,12},{8,0},{12,4},{16,24},{20,28},{24,16},{28,20},{1,9},{5... | collective-permute-start | bytes 393224 | tf_op jit(solution)/shard_map/ppermute | solution.py:306
  23.6 3.7 %shard_map.94 = (f32[128,1024]{1,0:T(8,128)S(1)}, f32[8,128,128]{2,1,0:T(8,128)S(1)}, f32[8,128,128]{2,1,0:T(8,128)S(1)}, f32[128,1024]{1,0:T(8,128)S(1)}, f32[1...) custom-call(s32[1]{0:T(128)} %bitcast.seat, f32[128,1024]{1,0:T(8,128)} %q_hbm.1, f32[128,1024]{1,0:T(8,128)S(1)} %get-tuple-element.47.k, ...), custom_call_target="tpu_custom_call" | custom-call | flops 201326592 | bytes 4727296 | tf_op jit(solution)/shard_map/pallas_call | solution.py:59
  27.8 1.1 %collective-permute-done.6.refs_0_.refs_7_ = f32[256,128]{1,0:T(8,128)S(1)} collective-permute-done((f32[256,128]{1,0:T(8,128)S(1)}, f32[256,128]{1,0:T(8,128)S(1)}, u32[]{:S(2)}, u32[]{:S(2)}) %collective-permute-start.6) | collective-permute-done | bytes 131104 | tf_op jit(solution)/shard_map/ppermute | solution.py:306
  29.2 1.6 %collective-permute-start.8 = (f32[8,128]{1,0:T(8,128)S(1)}, f32[8,128]{1,0:T(8,128)S(1)}, u32[]{:S(2)}, u32[]{:S(2)}) collective-permute-start(f32[8,128]{1,0:T(8,128)S(1)} %get-tuple-element.68.refs_4_), channel_id=1, source_target_pairs={{0,2},{1,3},{2,0},{3,1},{4,6},{5,7},{6,4},{7,5},{8,10},{9,11},{10,... | collective-permute-start | bytes 12296 | tf_op jit(solution)/shard_map/ppermute | solution.py:306
  31.1 1.2 %collective-permute-done.9.refs_7_ = f32[8,128]{1,0:T(8,128)S(1)} collective-permute-done((f32[8,128]{1,0:T(8,128)S(1)}, f32[8,128]{1,0:T(8,128)S(1)}, u32[]{:S(2)}, u32[]{:S(2)}) %collective-permute-start.9) | collective-permute-done | bytes 4128 | tf_op jit(solution)/shard_map/ppermute | solution.py:306
  33.4 1.7 %collective-permute-start.11 = (f32[264,128]{1,0:T(8,128)S(1)}, f32[264,128]{1,0:T(8,128)S(1)}, u32[]{:S(2)}, u32[]{:S(2)}) collective-permute-start(f32[264,128]{1,0:T(8,128)S(1)} %get-tuple-element.75), channel_id=1, source_target_pairs={{0,8},{4,12},{8,0},{12,4},{16,24},{20,28},{24,16},{28,20},{1,9},{5... | collective-permute-start | bytes 405512 | tf_op jit(solution)/shard_map/ppermute | solution.py:306
  35.5 1.4 %collective-permute-start.12 = (f32[256,128]{1,0:T(8,128)S(1)}, f32[256,128]{1,0:T(8,128)S(1)}, u32[]{:S(2)}, u32[]{:S(2)}) collective-permute-start(f32[256,128]{1,0:T(8,128)S(1)} %get-tuple-element.76), channel_id=1, source_target_pairs={{0,12},{4,8},{8,4},{12,0},{16,28},{20,24},{24,20},{28,16},{1,13},{... | collective-permute-start | bytes 393224 | tf_op jit(solution)/shard_map/ppermute | solution.py:306
  36.9 5.9 %collective-permute-done.10.refs_1_ = f32[256,128]{1,0:T(8,128)S(1)} collective-permute-done((f32[256,128]{1,0:T(8,128)S(1)}, f32[256,128]{1,0:T(8,128)S(1)}, u32[]{:S(2)}, u32[]{:S(2)}) %collective-permute-start.10) | collective-permute-done | bytes 131104 | tf_op jit(solution)/shard_map/ppermute | solution.py:306
  42.9 3.3 %collective-permute-start.13 = (f32[264,128]{1,0:T(8,128)S(1)}, f32[264,128]{1,0:T(8,128)S(1)}, u32[]{:S(2)}, u32[]{:S(2)}) collective-permute-start(f32[264,128]{1,0:T(8,128)S(1)} %shard_map.101.refs_4_), channel_id=1, source_target_pairs={{0,24},{4,28},{8,16},{12,20},{16,8},{20,12},{24,0},{28,4},{1,25},{... | collective-permute-start | bytes 405512 | tf_op jit(solution)/shard_map/ppermute | solution.py:306
  46.2 2.4 %shard_map.100 = (f32[128,1024]{1,0:T(8,128)S(1)}, f32[128,1024]{1,0:T(8,128)S(1)}, f32[128,1024]{1,0:T(8,128)S(1)}) custom-call(s32[1]{0:T(128)} %bitcast.seat, f32[128,1024]{1,0:T(8,128)S(1)} %get-tuple-element.49.q, f32[128,1024]{1,0:T(8,128)S(1)} %get-tuple-element.47.k, f32[128,1024]{1,0:T(8,128)S(1)} %get-tuple-element.48.v, ...), custom_call_target="tpu_custom_call" | custom-call | flops 503316480 | bytes 5246976 | tf_op jit(solution)/shard_map/pallas_call | solution.py:59
  48.6 1.2 %collective-permute-done.13.refs_5_ = f32[264,128]{1,0:T(8,128)S(1)} collective-permute-done((f32[264,128]{1,0:T(8,128)S(1)}, f32[264,128]{1,0:T(8,128)S(1)}, u32[]{:S(2)}, u32[]{:S(2)}) %collective-permute-start.13) | collective-permute-done | bytes 135200 | tf_op jit(solution)/shard_map/ppermute | solution.py:306
  50.9 2.7 %collective-permute-start.16 = (f32[256,128]{1,0:T(8,128)S(1)}, f32[256,128]{1,0:T(8,128)S(1)}, u32[]{:S(2)}, u32[]{:S(2)}) collective-permute-start(f32[256,128]{1,0:T(8,128)S(1)} %get-tuple-element.82), channel_id=1, source_target_pairs={{0,8},{4,12},{8,0},{12,4},{16,24},{20,28},{24,16},{28,20},{1,9},{5... | collective-permute-start | bytes 393224 | tf_op jit(solution)/shard_map/ppermute | solution.py:306
  53.6 1.5 %collective-permute-done.14.refs_1_ = f32[264,128]{1,0:T(8,128)S(1)} collective-permute-done((f32[264,128]{1,0:T(8,128)S(1)}, f32[264,128]{1,0:T(8,128)S(1)}, u32[]{:S(2)}, u32[]{:S(2)}) %collective-permute-start.14) | collective-permute-done | bytes 135200 | tf_op jit(solution)/shard_map/ppermute | solution.py:306
  55.1 1.8 %shard_map.103 = (f32[1,1]{1,0:T(1,128)}, f32[128,1024]{1,0:T(8,128)}, f32[128,1024]{1,0:T(8,128)}, f32[128,1024]{1,0:T(8,128)}) custom-call(s32[1]{0:T(128)} %bitcast.seat, f32[128,1024]{1,0:T(8,128)S(1)} %get-tuple-element.47.k, f32[128,1024]{1,0:T(8,128)S(1)} %get-tuple-element.48.v, f32[128,1024]{1,0:T(8,128)S(1)} %get-tuple-element.71.refs_6_.part_k, ...), custom_call_target="tpu_custom_call" | custom-call | flops 100663296 | bytes 4595716 | tf_op jit(solution)/shard_map/pallas_call | solution.py:59
  56.9 1.1 %collective-permute-done.16.refs_0_ = f32[256,128]{1,0:T(8,128)S(1)} collective-permute-done((f32[256,128]{1,0:T(8,128)S(1)}, f32[256,128]{1,0:T(8,128)S(1)}, u32[]{:S(2)}, u32[]{:S(2)}) %collective-permute-start.16) | collective-permute-done | bytes 131104 | tf_op jit(solution)/shard_map/ppermute | solution.py:306
  (23 shorter events, 6.8 us)
Async XLA Ops:
  2.3 6.5 %collective-permute-start = (f32[256,128]{1,0:T(8,128)S(1)}, f32[256,128]{1,0:T(8,128)S(1)}, u32[]{:S(2)}, u32[]{:S(2)}) collective-permute-start(f32[256,128]{1,0:T(8,128)S(1)} %get-tuple-element.55), channel_id=1, source_target_pairs={{0,4},{4,0},{8,12},{12,8},{16,20},{20,16},{24,28},{28,24},{1,5},{5... | collective-permute-start | bytes 393224 | tf_op jit(solution)/shard_map/ppermute | solution.py:306
  5.4 6.4 %collective-permute-start.1 = (f32[256,128]{1,0:T(8,128)S(1)}, f32[256,128]{1,0:T(8,128)S(1)}, u32[]{:S(2)}, u32[]{:S(2)}) collective-permute-start(f32[256,128]{1,0:T(8,128)S(1)} %get-tuple-element.56), channel_id=1, source_target_pairs={{0,8},{4,12},{8,0},{12,4},{16,24},{20,28},{24,16},{28,20},{1,9},{5... | collective-permute-start | bytes 393224 | tf_op jit(solution)/shard_map/ppermute | solution.py:306
  7.0 6.0 %collective-permute-start.2 = (f32[256,128]{1,0:T(8,128)S(1)}, f32[256,128]{1,0:T(8,128)S(1)}, u32[]{:S(2)}, u32[]{:S(2)}) collective-permute-start(f32[256,128]{1,0:T(8,128)S(1)} %get-tuple-element.57), channel_id=1, source_target_pairs={{0,12},{4,8},{8,4},{12,0},{16,28},{20,24},{24,20},{28,16},{1,13},{... | collective-permute-start | bytes 393224 | tf_op jit(solution)/shard_map/ppermute | solution.py:306
  13.0 6.9 %collective-permute-start.3 = (f32[256,128]{1,0:T(8,128)S(1)}, f32[256,128]{1,0:T(8,128)S(1)}, u32[]{:S(2)}, u32[]{:S(2)}) collective-permute-start(f32[256,128]{1,0:T(8,128)S(1)} %shard_map.95), channel_id=1, source_target_pairs={{0,24},{4,28},{8,16},{12,20},{16,8},{20,12},{24,0},{28,4},{1,25},{... | collective-permute-start | bytes 393224 | tf_op jit(solution)/shard_map/ppermute | solution.py:306
  20.0 7.3 %collective-permute-start.4 = (f32[256,128]{1,0:T(8,128)S(1)}, f32[256,128]{1,0:T(8,128)S(1)}, u32[]{:S(2)}, u32[]{:S(2)}) collective-permute-start(f32[256,128]{1,0:T(8,128)S(1)} %get-tuple-element.59), channel_id=1, source_target_pairs={{0,4},{4,0},{8,12},{12,8},{16,20},{20,16},{24,28},{28,24},{1,5},{5... | collective-permute-start | bytes 393224 | tf_op jit(solution)/shard_map/ppermute | solution.py:306
  21.8 5.7 %collective-permute-start.5 = (f32[256,128]{1,0:T(8,128)S(1)}, f32[256,128]{1,0:T(8,128)S(1)}, u32[]{:S(2)}, u32[]{:S(2)}) collective-permute-start(f32[256,128]{1,0:T(8,128)S(1)} %get-tuple-element.60), channel_id=1, source_target_pairs={{0,8},{4,12},{8,0},{12,4},{16,24},{20,28},{24,16},{28,20},{1,9},{5... | collective-permute-start | bytes 393224 | tf_op jit(solution)/shard_map/ppermute | solution.py:306
  23.0 5.9 %collective-permute-start.6 = (f32[256,128]{1,0:T(8,128)S(1)}, f32[256,128]{1,0:T(8,128)S(1)}, u32[]{:S(2)}, u32[]{:S(2)}) collective-permute-start(f32[256,128]{1,0:T(8,128)S(1)} %get-tuple-element.64), channel_id=1, source_target_pairs={{0,12},{4,8},{8,4},{12,0},{16,28},{20,24},{24,20},{28,16},{1,13},{... | collective-permute-start | bytes 393224 | tf_op jit(solution)/shard_map/ppermute | solution.py:306
  29.2 3.1 %collective-permute-start.9 = (f32[8,128]{1,0:T(8,128)S(1)}, f32[8,128]{1,0:T(8,128)S(1)}, u32[]{:S(2)}, u32[]{:S(2)}) collective-permute-start(f32[8,128]{1,0:T(8,128)S(1)} %get-tuple-element.68.refs_4_), channel_id=1, source_target_pairs={{0,3},{1,2},{2,1},{3,0},{4,7},{5,6},{6,5},{7,4},{8,11},{9,10},{10,... | collective-permute-start | bytes 12296 | tf_op jit(solution)/shard_map/ppermute | solution.py:306
  29.2 3.7 %collective-permute-start.8 = (f32[8,128]{1,0:T(8,128)S(1)}, f32[8,128]{1,0:T(8,128)S(1)}, u32[]{:S(2)}, u32[]{:S(2)}) collective-permute-start(f32[8,128]{1,0:T(8,128)S(1)} %get-tuple-element.68.refs_4_), channel_id=1, source_target_pairs={{0,2},{1,3},{2,0},{3,1},{4,6},{5,7},{6,4},{7,5},{8,10},{9,11},{10,... | collective-permute-start | bytes 12296 | tf_op jit(solution)/shard_map/ppermute | solution.py:306
  30.8 2.1 %collective-permute-start.7 = (f32[8,128]{1,0:T(8,128)S(1)}, f32[8,128]{1,0:T(8,128)S(1)}, u32[]{:S(2)}, u32[]{:S(2)}) collective-permute-start(f32[8,128]{1,0:T(8,128)S(1)} %get-tuple-element.68.refs_4_), channel_id=1, source_target_pairs={{0,1},{1,0},{2,3},{3,2},{4,5},{5,4},{6,7},{7,6},{8,9},{9,8},{10,11... | collective-permute-start | bytes 12296 | tf_op jit(solution)/shard_map/ppermute | solution.py:306
  33.4 9.5 %collective-permute-start.11 = (f32[264,128]{1,0:T(8,128)S(1)}, f32[264,128]{1,0:T(8,128)S(1)}, u32[]{:S(2)}, u32[]{:S(2)}) collective-permute-start(f32[264,128]{1,0:T(8,128)S(1)} %get-tuple-element.75), channel_id=1, source_target_pairs={{0,8},{4,12},{8,0},{12,4},{16,24},{20,28},{24,16},{28,20},{1,9},{5... | collective-permute-start | bytes 405512 | tf_op jit(solution)/shard_map/ppermute | solution.py:306
  35.1 7.8 %collective-permute-start.10 = (f32[256,128]{1,0:T(8,128)S(1)}, f32[256,128]{1,0:T(8,128)S(1)}, u32[]{:S(2)}, u32[]{:S(2)}) collective-permute-start(f32[256,128]{1,0:T(8,128)S(1)} %get-tuple-element.74), channel_id=1, source_target_pairs={{0,4},{4,0},{8,12},{12,8},{16,20},{20,16},{24,28},{28,24},{1,5},{5... | collective-permute-start | bytes 393224 | tf_op jit(solution)/shard_map/ppermute | solution.py:306
  35.5 7.4 %collective-permute-start.12 = (f32[256,128]{1,0:T(8,128)S(1)}, f32[256,128]{1,0:T(8,128)S(1)}, u32[]{:S(2)}, u32[]{:S(2)}) collective-permute-start(f32[256,128]{1,0:T(8,128)S(1)} %get-tuple-element.76), channel_id=1, source_target_pairs={{0,12},{4,8},{8,4},{12,0},{16,28},{20,24},{24,20},{28,16},{1,13},{... | collective-permute-start | bytes 393224 | tf_op jit(solution)/shard_map/ppermute | solution.py:306
  42.9 6.9 %collective-permute-start.13 = (f32[264,128]{1,0:T(8,128)S(1)}, f32[264,128]{1,0:T(8,128)S(1)}, u32[]{:S(2)}, u32[]{:S(2)}) collective-permute-start(f32[264,128]{1,0:T(8,128)S(1)} %shard_map.101.refs_4_), channel_id=1, source_target_pairs={{0,24},{4,28},{8,16},{12,20},{16,8},{20,12},{24,0},{28,4},{1,25},{... | collective-permute-start | bytes 405512 | tf_op jit(solution)/shard_map/ppermute | solution.py:306
  50.0 5.1 %collective-permute-start.14 = (f32[264,128]{1,0:T(8,128)S(1)}, f32[264,128]{1,0:T(8,128)S(1)}, u32[]{:S(2)}, u32[]{:S(2)}) collective-permute-start(f32[264,128]{1,0:T(8,128)S(1)} %get-tuple-element.77.sent), channel_id=1, source_target_pairs={{0,4},{4,0},{8,12},{12,8},{16,20},{20,16},{24,28},{28,24},{1,5},{5... | collective-permute-start | bytes 405512 | tf_op jit(solution)/shard_map/ppermute | solution.py:306
  50.9 7.1 %collective-permute-start.16 = (f32[256,128]{1,0:T(8,128)S(1)}, f32[256,128]{1,0:T(8,128)S(1)}, u32[]{:S(2)}, u32[]{:S(2)}) collective-permute-start(f32[256,128]{1,0:T(8,128)S(1)} %get-tuple-element.82), channel_id=1, source_target_pairs={{0,8},{4,12},{8,0},{12,4},{16,24},{20,28},{24,16},{28,20},{1,9},{5... | collective-permute-start | bytes 393224 | tf_op jit(solution)/shard_map/ppermute | solution.py:306
  53.6 5.9 %collective-permute-start.15 = (f32[256,128]{1,0:T(8,128)S(1)}, f32[256,128]{1,0:T(8,128)S(1)}, u32[]{:S(2)}, u32[]{:S(2)}) collective-permute-start(f32[256,128]{1,0:T(8,128)S(1)} %get-tuple-element.81), channel_id=1, source_target_pairs={{0,12},{4,8},{8,4},{12,0},{16,28},{20,24},{24,20},{28,16},{1,13},{... | collective-permute-start | bytes 393224 | tf_op jit(solution)/shard_map/ppermute | solution.py:306

commit v7 on v6

--- a/solution.py
+++ b/solution.py
@@ -180,7 +180,7 @@
 
 def prior_kernel(plan, seat, *refs):
     group = plan.group
-    parts, totals, outs = refs[:group], refs[group : -group], refs[-group:]
+    parts, totals, outs = refs[:group], refs[group : -group - 1], refs[-group:]
     outer = outer_sum(plan, seat[0], False, totals)
     for x in range(group):
         outs[x][...] = state_at(plan, seat[0], False, x, outer, parts)
@@ -290,9 +290,11 @@
             state = split(later[j][rows_of(i), :])
             block_k[j, :, rows_of(i)] = factor * (part_k[:, cols] + dot(split(v[:, cols]), state, NT))
             block_v[j, :, rows_of(i)] = factor * (part_v[:, cols] + dot(split(k[:, cols]), state, NN))
-        for m, (block, out) in enumerate(((block_k, grad_k), (block_v, grad_v))):
-            copies.append(pltpu.make_async_copy(block.at[j], out.at[:, plan.share(seat[0], x)], sems.at[m, j]))
-            copies[-1].start()
+            for m, (block, out) in enumerate(((block_k, grad_k), (block_v, grad_v))):
+                copies.append(
+                    pltpu.make_async_copy(block.at[j, :, rows_of(i)], out.at[:, cols], sems.at[m, j * plan.own + i])
+                )
+                copies[-1].start()
     if first:
         block_q[...] = factor * part_q[...]
         copies.append(pltpu.make_async_copy(block_q, grad_q, sems.at[2, 0]))
@@ -362,7 +364,16 @@
     kv = swap_all(kv, "seq")
     (total,) = call(bind(total_kernel), [state], 0, seat, *kv)
     totals = swap_totals(plan, total)
-    priors = call(bind(prior_kernel), [state] * group, 0, seat, *kv, *totals[1:])
+    priors = call(
+        bind(prior_kernel),
+        [state] * group,
+        0,
+        seat,
+        *kv,
+        *totals[1:],
+        scores,
+        specs=[VMEM] * (group + len(totals) - 1) + [ANY],
+    )
     priors = swap_all(priors, "seq")
     early, late = list(range(group - 1)), [group - 1]
     column_sum = shape(length, HEAD_DIM)
@@ -432,7 +443,7 @@
                 *inputs,
                 part_query,
                 out_specs=[VMEM] + [ANY] * 3,
-                scratch=[block, block, pltpu.VMEM((length, columns), f32), pltpu.SemaphoreType.DMA((3, len(which)))],
+                scratch=[block, block, pltpu.VMEM((length, columns), f32), pltpu.SemaphoreType.DMA((3, own * len(which)))],
             )
             continue
         inputs.append(later[1])
@@ -445,7 +456,7 @@
             *grads,
             specs=[VMEM] * len(inputs) + [ANY] * 2,
             out_specs=[ANY] * 2,
-            scratch=[block, block, pltpu.SemaphoreType.DMA((2, len(which)))],
+            scratch=[block, block, pltpu.SemaphoreType.DMA((2, own * len(which)))],
             aliases={1 + len(inputs) + i: i for i in range(2)},
         )
     grad_key, grad_value = grads

time: 60.6 us -> 60.8 us (level)
  no operation moved by 1% of the time
where the time goes in v7:
time: 60.8 us; the launch traced here: 60.6 us
  starting transfers between devices  24 us (39%)
  waiting for transfers between devices  22.9 us (38%)
  Pallas kernels  12.9 us (21%)
  between operations  0.74 us (1%)
    ppermute x17, starting transfers between devices, swap(): lax.ppermute(value, axis, [(i, i ^ step) for i in range(lax.axis_size(axi...  24 us
    ppermute x17, waiting for transfers between devices, swap(): lax.ppermute(value, axis, [(i, i ^ step) for i in range(lax.axis_size(axi...  22.9 us
    pallas_call x13, Pallas kernels, call(): pl.pallas_call(kernel, out_shape=outs, in_specs=[SMEM] * len(place) + spe...  12.9 us
  transfers between devices with their start and end apart: 17, of which 13 were waited for; matrix products, arithmetic and copies ran while one was open for 0% of the time, Pallas kernels for 15%

profile of v7, /device:TPU:0, one launch (start us, length us, event | category | flops | bytes accessed | tf_op | source)
XLA Modules:
  0.0 60.6 jit_solution(11447702128774799859)
XLA Ops:
  0.6 1.7 %shard_map.93 = (f32[256,128]{1,0:T(8,128)S(1)}, f32[256,128]{1,0:T(8,128)S(1)}, f32[256,128]{1,0:T(8,128)S(1)}, f32[256,128]{1,0:T(8,128)S(1)}, f32[128,1024]{1,0:T(8,128)S(1)}, /*index=5*/f32[128,1024]{1,0:T(8,128)S(1)}) custom-call(f32[128,1024]{1,0:T(8,128)} %k_hbm.1, f32[128,1024]{1,0:T(8,128)} %v_hbm.1), custom_call_target="tpu_custom_call" | custom-call | flops 100663296 | bytes 2621440 | tf_op jit(solution)/shard_map/pallas_call | solution.py:59
  2.3 3.0 %collective-permute-start = (f32[256,128]{1,0:T(8,128)S(1)}, f32[256,128]{1,0:T(8,128)S(1)}, u32[]{:S(2)}, u32[]{:S(2)}) collective-permute-start(f32[256,128]{1,0:T(8,128)S(1)} %get-tuple-element.55), channel_id=1, source_target_pairs={{0,4},{4,0},{8,12},{12,8},{16,20},{20,16},{24,28},{28,24},{1,5},{5... | collective-permute-start | bytes 393224 | tf_op jit(solution)/shard_map/ppermute | solution.py:308
  5.4 1.6 %collective-permute-start.1 = (f32[256,128]{1,0:T(8,128)S(1)}, f32[256,128]{1,0:T(8,128)S(1)}, u32[]{:S(2)}, u32[]{:S(2)}) collective-permute-start(f32[256,128]{1,0:T(8,128)S(1)} %get-tuple-element.56), channel_id=1, source_target_pairs={{0,8},{4,12},{8,0},{12,4},{16,24},{20,28},{24,16},{28,20},{1,9},{5... | collective-permute-start | bytes 393224 | tf_op jit(solution)/shard_map/ppermute | solution.py:308
  7.0 1.9 %collective-permute-done.refs_1_ = f32[256,128]{1,0:T(8,128)S(1)} collective-permute-done((f32[256,128]{1,0:T(8,128)S(1)}, f32[256,128]{1,0:T(8,128)S(1)}, u32[]{:S(2)}, u32[]{:S(2)}) %collective-permute-start) | collective-permute-done | bytes 131104 | tf_op jit(solution)/shard_map/ppermute | solution.py:308
  8.9 2.9 %collective-permute-done.1.refs_2_ = f32[256,128]{1,0:T(8,128)S(1)} collective-permute-done((f32[256,128]{1,0:T(8,128)S(1)}, f32[256,128]{1,0:T(8,128)S(1)}, u32[]{:S(2)}, u32[]{:S(2)}) %collective-permute-start.1) | collective-permute-done | bytes 131104 | tf_op jit(solution)/shard_map/ppermute | solution.py:308
  11.7 1.2 %collective-permute-done.2.refs_3_ = f32[256,128]{1,0:T(8,128)S(1)} collective-permute-done((f32[256,128]{1,0:T(8,128)S(1)}, f32[256,128]{1,0:T(8,128)S(1)}, u32[]{:S(2)}, u32[]{:S(2)}) %collective-permute-start.2) | collective-permute-done | bytes 131104 | tf_op jit(solution)/shard_map/ppermute | solution.py:308
  13.0 3.8 %collective-permute-start.3 = (f32[256,128]{1,0:T(8,128)S(1)}, f32[256,128]{1,0:T(8,128)S(1)}, u32[]{:S(2)}, u32[]{:S(2)}) collective-permute-start(f32[256,128]{1,0:T(8,128)S(1)} %shard_map.95), channel_id=1, source_target_pairs={{0,24},{4,28},{8,16},{12,20},{16,8},{20,12},{24,0},{28,4},{1,25},{... | collective-permute-start | bytes 393224 | tf_op jit(solution)/shard_map/ppermute | solution.py:308
  16.8 3.7 %shard_map.94 = (f32[128,1024]{1,0:T(8,128)S(1)}, f32[8,128,128]{2,1,0:T(8,128)S(1)}, f32[8,128,128]{2,1,0:T(8,128)S(1)}, f32[128,1024]{1,0:T(8,128)S(1)}, f32[1...) custom-call(s32[1]{0:T(128)} %bitcast.seat, f32[128,1024]{1,0:T(8,128)} %q_hbm.1, f32[128,1024]{1,0:T(8,128)S(1)} %get-tuple-element.47.k, ...), custom_call_target="tpu_custom_call" | custom-call | flops 201326592 | bytes 4727296 | tf_op jit(solution)/shard_map/pallas_call | solution.py:59
  20.6 1.6 %collective-permute-start.4 = (f32[256,128]{1,0:T(8,128)S(1)}, f32[256,128]{1,0:T(8,128)S(1)}, u32[]{:S(2)}, u32[]{:S(2)}) collective-permute-start(f32[256,128]{1,0:T(8,128)S(1)} %get-tuple-element.60), channel_id=1, source_target_pairs={{0,4},{4,0},{8,12},{12,8},{16,20},{20,16},{24,28},{28,24},{1,5},{5... | collective-permute-start | bytes 393224 | tf_op jit(solution)/shard_map/ppermute | solution.py:308
  23.0 1.2 %collective-permute-start.6 = (f32[256,128]{1,0:T(8,128)S(1)}, f32[256,128]{1,0:T(8,128)S(1)}, u32[]{:S(2)}, u32[]{:S(2)}) collective-permute-start(f32[256,128]{1,0:T(8,128)S(1)} %get-tuple-element.65), channel_id=1, source_target_pairs={{0,12},{4,8},{8,4},{12,0},{16,28},{20,24},{24,20},{28,16},{1,13},{... | collective-permute-start | bytes 393224 | tf_op jit(solution)/shard_map/ppermute | solution.py:308
  24.2 2.9 %collective-permute-done.4.refs_1_.refs_5_ = f32[256,128]{1,0:T(8,128)S(1)} collective-permute-done((f32[256,128]{1,0:T(8,128)S(1)}, f32[256,128]{1,0:T(8,128)S(1)}, u32[]{:S(2)}, u32[]{:S(2)}) %collective-permute-start.4) | collective-permute-done | bytes 131104 | tf_op jit(solution)/shard_map/ppermute | solution.py:308
  27.8 1.1 %collective-permute-done.6.refs_0_.refs_7_ = f32[256,128]{1,0:T(8,128)S(1)} collective-permute-done((f32[256,128]{1,0:T(8,128)S(1)}, f32[256,128]{1,0:T(8,128)S(1)}, u32[]{:S(2)}, u32[]{:S(2)}) %collective-permute-start.6) | collective-permute-done | bytes 131104 | tf_op jit(solution)/shard_map/ppermute | solution.py:308
  29.2 1.6 %collective-permute-start.8 = (f32[8,128]{1,0:T(8,128)S(1)}, f32[8,128]{1,0:T(8,128)S(1)}, u32[]{:S(2)}, u32[]{:S(2)}) collective-permute-start(f32[8,128]{1,0:T(8,128)S(1)} %get-tuple-element.69.refs_4_), channel_id=1, source_target_pairs={{0,2},{1,3},{2,0},{3,1},{4,6},{5,7},{6,4},{7,5},{8,10},{9,11},{10,... | collective-permute-start | bytes 12296 | tf_op jit(solution)/shard_map/ppermute | solution.py:308
  31.1 1.2 %collective-permute-done.9.refs_7_ = f32[8,128]{1,0:T(8,128)S(1)} collective-permute-done((f32[8,128]{1,0:T(8,128)S(1)}, f32[8,128]{1,0:T(8,128)S(1)}, u32[]{:S(2)}, u32[]{:S(2)}) %collective-permute-start.9) | collective-permute-done | bytes 4128 | tf_op jit(solution)/shard_map/ppermute | solution.py:308
  33.4 1.7 %collective-permute-start.11 = (f32[264,128]{1,0:T(8,128)S(1)}, f32[264,128]{1,0:T(8,128)S(1)}, u32[]{:S(2)}, u32[]{:S(2)}) collective-permute-start(f32[264,128]{1,0:T(8,128)S(1)} %get-tuple-element.75), channel_id=1, source_target_pairs={{0,8},{4,12},{8,0},{12,4},{16,24},{20,28},{24,16},{28,20},{1,9},{5... | collective-permute-start | bytes 405512 | tf_op jit(solution)/shard_map/ppermute | solution.py:308
  35.5 1.4 %collective-permute-start.12 = (f32[256,128]{1,0:T(8,128)S(1)}, f32[256,128]{1,0:T(8,128)S(1)}, u32[]{:S(2)}, u32[]{:S(2)}) collective-permute-start(f32[256,128]{1,0:T(8,128)S(1)} %get-tuple-element.76), channel_id=1, source_target_pairs={{0,12},{4,8},{8,4},{12,0},{16,28},{20,24},{24,20},{28,16},{1,13},{... | collective-permute-start | bytes 393224 | tf_op jit(solution)/shard_map/ppermute | solution.py:308
  36.9 6.2 %collective-permute-done.10.refs_1_ = f32[256,128]{1,0:T(8,128)S(1)} collective-permute-done((f32[256,128]{1,0:T(8,128)S(1)}, f32[256,128]{1,0:T(8,128)S(1)}, u32[]{:S(2)}, u32[]{:S(2)}) %collective-permute-start.10) | collective-permute-done | bytes 131104 | tf_op jit(solution)/shard_map/ppermute | solution.py:308
  43.2 3.0 %collective-permute-start.13 = (f32[264,128]{1,0:T(8,128)S(1)}, f32[264,128]{1,0:T(8,128)S(1)}, u32[]{:S(2)}, u32[]{:S(2)}) collective-permute-start(f32[264,128]{1,0:T(8,128)S(1)} %shard_map.101.refs_4_), channel_id=1, source_target_pairs={{0,24},{4,28},{8,16},{12,20},{16,8},{20,12},{24,0},{28,4},{1,25},{... | collective-permute-start | bytes 405512 | tf_op jit(solution)/shard_map/ppermute | solution.py:308
  46.2 2.4 %shard_map.100 = (f32[128,1024]{1,0:T(8,128)S(1)}, f32[128,1024]{1,0:T(8,128)S(1)}, f32[128,1024]{1,0:T(8,128)S(1)}) custom-call(s32[1]{0:T(128)} %bitcast.seat, f32[128,1024]{1,0:T(8,128)S(1)} %get-tuple-element.49.q, f32[128,1024]{1,0:T(8,128)S(1)} %get-tuple-element.47.k, f32[128,1024]{1,0:T(8,128)S(1)} %get-tuple-element.48.v, ...), custom_call_target="tpu_custom_call" | custom-call | flops 503316480 | bytes 5246976 | tf_op jit(solution)/shard_map/pallas_call | solution.py:59
  48.6 1.5 %collective-permute-done.13.refs_5_ = f32[264,128]{1,0:T(8,128)S(1)} collective-permute-done((f32[264,128]{1,0:T(8,128)S(1)}, f32[264,128]{1,0:T(8,128)S(1)}, u32[]{:S(2)}, u32[]{:S(2)}) %collective-permute-start.13) | collective-permute-done | bytes 135200 | tf_op jit(solution)/shard_map/ppermute | solution.py:308
  50.9 2.7 %collective-permute-start.16 = (f32[256,128]{1,0:T(8,128)S(1)}, f32[256,128]{1,0:T(8,128)S(1)}, u32[]{:S(2)}, u32[]{:S(2)}) collective-permute-start(f32[256,128]{1,0:T(8,128)S(1)} %get-tuple-element.82), channel_id=1, source_target_pairs={{0,8},{4,12},{8,0},{12,4},{16,24},{20,28},{24,16},{28,20},{1,9},{5... | collective-permute-start | bytes 393224 | tf_op jit(solution)/shard_map/ppermute | solution.py:308
  53.9 1.5 %collective-permute-done.14.refs_1_ = f32[264,128]{1,0:T(8,128)S(1)} collective-permute-done((f32[264,128]{1,0:T(8,128)S(1)}, f32[264,128]{1,0:T(8,128)S(1)}, u32[]{:S(2)}, u32[]{:S(2)}) %collective-permute-start.14) | collective-permute-done | bytes 135200 | tf_op jit(solution)/shard_map/ppermute | solution.py:308
  55.4 1.8 %shard_map.103 = (f32[1,1]{1,0:T(1,128)}, f32[128,1024]{1,0:T(8,128)}, f32[128,1024]{1,0:T(8,128)}, f32[128,1024]{1,0:T(8,128)}) custom-call(s32[1]{0:T(128)} %bitcast.seat, f32[128,1024]{1,0:T(8,128)S(1)} %get-tuple-element.47.k, f32[128,1024]{1,0:T(8,128)S(1)} %get-tuple-element.48.v, f32[128,1024]{1,0:T(8,128)S(1)} %get-tuple-element.71.refs_6_.part_k, ...), custom_call_target="tpu_custom_call" | custom-call | flops 100663296 | bytes 4595716 | tf_op jit(solution)/shard_map/pallas_call | solution.py:59
  58.0 1.0 %shard_map.104 = (f32[128,1024]{1,0:T(8,128)}, f32[128,1024]{1,0:T(8,128)}) custom-call(s32[1]{0:T(128)} %bitcast.seat, f32[128,1024]{1,0:T(8,128)S(1)} %get-tuple-element.47.k, f32[128,1024]{1,0:T(8,128)S(1)} %get-tuple-element.48.v, f32[128,1024]{1,0:T(8,128)S(1)} %get-tuple-element.71.refs_6_.part_k, ...), custom_call_target="tpu_custom_call", output_to_operand_aliasing={{0}: (8, {}), {1}: (9, {})} | custom-call | flops 50331648 | bytes 4595712 | tf_op jit(solution)/shard_map/pallas_call | solution.py:59
  (23 shorter events, 7.2 us)
Async XLA Ops:
  2.3 6.5 %collective-permute-start = (f32[256,128]{1,0:T(8,128)S(1)}, f32[256,128]{1,0:T(8,128)S(1)}, u32[]{:S(2)}, u32[]{:S(2)}) collective-permute-start(f32[256,128]{1,0:T(8,128)S(1)} %get-tuple-element.55), channel_id=1, source_target_pairs={{0,4},{4,0},{8,12},{12,8},{16,20},{20,16},{24,28},{28,24},{1,5},{5... | collective-permute-start | bytes 393224 | tf_op jit(solution)/shard_map/ppermute | solution.py:308
  5.4 6.4 %collective-permute-start.1 = (f32[256,128]{1,0:T(8,128)S(1)}, f32[256,128]{1,0:T(8,128)S(1)}, u32[]{:S(2)}, u32[]{:S(2)}) collective-permute-start(f32[256,128]{1,0:T(8,128)S(1)} %get-tuple-element.56), channel_id=1, source_target_pairs={{0,8},{4,12},{8,0},{12,4},{16,24},{20,28},{24,16},{28,20},{1,9},{5... | collective-permute-start | bytes 393224 | tf_op jit(solution)/shard_map/ppermute | solution.py:308
  7.0 6.0 %collective-permute-start.2 = (f32[256,128]{1,0:T(8,128)S(1)}, f32[256,128]{1,0:T(8,128)S(1)}, u32[]{:S(2)}, u32[]{:S(2)}) collective-permute-start(f32[256,128]{1,0:T(8,128)S(1)} %get-tuple-element.57), channel_id=1, source_target_pairs={{0,12},{4,8},{8,4},{12,0},{16,28},{20,24},{24,20},{28,16},{1,13},{... | collective-permute-start | bytes 393224 | tf_op jit(solution)/shard_map/ppermute | solution.py:308
  13.0 7.5 %collective-permute-start.3 = (f32[256,128]{1,0:T(8,128)S(1)}, f32[256,128]{1,0:T(8,128)S(1)}, u32[]{:S(2)}, u32[]{:S(2)}) collective-permute-start(f32[256,128]{1,0:T(8,128)S(1)} %shard_map.95), channel_id=1, source_target_pairs={{0,24},{4,28},{8,16},{12,20},{16,8},{20,12},{24,0},{28,4},{1,25},{... | collective-permute-start | bytes 393224 | tf_op jit(solution)/shard_map/ppermute | solution.py:308
  20.6 6.4 %collective-permute-start.4 = (f32[256,128]{1,0:T(8,128)S(1)}, f32[256,128]{1,0:T(8,128)S(1)}, u32[]{:S(2)}, u32[]{:S(2)}) collective-permute-start(f32[256,128]{1,0:T(8,128)S(1)} %get-tuple-element.60), channel_id=1, source_target_pairs={{0,4},{4,0},{8,12},{12,8},{16,20},{20,16},{24,28},{28,24},{1,5},{5... | collective-permute-start | bytes 393224 | tf_op jit(solution)/shard_map/ppermute | solution.py:308
  22.2 5.3 %collective-permute-start.5 = (f32[256,128]{1,0:T(8,128)S(1)}, f32[256,128]{1,0:T(8,128)S(1)}, u32[]{:S(2)}, u32[]{:S(2)}) collective-permute-start(f32[256,128]{1,0:T(8,128)S(1)} %get-tuple-element.61), channel_id=1, source_target_pairs={{0,8},{4,12},{8,0},{12,4},{16,24},{20,28},{24,16},{28,20},{1,9},{5... | collective-permute-start | bytes 393224 | tf_op jit(solution)/shard_map/ppermute | solution.py:308
  23.0 5.9 %collective-permute-start.6 = (f32[256,128]{1,0:T(8,128)S(1)}, f32[256,128]{1,0:T(8,128)S(1)}, u32[]{:S(2)}, u32[]{:S(2)}) collective-permute-start(f32[256,128]{1,0:T(8,128)S(1)} %get-tuple-element.65), channel_id=1, source_target_pairs={{0,12},{4,8},{8,4},{12,0},{16,28},{20,24},{24,20},{28,16},{1,13},{... | collective-permute-start | bytes 393224 | tf_op jit(solution)/shard_map/ppermute | solution.py:308
  29.2 3.1 %collective-permute-start.9 = (f32[8,128]{1,0:T(8,128)S(1)}, f32[8,128]{1,0:T(8,128)S(1)}, u32[]{:S(2)}, u32[]{:S(2)}) collective-permute-start(f32[8,128]{1,0:T(8,128)S(1)} %get-tuple-element.69.refs_4_), channel_id=1, source_target_pairs={{0,3},{1,2},{2,1},{3,0},{4,7},{5,6},{6,5},{7,4},{8,11},{9,10},{10,... | collective-permute-start | bytes 12296 | tf_op jit(solution)/shard_map/ppermute | solution.py:308
  29.2 3.7 %collective-permute-start.8 = (f32[8,128]{1,0:T(8,128)S(1)}, f32[8,128]{1,0:T(8,128)S(1)}, u32[]{:S(2)}, u32[]{:S(2)}) collective-permute-start(f32[8,128]{1,0:T(8,128)S(1)} %get-tuple-element.69.refs_4_), channel_id=1, source_target_pairs={{0,2},{1,3},{2,0},{3,1},{4,6},{5,7},{6,4},{7,5},{8,10},{9,11},{10,... | collective-permute-start | bytes 12296 | tf_op jit(solution)/shard_map/ppermute | solution.py:308
  30.8 2.1 %collective-permute-start.7 = (f32[8,128]{1,0:T(8,128)S(1)}, f32[8,128]{1,0:T(8,128)S(1)}, u32[]{:S(2)}, u32[]{:S(2)}) collective-permute-start(f32[8,128]{1,0:T(8,128)S(1)} %get-tuple-element.69.refs_4_), channel_id=1, source_target_pairs={{0,1},{1,0},{2,3},{3,2},{4,5},{5,4},{6,7},{7,6},{8,9},{9,8},{10,11... | collective-permute-start | bytes 12296 | tf_op jit(solution)/shard_map/ppermute | solution.py:308
  33.4 9.8 %collective-permute-start.11 = (f32[264,128]{1,0:T(8,128)S(1)}, f32[264,128]{1,0:T(8,128)S(1)}, u32[]{:S(2)}, u32[]{:S(2)}) collective-permute-start(f32[264,128]{1,0:T(8,128)S(1)} %get-tuple-element.75), channel_id=1, source_target_pairs={{0,8},{4,12},{8,0},{12,4},{16,24},{20,28},{24,16},{28,20},{1,9},{5... | collective-permute-start | bytes 405512 | tf_op jit(solution)/shard_map/ppermute | solution.py:308
  35.1 8.0 %collective-permute-start.10 = (f32[256,128]{1,0:T(8,128)S(1)}, f32[256,128]{1,0:T(8,128)S(1)}, u32[]{:S(2)}, u32[]{:S(2)}) collective-permute-start(f32[256,128]{1,0:T(8,128)S(1)} %get-tuple-element.74), channel_id=1, source_target_pairs={{0,4},{4,0},{8,12},{12,8},{16,20},{20,16},{24,28},{28,24},{1,5},{5... | collective-permute-start | bytes 393224 | tf_op jit(solution)/shard_map/ppermute | solution.py:308
  35.5 7.6 %collective-permute-start.12 = (f32[256,128]{1,0:T(8,128)S(1)}, f32[256,128]{1,0:T(8,128)S(1)}, u32[]{:S(2)}, u32[]{:S(2)}) collective-permute-start(f32[256,128]{1,0:T(8,128)S(1)} %get-tuple-element.76), channel_id=1, source_target_pairs={{0,12},{4,8},{8,4},{12,0},{16,28},{20,24},{24,20},{28,16},{1,13},{... | collective-permute-start | bytes 393224 | tf_op jit(solution)/shard_map/ppermute | solution.py:308
  43.2 7.0 %collective-permute-start.13 = (f32[264,128]{1,0:T(8,128)S(1)}, f32[264,128]{1,0:T(8,128)S(1)}, u32[]{:S(2)}, u32[]{:S(2)}) collective-permute-start(f32[264,128]{1,0:T(8,128)S(1)} %shard_map.101.refs_4_), channel_id=1, source_target_pairs={{0,24},{4,28},{8,16},{12,20},{16,8},{20,12},{24,0},{28,4},{1,25},{... | collective-permute-start | bytes 405512 | tf_op jit(solution)/shard_map/ppermute | solution.py:308
  50.3 5.1 %collective-permute-start.14 = (f32[264,128]{1,0:T(8,128)S(1)}, f32[264,128]{1,0:T(8,128)S(1)}, u32[]{:S(2)}, u32[]{:S(2)}) collective-permute-start(f32[264,128]{1,0:T(8,128)S(1)} %get-tuple-element.77.sent), channel_id=1, source_target_pairs={{0,4},{4,0},{8,12},{12,8},{16,20},{20,16},{24,28},{28,24},{1,5},{5... | collective-permute-start | bytes 405512 | tf_op jit(solution)/shard_map/ppermute | solution.py:308
  50.9 7.1 %collective-permute-start.16 = (f32[256,128]{1,0:T(8,128)S(1)}, f32[256,128]{1,0:T(8,128)S(1)}, u32[]{:S(2)}, u32[]{:S(2)}) collective-permute-start(f32[256,128]{1,0:T(8,128)S(1)} %get-tuple-element.82), channel_id=1, source_target_pairs={{0,8},{4,12},{8,0},{12,4},{16,24},{20,28},{24,16},{28,20},{1,9},{5... | collective-permute-start | bytes 393224 | tf_op jit(solution)/shard_map/ppermute | solution.py:308
  53.6 6.0 %collective-permute-start.15 = (f32[256,128]{1,0:T(8,128)S(1)}, f32[256,128]{1,0:T(8,128)S(1)}, u32[]{:S(2)}, u32[]{:S(2)}) collective-permute-start(f32[256,128]{1,0:T(8,128)S(1)} %get-tuple-element.81), channel_id=1, source_target_pairs={{0,12},{4,8},{8,4},{12,0},{16,28},{20,24},{24,20},{28,16},{1,13},{... | collective-permute-start | bytes 393224 | tf_op jit(solution)/shard_map/ppermute | solution.py:308

commit v8 on v7

--- a/solution.py
+++ b/solution.py
@@ -259,7 +259,7 @@
 
 def later_kernel(plan, seat, *refs):
     group = plan.group
-    states, totals, outs = refs[:group], refs[group : -group - 1], refs[-group:]
+    states, totals, outs = refs[:group], refs[group:-group], refs[-group:]
     outer = outer_sum(plan, seat[0], True, totals[1:])
     tail = totals[0][plan.tail, :]
     for other in totals[1:]:
@@ -425,8 +425,6 @@
         seat,
         *states,
         *grad_totals,
-        part_key,
-        specs=[VMEM] * (group + len(grad_totals)) + [ANY],
     )
     sent = later[min(1, group - 1)]
     later = swap_all(later, "seq")

time: 60.8 us -> 60.8 us (level)
  transfers between devices with their start and end apart: 17 -> 17, of which waited for: 13 -> 11; matrix products, arithmetic and copies ran while one was open for 0% -> 0% of each run, Pallas kernels for 15% -> 15%
where the time goes in v8:
time: 60.8 us; the launch traced here: 60.6 us
  starting transfers between devices  24 us (39%)
  waiting for transfers between devices  22.9 us (38%)
  Pallas kernels  12.9 us (21%)
  between operations  0.75 us (1%)
    ppermute x17, starting transfers between devices, swap(): lax.ppermute(value, axis, [(i, i ^ step) for i in range(lax.axis_size(axi...  24 us
    ppermute x17, waiting for transfers between devices, swap(): lax.ppermute(value, axis, [(i, i ^ step) for i in range(lax.axis_size(axi...  22.9 us
    pallas_call x13, Pallas kernels, call(): pl.pallas_call(kernel, out_shape=outs, in_specs=[SMEM] * len(place) + spe...  12.9 us
  transfers between devices with their start and end apart: 17, of which 11 were waited for; matrix products, arithmetic and copies ran while one was open for 0% of the time, Pallas kernels for 15%

profile of v8, /device:TPU:0, one launch (start us, length us, event | category | flops | bytes accessed | tf_op | source)
XLA Modules:
  0.0 60.6 jit_solution(11770996447051696627)
XLA Ops:
  0.6 1.7 %shard_map.93 = (f32[256,128]{1,0:T(8,128)S(1)}, f32[256,128]{1,0:T(8,128)S(1)}, f32[256,128]{1,0:T(8,128)S(1)}, f32[256,128]{1,0:T(8,128)S(1)}, f32[128,1024]{1,0:T(8,128)S(1)}, /*index=5*/f32[128,1024]{1,0:T(8,128)S(1)}) custom-call(f32[128,1024]{1,0:T(8,128)} %k_hbm.1, f32[128,1024]{1,0:T(8,128)} %v_hbm.1), custom_call_target="tpu_custom_call" | custom-call | flops 100663296 | bytes 2621440 | tf_op jit(solution)/shard_map/pallas_call | solution.py:59
  2.3 3.0 %collective-permute-start = (f32[256,128]{1,0:T(8,128)S(1)}, f32[256,128]{1,0:T(8,128)S(1)}, u32[]{:S(2)}, u32[]{:S(2)}) collective-permute-start(f32[256,128]{1,0:T(8,128)S(1)} %get-tuple-element.55), channel_id=1, source_target_pairs={{0,4},{4,0},{8,12},{12,8},{16,20},{20,16},{24,28},{28,24},{1,5},{5... | collective-permute-start | bytes 393224 | tf_op jit(solution)/shard_map/ppermute | solution.py:308
  5.4 1.6 %collective-permute-start.1 = (f32[256,128]{1,0:T(8,128)S(1)}, f32[256,128]{1,0:T(8,128)S(1)}, u32[]{:S(2)}, u32[]{:S(2)}) collective-permute-start(f32[256,128]{1,0:T(8,128)S(1)} %get-tuple-element.56), channel_id=1, source_target_pairs={{0,8},{4,12},{8,0},{12,4},{16,24},{20,28},{24,16},{28,20},{1,9},{5... | collective-permute-start | bytes 393224 | tf_op jit(solution)/shard_map/ppermute | solution.py:308
  7.0 1.9 %collective-permute-done.refs_1_ = f32[256,128]{1,0:T(8,128)S(1)} collective-permute-done((f32[256,128]{1,0:T(8,128)S(1)}, f32[256,128]{1,0:T(8,128)S(1)}, u32[]{:S(2)}, u32[]{:S(2)}) %collective-permute-start) | collective-permute-done | bytes 131104 | tf_op jit(solution)/shard_map/ppermute | solution.py:308
  8.9 2.9 %collective-permute-done.1.refs_2_ = f32[256,128]{1,0:T(8,128)S(1)} collective-permute-done((f32[256,128]{1,0:T(8,128)S(1)}, f32[256,128]{1,0:T(8,128)S(1)}, u32[]{:S(2)}, u32[]{:S(2)}) %collective-permute-start.1) | collective-permute-done | bytes 131104 | tf_op jit(solution)/shard_map/ppermute | solution.py:308
  11.7 1.2 %collective-permute-done.2.refs_3_ = f32[256,128]{1,0:T(8,128)S(1)} collective-permute-done((f32[256,128]{1,0:T(8,128)S(1)}, f32[256,128]{1,0:T(8,128)S(1)}, u32[]{:S(2)}, u32[]{:S(2)}) %collective-permute-start.2) | collective-permute-done | bytes 131104 | tf_op jit(solution)/shard_map/ppermute | solution.py:308
  13.0 3.8 %collective-permute-start.3 = (f32[256,128]{1,0:T(8,128)S(1)}, f32[256,128]{1,0:T(8,128)S(1)}, u32[]{:S(2)}, u32[]{:S(2)}) collective-permute-start(f32[256,128]{1,0:T(8,128)S(1)} %shard_map.95), channel_id=1, source_target_pairs={{0,24},{4,28},{8,16},{12,20},{16,8},{20,12},{24,0},{28,4},{1,25},{... | collective-permute-start | bytes 393224 | tf_op jit(solution)/shard_map/ppermute | solution.py:308
  16.8 3.7 %shard_map.94 = (f32[128,1024]{1,0:T(8,128)S(1)}, f32[8,128,128]{2,1,0:T(8,128)S(1)}, f32[8,128,128]{2,1,0:T(8,128)S(1)}, f32[128,1024]{1,0:T(8,128)S(1)}, f32[1...) custom-call(s32[1]{0:T(128)} %bitcast.seat, f32[128,1024]{1,0:T(8,128)} %q_hbm.1, f32[128,1024]{1,0:T(8,128)S(1)} %get-tuple-element.47.k, ...), custom_call_target="tpu_custom_call" | custom-call | flops 201326592 | bytes 4727296 | tf_op jit(solution)/shard_map/pallas_call | solution.py:59
  20.6 1.6 %collective-permute-start.4 = (f32[256,128]{1,0:T(8,128)S(1)}, f32[256,128]{1,0:T(8,128)S(1)}, u32[]{:S(2)}, u32[]{:S(2)}) collective-permute-start(f32[256,128]{1,0:T(8,128)S(1)} %get-tuple-element.60), channel_id=1, source_target_pairs={{0,4},{4,0},{8,12},{12,8},{16,20},{20,16},{24,28},{28,24},{1,5},{5... | collective-permute-start | bytes 393224 | tf_op jit(solution)/shard_map/ppermute | solution.py:308
  23.0 1.2 %collective-permute-start.6 = (f32[256,128]{1,0:T(8,128)S(1)}, f32[256,128]{1,0:T(8,128)S(1)}, u32[]{:S(2)}, u32[]{:S(2)}) collective-permute-start(f32[256,128]{1,0:T(8,128)S(1)} %get-tuple-element.65), channel_id=1, source_target_pairs={{0,12},{4,8},{8,4},{12,0},{16,28},{20,24},{24,20},{28,16},{1,13},{... | collective-permute-start | bytes 393224 | tf_op jit(solution)/shard_map/ppermute | solution.py:308
  24.2 2.9 %collective-permute-done.4.refs_1_.refs_5_ = f32[256,128]{1,0:T(8,128)S(1)} collective-permute-done((f32[256,128]{1,0:T(8,128)S(1)}, f32[256,128]{1,0:T(8,128)S(1)}, u32[]{:S(2)}, u32[]{:S(2)}) %collective-permute-start.4) | collective-permute-done | bytes 131104 | tf_op jit(solution)/shard_map/ppermute | solution.py:308
  27.8 1.1 %collective-permute-done.6.refs_0_.refs_7_ = f32[256,128]{1,0:T(8,128)S(1)} collective-permute-done((f32[256,128]{1,0:T(8,128)S(1)}, f32[256,128]{1,0:T(8,128)S(1)}, u32[]{:S(2)}, u32[]{:S(2)}) %collective-permute-start.6) | collective-permute-done | bytes 131104 | tf_op jit(solution)/shard_map/ppermute | solution.py:308
  29.2 1.6 %collective-permute-start.8 = (f32[8,128]{1,0:T(8,128)S(1)}, f32[8,128]{1,0:T(8,128)S(1)}, u32[]{:S(2)}, u32[]{:S(2)}) collective-permute-start(f32[8,128]{1,0:T(8,128)S(1)} %get-tuple-element.69.refs_4_), channel_id=1, source_target_pairs={{0,2},{1,3},{2,0},{3,1},{4,6},{5,7},{6,4},{7,5},{8,10},{9,11},{10,... | collective-permute-start | bytes 12296 | tf_op jit(solution)/shard_map/ppermute | solution.py:308
  31.1 1.2 %collective-permute-done.9.refs_7_ = f32[8,128]{1,0:T(8,128)S(1)} collective-permute-done((f32[8,128]{1,0:T(8,128)S(1)}, f32[8,128]{1,0:T(8,128)S(1)}, u32[]{:S(2)}, u32[]{:S(2)}) %collective-permute-start.9) | collective-permute-done | bytes 4128 | tf_op jit(solution)/shard_map/ppermute | solution.py:308
  33.4 1.7 %collective-permute-start.11 = (f32[264,128]{1,0:T(8,128)S(1)}, f32[264,128]{1,0:T(8,128)S(1)}, u32[]{:S(2)}, u32[]{:S(2)}) collective-permute-start(f32[264,128]{1,0:T(8,128)S(1)} %get-tuple-element.75), channel_id=1, source_target_pairs={{0,8},{4,12},{8,0},{12,4},{16,24},{20,28},{24,16},{28,20},{1,9},{5... | collective-permute-start | bytes 405512 | tf_op jit(solution)/shard_map/ppermute | solution.py:308
  35.5 1.4 %collective-permute-start.12 = (f32[256,128]{1,0:T(8,128)S(1)}, f32[256,128]{1,0:T(8,128)S(1)}, u32[]{:S(2)}, u32[]{:S(2)}) collective-permute-start(f32[256,128]{1,0:T(8,128)S(1)} %get-tuple-element.76), channel_id=1, source_target_pairs={{0,12},{4,8},{8,4},{12,0},{16,28},{20,24},{24,20},{28,16},{1,13},{... | collective-permute-start | bytes 393224 | tf_op jit(solution)/shard_map/ppermute | solution.py:308
  37.0 6.2 %collective-permute-done.10.refs_1_ = f32[256,128]{1,0:T(8,128)S(1)} collective-permute-done((f32[256,128]{1,0:T(8,128)S(1)}, f32[256,128]{1,0:T(8,128)S(1)}, u32[]{:S(2)}, u32[]{:S(2)}) %collective-permute-start.10) | collective-permute-done | bytes 131104 | tf_op jit(solution)/shard_map/ppermute | solution.py:308
  43.2 3.0 %collective-permute-start.13 = (f32[264,128]{1,0:T(8,128)S(1)}, f32[264,128]{1,0:T(8,128)S(1)}, u32[]{:S(2)}, u32[]{:S(2)}) collective-permute-start(f32[264,128]{1,0:T(8,128)S(1)} %shard_map.101.refs_4_), channel_id=1, source_target_pairs={{0,24},{4,28},{8,16},{12,20},{16,8},{20,12},{24,0},{28,4},{1,25},{... | collective-permute-start | bytes 405512 | tf_op jit(solution)/shard_map/ppermute | solution.py:308
  46.2 4.0 %collective-permute-done.13.refs_5_ = f32[264,128]{1,0:T(8,128)S(1)} collective-permute-done((f32[264,128]{1,0:T(8,128)S(1)}, f32[264,128]{1,0:T(8,128)S(1)}, u32[]{:S(2)}, u32[]{:S(2)}) %collective-permute-start.13) | collective-permute-done | bytes 135200 | tf_op jit(solution)/shard_map/ppermute | solution.py:308
  50.9 2.7 %collective-permute-start.16 = (f32[256,128]{1,0:T(8,128)S(1)}, f32[256,128]{1,0:T(8,128)S(1)}, u32[]{:S(2)}, u32[]{:S(2)}) collective-permute-start(f32[256,128]{1,0:T(8,128)S(1)} %get-tuple-element.82), channel_id=1, source_target_pairs={{0,8},{4,12},{8,0},{12,4},{16,24},{20,28},{24,16},{28,20},{1,9},{5... | collective-permute-start | bytes 393224 | tf_op jit(solution)/shard_map/ppermute | solution.py:308
  53.9 2.4 %shard_map.100 = (f32[128,1024]{1,0:T(8,128)S(1)}, f32[128,1024]{1,0:T(8,128)S(1)}, f32[128,1024]{1,0:T(8,128)S(1)}) custom-call(s32[1]{0:T(128)} %bitcast.seat, f32[128,1024]{1,0:T(8,128)S(1)} %get-tuple-element.49.q, f32[128,1024]{1,0:T(8,128)S(1)} %get-tuple-element.47.k, f32[128,1024]{1,0:T(8,128)S(1)} %get-tuple-element.48.v, ...), custom_call_target="tpu_custom_call" | custom-call | flops 503316480 | bytes 5246976 | tf_op jit(solution)/shard_map/pallas_call | solution.py:59
  56.3 1.8 %shard_map.103 = (f32[1,1]{1,0:T(1,128)}, f32[128,1024]{1,0:T(8,128)}, f32[128,1024]{1,0:T(8,128)}, f32[128,1024]{1,0:T(8,128)}) custom-call(s32[1]{0:T(128)} %bitcast.seat, f32[128,1024]{1,0:T(8,128)S(1)} %get-tuple-element.47.k, f32[128,1024]{1,0:T(8,128)S(1)} %get-tuple-element.48.v, f32[128,1024]{1,0:T(8,128)S(1)} %get-tuple-element.71.part_k, ...), custom_call_target="tpu_custom_call" | custom-call | flops 100663296 | bytes 4595716 | tf_op jit(solution)/shard_map/pallas_call | solution.py:59
  58.2 1.0 %shard_map.104 = (f32[128,1024]{1,0:T(8,128)}, f32[128,1024]{1,0:T(8,128)}) custom-call(s32[1]{0:T(128)} %bitcast.seat, f32[128,1024]{1,0:T(8,128)S(1)} %get-tuple-element.47.k, f32[128,1024]{1,0:T(8,128)S(1)} %get-tuple-element.48.v, f32[128,1024]{1,0:T(8,128)S(1)} %get-tuple-element.71.part_k, ...), custom_call_target="tpu_custom_call", output_to_operand_aliasing={{0}: (8, {}), {1}: (9, {})} | custom-call | flops 50331648 | bytes 4595712 | tf_op jit(solution)/shard_map/pallas_call | solution.py:59
  59.6 1.0 %shard_map.105 = (f32[128,1024]{1,0:T(8,128)}, f32[128,1024]{1,0:T(8,128)}) custom-call(s32[1]{0:T(128)} %bitcast.seat, f32[128,1024]{1,0:T(8,128)S(1)} %get-tuple-element.47.k, f32[128,1024]{1,0:T(8,128)S(1)} %get-tuple-element.48.v, f32[128,1024]{1,0:T(8,128)S(1)} %get-tuple-element.71.part_k, ...), custom_call_target="tpu_custom_call", output_to_operand_aliasing={{0}: (8, {}), {1}: (9, {})} | custom-call | flops 50331648 | bytes 4595712 | tf_op jit(solution)/shard_map/pallas_call | solution.py:59
  (23 shorter events, 5.4 us)
Async XLA Ops:
  2.3 6.5 %collective-permute-start = (f32[256,128]{1,0:T(8,128)S(1)}, f32[256,128]{1,0:T(8,128)S(1)}, u32[]{:S(2)}, u32[]{:S(2)}) collective-permute-start(f32[256,128]{1,0:T(8,128)S(1)} %get-tuple-element.55), channel_id=1, source_target_pairs={{0,4},{4,0},{8,12},{12,8},{16,20},{20,16},{24,28},{28,24},{1,5},{5... | collective-permute-start | bytes 393224 | tf_op jit(solution)/shard_map/ppermute | solution.py:308
  5.4 6.4 %collective-permute-start.1 = (f32[256,128]{1,0:T(8,128)S(1)}, f32[256,128]{1,0:T(8,128)S(1)}, u32[]{:S(2)}, u32[]{:S(2)}) collective-permute-start(f32[256,128]{1,0:T(8,128)S(1)} %get-tuple-element.56), channel_id=1, source_target_pairs={{0,8},{4,12},{8,0},{12,4},{16,24},{20,28},{24,16},{28,20},{1,9},{5... | collective-permute-start | bytes 393224 | tf_op jit(solution)/shard_map/ppermute | solution.py:308
  7.0 6.0 %collective-permute-start.2 = (f32[256,128]{1,0:T(8,128)S(1)}, f32[256,128]{1,0:T(8,128)S(1)}, u32[]{:S(2)}, u32[]{:S(2)}) collective-permute-start(f32[256,128]{1,0:T(8,128)S(1)} %get-tuple-element.57), channel_id=1, source_target_pairs={{0,12},{4,8},{8,4},{12,0},{16,28},{20,24},{24,20},{28,16},{1,13},{... | collective-permute-start | bytes 393224 | tf_op jit(solution)/shard_map/ppermute | solution.py:308
  13.0 7.5 %collective-permute-start.3 = (f32[256,128]{1,0:T(8,128)S(1)}, f32[256,128]{1,0:T(8,128)S(1)}, u32[]{:S(2)}, u32[]{:S(2)}) collective-permute-start(f32[256,128]{1,0:T(8,128)S(1)} %shard_map.95), channel_id=1, source_target_pairs={{0,24},{4,28},{8,16},{12,20},{16,8},{20,12},{24,0},{28,4},{1,25},{... | collective-permute-start | bytes 393224 | tf_op jit(solution)/shard_map/ppermute | solution.py:308
  20.6 6.4 %collective-permute-start.4 = (f32[256,128]{1,0:T(8,128)S(1)}, f32[256,128]{1,0:T(8,128)S(1)}, u32[]{:S(2)}, u32[]{:S(2)}) collective-permute-start(f32[256,128]{1,0:T(8,128)S(1)} %get-tuple-element.60), channel_id=1, source_target_pairs={{0,4},{4,0},{8,12},{12,8},{16,20},{20,16},{24,28},{28,24},{1,5},{5... | collective-permute-start | bytes 393224 | tf_op jit(solution)/shard_map/ppermute | solution.py:308
  22.2 5.3 %collective-permute-start.5 = (f32[256,128]{1,0:T(8,128)S(1)}, f32[256,128]{1,0:T(8,128)S(1)}, u32[]{:S(2)}, u32[]{:S(2)}) collective-permute-start(f32[256,128]{1,0:T(8,128)S(1)} %get-tuple-element.61), channel_id=1, source_target_pairs={{0,8},{4,12},{8,0},{12,4},{16,24},{20,28},{24,16},{28,20},{1,9},{5... | collective-permute-start | bytes 393224 | tf_op jit(solution)/shard_map/ppermute | solution.py:308
  23.0 5.9 %collective-permute-start.6 = (f32[256,128]{1,0:T(8,128)S(1)}, f32[256,128]{1,0:T(8,128)S(1)}, u32[]{:S(2)}, u32[]{:S(2)}) collective-permute-start(f32[256,128]{1,0:T(8,128)S(1)} %get-tuple-element.65), channel_id=1, source_target_pairs={{0,12},{4,8},{8,4},{12,0},{16,28},{20,24},{24,20},{28,16},{1,13},{... | collective-permute-start | bytes 393224 | tf_op jit(solution)/shard_map/ppermute | solution.py:308
  29.2 3.1 %collective-permute-start.9 = (f32[8,128]{1,0:T(8,128)S(1)}, f32[8,128]{1,0:T(8,128)S(1)}, u32[]{:S(2)}, u32[]{:S(2)}) collective-permute-start(f32[8,128]{1,0:T(8,128)S(1)} %get-tuple-element.69.refs_4_), channel_id=1, source_target_pairs={{0,3},{1,2},{2,1},{3,0},{4,7},{5,6},{6,5},{7,4},{8,11},{9,10},{10,... | collective-permute-start | bytes 12296 | tf_op jit(solution)/shard_map/ppermute | solution.py:308
  29.2 3.7 %collective-permute-start.8 = (f32[8,128]{1,0:T(8,128)S(1)}, f32[8,128]{1,0:T(8,128)S(1)}, u32[]{:S(2)}, u32[]{:S(2)}) collective-permute-start(f32[8,128]{1,0:T(8,128)S(1)} %get-tuple-element.69.refs_4_), channel_id=1, source_target_pairs={{0,2},{1,3},{2,0},{3,1},{4,6},{5,7},{6,4},{7,5},{8,10},{9,11},{10,... | collective-permute-start | bytes 12296 | tf_op jit(solution)/shard_map/ppermute | solution.py:308
  30.8 2.1 %collective-permute-start.7 = (f32[8,128]{1,0:T(8,128)S(1)}, f32[8,128]{1,0:T(8,128)S(1)}, u32[]{:S(2)}, u32[]{:S(2)}) collective-permute-start(f32[8,128]{1,0:T(8,128)S(1)} %get-tuple-element.69.refs_4_), channel_id=1, source_target_pairs={{0,1},{1,0},{2,3},{3,2},{4,5},{5,4},{6,7},{7,6},{8,9},{9,8},{10,11... | collective-permute-start | bytes 12296 | tf_op jit(solution)/shard_map/ppermute | solution.py:308
  33.4 9.8 %collective-permute-start.11 = (f32[264,128]{1,0:T(8,128)S(1)}, f32[264,128]{1,0:T(8,128)S(1)}, u32[]{:S(2)}, u32[]{:S(2)}) collective-permute-start(f32[264,128]{1,0:T(8,128)S(1)} %get-tuple-element.75), channel_id=1, source_target_pairs={{0,8},{4,12},{8,0},{12,4},{16,24},{20,28},{24,16},{28,20},{1,9},{5... | collective-permute-start | bytes 405512 | tf_op jit(solution)/shard_map/ppermute | solution.py:308
  35.1 8.0 %collective-permute-start.10 = (f32[256,128]{1,0:T(8,128)S(1)}, f32[256,128]{1,0:T(8,128)S(1)}, u32[]{:S(2)}, u32[]{:S(2)}) collective-permute-start(f32[256,128]{1,0:T(8,128)S(1)} %get-tuple-element.74), channel_id=1, source_target_pairs={{0,4},{4,0},{8,12},{12,8},{16,20},{20,16},{24,28},{28,24},{1,5},{5... | collective-permute-start | bytes 393224 | tf_op jit(solution)/shard_map/ppermute | solution.py:308
  35.5 7.6 %collective-permute-start.12 = (f32[256,128]{1,0:T(8,128)S(1)}, f32[256,128]{1,0:T(8,128)S(1)}, u32[]{:S(2)}, u32[]{:S(2)}) collective-permute-start(f32[256,128]{1,0:T(8,128)S(1)} %get-tuple-element.76), channel_id=1, source_target_pairs={{0,12},{4,8},{8,4},{12,0},{16,28},{20,24},{24,20},{28,16},{1,13},{... | collective-permute-start | bytes 393224 | tf_op jit(solution)/shard_map/ppermute | solution.py:308
  43.2 7.0 %collective-permute-start.13 = (f32[264,128]{1,0:T(8,128)S(1)}, f32[264,128]{1,0:T(8,128)S(1)}, u32[]{:S(2)}, u32[]{:S(2)}) collective-permute-start(f32[264,128]{1,0:T(8,128)S(1)} %shard_map.101.refs_4_), channel_id=1, source_target_pairs={{0,24},{4,28},{8,16},{12,20},{16,8},{20,12},{24,0},{28,4},{1,25},{... | collective-permute-start | bytes 405512 | tf_op jit(solution)/shard_map/ppermute | solution.py:308
  50.3 6.0 %collective-permute-start.14 = (f32[264,128]{1,0:T(8,128)S(1)}, f32[264,128]{1,0:T(8,128)S(1)}, u32[]{:S(2)}, u32[]{:S(2)}) collective-permute-start(f32[264,128]{1,0:T(8,128)S(1)} %get-tuple-element.77.sent), channel_id=1, source_target_pairs={{0,4},{4,0},{8,12},{12,8},{16,20},{20,16},{24,28},{28,24},{1,5},{5... | collective-permute-start | bytes 405512 | tf_op jit(solution)/shard_map/ppermute | solution.py:308
  50.9 7.3 %collective-permute-start.16 = (f32[256,128]{1,0:T(8,128)S(1)}, f32[256,128]{1,0:T(8,128)S(1)}, u32[]{:S(2)}, u32[]{:S(2)}) collective-permute-start(f32[256,128]{1,0:T(8,128)S(1)} %get-tuple-element.82), channel_id=1, source_target_pairs={{0,8},{4,12},{8,0},{12,4},{16,24},{20,28},{24,16},{28,20},{1,9},{5... | collective-permute-start | bytes 393224 | tf_op jit(solution)/shard_map/ppermute | solution.py:308
  53.6 6.0 %collective-permute-start.15 = (f32[256,128]{1,0:T(8,128)S(1)}, f32[256,128]{1,0:T(8,128)S(1)}, u32[]{:S(2)}, u32[]{:S(2)}) collective-permute-start(f32[256,128]{1,0:T(8,128)S(1)} %get-tuple-element.81), channel_id=1, source_target_pairs={{0,12},{4,8},{8,4},{12,0},{16,28},{20,24},{24,20},{28,16},{1,13},{... | collective-permute-start | bytes 393224 | tf_op jit(solution)/shard_map/ppermute | solution.py:308

commit v9 on v7

--- a/solution.py
+++ b/solution.py
@@ -431,7 +431,7 @@
     sent = later[min(1, group - 1)]
     later = swap_all(later, "seq")
     grads = []
-    for which in [early[:2], *([x] for x in early[2:]), late]:
+    for which in [early[:2], early[2:] + late]:
         block = pltpu.VMEM((len(which), length, plan.state_rows), f32)
         inputs = [key_rows, value_rows, part_key, part_value, sent, *(later[x] for x in which)]
         if not grads:

time: 60.8 us -> 60.9 us (level)
  waiting for transfers between devices: 22.9 us -> 23.9 us
  Pallas kernels: 12.9 us -> 12.1 us
    ppermute x17, waiting for transfers between devices: 22.9 us -> 23.9 us  [swap(): lax.ppermute(value, axis, [(i, i ^ step) for i in range(lax.axis_size(axi...]
    pallas_call x13 -> x12, Pallas kernels: 12.9 us -> 12.1 us  [call(): pl.pallas_call(kernel, out_shape=outs, in_specs=[SMEM] * len(place) + spe...]
  transfers between devices with their start and end apart: 17 -> 17, of which waited for: 13 -> 13; matrix products, arithmetic and copies ran while one was open for 0% -> 0% of each run, Pallas kernels for 15% -> 14%
where the time goes in v9:
time: 60.9 us; the launch traced here: 60.7 us
  starting transfers between devices  24 us (39%)
  waiting for transfers between devices  23.9 us (39%)
  Pallas kernels  12.1 us (20%)
  between operations  0.73 us (1%)
    ppermute x17, starting transfers between devices, swap(): lax.ppermute(value, axis, [(i, i ^ step) for i in range(lax.axis_size(axi...  24 us
    ppermute x17, waiting for transfers between devices, swap(): lax.ppermute(value, axis, [(i, i ^ step) for i in range(lax.axis_size(axi...  23.9 us
    pallas_call x12, Pallas kernels, call(): pl.pallas_call(kernel, out_shape=outs, in_specs=[SMEM] * len(place) + spe...  12.1 us
  transfers between devices with their start and end apart: 17, of which 13 were waited for; matrix products, arithmetic and copies ran while one was open for 0% of the time, Pallas kernels for 14%

profile of v9, /device:TPU:0, one launch (start us, length us, event | category | flops | bytes accessed | tf_op | source)
XLA Modules:
  0.0 60.7 jit_solution(6556389897233332729)
XLA Ops:
  0.6 1.7 %shard_map.93 = (f32[256,128]{1,0:T(8,128)S(1)}, f32[256,128]{1,0:T(8,128)S(1)}, f32[256,128]{1,0:T(8,128)S(1)}, f32[256,128]{1,0:T(8,128)S(1)}, f32[128,1024]{1,0:T(8,128)S(1)}, /*index=5*/f32[128,1024]{1,0:T(8,128)S(1)}) custom-call(f32[128,1024]{1,0:T(8,128)} %k_hbm.1, f32[128,1024]{1,0:T(8,128)} %v_hbm.1), custom_call_target="tpu_custom_call" | custom-call | flops 100663296 | bytes 2621440 | tf_op jit(solution)/shard_map/pallas_call | solution.py:59
  2.3 3.0 %collective-permute-start = (f32[256,128]{1,0:T(8,128)S(1)}, f32[256,128]{1,0:T(8,128)S(1)}, u32[]{:S(2)}, u32[]{:S(2)}) collective-permute-start(f32[256,128]{1,0:T(8,128)S(1)} %get-tuple-element.53), channel_id=1, source_target_pairs={{0,4},{4,0},{8,12},{12,8},{16,20},{20,16},{24,28},{28,24},{1,5},{5... | collective-permute-start | bytes 393224 | tf_op jit(solution)/shard_map/ppermute | solution.py:308
  5.4 1.6 %collective-permute-start.1 = (f32[256,128]{1,0:T(8,128)S(1)}, f32[256,128]{1,0:T(8,128)S(1)}, u32[]{:S(2)}, u32[]{:S(2)}) collective-permute-start(f32[256,128]{1,0:T(8,128)S(1)} %get-tuple-element.54), channel_id=1, source_target_pairs={{0,8},{4,12},{8,0},{12,4},{16,24},{20,28},{24,16},{28,20},{1,9},{5... | collective-permute-start | bytes 393224 | tf_op jit(solution)/shard_map/ppermute | solution.py:308
  7.0 1.9 %collective-permute-done.refs_1_ = f32[256,128]{1,0:T(8,128)S(1)} collective-permute-done((f32[256,128]{1,0:T(8,128)S(1)}, f32[256,128]{1,0:T(8,128)S(1)}, u32[]{:S(2)}, u32[]{:S(2)}) %collective-permute-start) | collective-permute-done | bytes 131104 | tf_op jit(solution)/shard_map/ppermute | solution.py:308
  8.9 2.9 %collective-permute-done.1.refs_2_ = f32[256,128]{1,0:T(8,128)S(1)} collective-permute-done((f32[256,128]{1,0:T(8,128)S(1)}, f32[256,128]{1,0:T(8,128)S(1)}, u32[]{:S(2)}, u32[]{:S(2)}) %collective-permute-start.1) | collective-permute-done | bytes 131104 | tf_op jit(solution)/shard_map/ppermute | solution.py:308
  11.7 1.2 %collective-permute-done.2.refs_3_ = f32[256,128]{1,0:T(8,128)S(1)} collective-permute-done((f32[256,128]{1,0:T(8,128)S(1)}, f32[256,128]{1,0:T(8,128)S(1)}, u32[]{:S(2)}, u32[]{:S(2)}) %collective-permute-start.2) | collective-permute-done | bytes 131104 | tf_op jit(solution)/shard_map/ppermute | solution.py:308
  13.0 3.8 %collective-permute-start.3 = (f32[256,128]{1,0:T(8,128)S(1)}, f32[256,128]{1,0:T(8,128)S(1)}, u32[]{:S(2)}, u32[]{:S(2)}) collective-permute-start(f32[256,128]{1,0:T(8,128)S(1)} %shard_map.95), channel_id=1, source_target_pairs={{0,24},{4,28},{8,16},{12,20},{16,8},{20,12},{24,0},{28,4},{1,25},{... | collective-permute-start | bytes 393224 | tf_op jit(solution)/shard_map/ppermute | solution.py:308
  16.8 3.7 %shard_map.94 = (f32[128,1024]{1,0:T(8,128)S(1)}, f32[8,128,128]{2,1,0:T(8,128)S(1)}, f32[8,128,128]{2,1,0:T(8,128)S(1)}, f32[128,1024]{1,0:T(8,128)S(1)}, f32[1...) custom-call(s32[1]{0:T(128)} %bitcast.seat, f32[128,1024]{1,0:T(8,128)} %q_hbm.1, f32[128,1024]{1,0:T(8,128)S(1)} %get-tuple-element.45.k, ...), custom_call_target="tpu_custom_call" | custom-call | flops 201326592 | bytes 4727296 | tf_op jit(solution)/shard_map/pallas_call | solution.py:59
  20.6 1.6 %collective-permute-start.4 = (f32[256,128]{1,0:T(8,128)S(1)}, f32[256,128]{1,0:T(8,128)S(1)}, u32[]{:S(2)}, u32[]{:S(2)}) collective-permute-start(f32[256,128]{1,0:T(8,128)S(1)} %get-tuple-element.58), channel_id=1, source_target_pairs={{0,4},{4,0},{8,12},{12,8},{16,20},{20,16},{24,28},{28,24},{1,5},{5... | collective-permute-start | bytes 393224 | tf_op jit(solution)/shard_map/ppermute | solution.py:308
  23.0 1.2 %collective-permute-start.6 = (f32[256,128]{1,0:T(8,128)S(1)}, f32[256,128]{1,0:T(8,128)S(1)}, u32[]{:S(2)}, u32[]{:S(2)}) collective-permute-start(f32[256,128]{1,0:T(8,128)S(1)} %get-tuple-element.63), channel_id=1, source_target_pairs={{0,12},{4,8},{8,4},{12,0},{16,28},{20,24},{24,20},{28,16},{1,13},{... | collective-permute-start | bytes 393224 | tf_op jit(solution)/shard_map/ppermute | solution.py:308
  24.2 2.9 %collective-permute-done.4.refs_1_.refs_5_ = f32[256,128]{1,0:T(8,128)S(1)} collective-permute-done((f32[256,128]{1,0:T(8,128)S(1)}, f32[256,128]{1,0:T(8,128)S(1)}, u32[]{:S(2)}, u32[]{:S(2)}) %collective-permute-start.4) | collective-permute-done | bytes 131104 | tf_op jit(solution)/shard_map/ppermute | solution.py:308
  29.2 1.6 %collective-permute-start.8 = (f32[8,128]{1,0:T(8,128)S(1)}, f32[8,128]{1,0:T(8,128)S(1)}, u32[]{:S(2)}, u32[]{:S(2)}) collective-permute-start(f32[8,128]{1,0:T(8,128)S(1)} %get-tuple-element.67.refs_4_), channel_id=1, source_target_pairs={{0,2},{1,3},{2,0},{3,1},{4,6},{5,7},{6,4},{7,5},{8,10},{9,11},{10,... | collective-permute-start | bytes 12296 | tf_op jit(solution)/shard_map/ppermute | solution.py:308
  31.1 1.2 %collective-permute-done.9.refs_7_ = f32[8,128]{1,0:T(8,128)S(1)} collective-permute-done((f32[8,128]{1,0:T(8,128)S(1)}, f32[8,128]{1,0:T(8,128)S(1)}, u32[]{:S(2)}, u32[]{:S(2)}) %collective-permute-start.9) | collective-permute-done | bytes 4128 | tf_op jit(solution)/shard_map/ppermute | solution.py:308
  33.4 1.7 %collective-permute-start.11 = (f32[264,128]{1,0:T(8,128)S(1)}, f32[264,128]{1,0:T(8,128)S(1)}, u32[]{:S(2)}, u32[]{:S(2)}) collective-permute-start(f32[264,128]{1,0:T(8,128)S(1)} %get-tuple-element.73), channel_id=1, source_target_pairs={{0,8},{4,12},{8,0},{12,4},{16,24},{20,28},{24,16},{28,20},{1,9},{5... | collective-permute-start | bytes 405512 | tf_op jit(solution)/shard_map/ppermute | solution.py:308
  35.5 1.4 %collective-permute-start.12 = (f32[256,128]{1,0:T(8,128)S(1)}, f32[256,128]{1,0:T(8,128)S(1)}, u32[]{:S(2)}, u32[]{:S(2)}) collective-permute-start(f32[256,128]{1,0:T(8,128)S(1)} %get-tuple-element.74), channel_id=1, source_target_pairs={{0,12},{4,8},{8,4},{12,0},{16,28},{20,24},{24,20},{28,16},{1,13},{... | collective-permute-start | bytes 393224 | tf_op jit(solution)/shard_map/ppermute | solution.py:308
  36.9 6.2 %collective-permute-done.10.refs_1_ = f32[256,128]{1,0:T(8,128)S(1)} collective-permute-done((f32[256,128]{1,0:T(8,128)S(1)}, f32[256,128]{1,0:T(8,128)S(1)}, u32[]{:S(2)}, u32[]{:S(2)}) %collective-permute-start.10) | collective-permute-done | bytes 131104 | tf_op jit(solution)/shard_map/ppermute | solution.py:308
  43.2 3.0 %collective-permute-start.13 = (f32[264,128]{1,0:T(8,128)S(1)}, f32[264,128]{1,0:T(8,128)S(1)}, u32[]{:S(2)}, u32[]{:S(2)}) collective-permute-start(f32[264,128]{1,0:T(8,128)S(1)} %shard_map.101.refs_4_), channel_id=1, source_target_pairs={{0,24},{4,28},{8,16},{12,20},{16,8},{20,12},{24,0},{28,4},{1,25},{... | collective-permute-start | bytes 405512 | tf_op jit(solution)/shard_map/ppermute | solution.py:308
  46.2 2.4 %shard_map.100 = (f32[128,1024]{1,0:T(8,128)S(1)}, f32[128,1024]{1,0:T(8,128)S(1)}, f32[128,1024]{1,0:T(8,128)S(1)}) custom-call(s32[1]{0:T(128)} %bitcast.seat, f32[128,1024]{1,0:T(8,128)S(1)} %get-tuple-element.47.q, f32[128,1024]{1,0:T(8,128)S(1)} %get-tuple-element.45.k, f32[128,1024]{1,0:T(8,128)S(1)} %get-tuple-element.46.v, ...), custom_call_target="tpu_custom_call" | custom-call | flops 503316480 | bytes 5246976 | tf_op jit(solution)/shard_map/pallas_call | solution.py:59
  48.6 1.5 %collective-permute-done.13.refs_5_ = f32[264,128]{1,0:T(8,128)S(1)} collective-permute-done((f32[264,128]{1,0:T(8,128)S(1)}, f32[264,128]{1,0:T(8,128)S(1)}, u32[]{:S(2)}, u32[]{:S(2)}) %collective-permute-start.13) | collective-permute-done | bytes 135200 | tf_op jit(solution)/shard_map/ppermute | solution.py:308
  50.9 2.7 %collective-permute-start.15 = (f32[256,128]{1,0:T(8,128)S(1)}, f32[256,128]{1,0:T(8,128)S(1)}, u32[]{:S(2)}, u32[]{:S(2)}) collective-permute-start(f32[256,128]{1,0:T(8,128)S(1)} %get-tuple-element.79), channel_id=1, source_target_pairs={{0,8},{4,12},{8,0},{12,4},{16,24},{20,28},{24,16},{28,20},{1,9},{5... | collective-permute-start | bytes 393224 | tf_op jit(solution)/shard_map/ppermute | solution.py:308
  53.9 1.5 %collective-permute-done.14.refs_1_.refs_2_ = f32[264,128]{1,0:T(8,128)S(1)} collective-permute-done((f32[264,128]{1,0:T(8,128)S(1)}, f32[264,128]{1,0:T(8,128)S(1)}, u32[]{:S(2)}, u32[]{:S(2)}) %collective-permute-start.14) | collective-permute-done | bytes 135200 | tf_op jit(solution)/shard_map/ppermute | solution.py:308
  55.4 1.8 %shard_map.103 = (f32[1,1]{1,0:T(1,128)}, f32[128,1024]{1,0:T(8,128)}, f32[128,1024]{1,0:T(8,128)}, f32[128,1024]{1,0:T(8,128)}) custom-call(s32[1]{0:T(128)} %bitcast.seat, f32[128,1024]{1,0:T(8,128)S(1)} %get-tuple-element.45.k, f32[128,1024]{1,0:T(8,128)S(1)} %get-tuple-element.46.v, f32[128,1024]{1,0:T(8,128)S(1)} %get-tuple-element.69.refs_6_.part_k, ...), custom_call_target="tpu_custom_call" | custom-call | flops 100663296 | bytes 4595716 | tf_op jit(solution)/shard_map/pallas_call | solution.py:59
  58.0 1.6 %collective-permute-done.16.refs_1_ = f32[256,128]{1,0:T(8,128)S(1)} collective-permute-done((f32[256,128]{1,0:T(8,128)S(1)}, f32[256,128]{1,0:T(8,128)S(1)}, u32[]{:S(2)}, u32[]{:S(2)}) %collective-permute-start.16) | collective-permute-done | bytes 131104 | tf_op jit(solution)/shard_map/ppermute | solution.py:308
  59.6 1.1 %shard_map.104 = (f32[128,1024]{1,0:T(8,128)}, f32[128,1024]{1,0:T(8,128)}) custom-call(s32[1]{0:T(128)} %bitcast.seat, f32[128,1024]{1,0:T(8,128)S(1)} %get-tuple-element.45.k, f32[128,1024]{1,0:T(8,128)S(1)} %get-tuple-element.46.v, f32[128,1024]{1,0:T(8,128)S(1)} %get-tuple-element.69.refs_6_.part_k, ...), custom_call_target="tpu_custom_call", output_to_operand_aliasing={{0}: (9, {}), {1}: (10, {})} | custom-call | flops 100663296 | bytes 4726784 | tf_op jit(solution)/shard_map/pallas_call | solution.py:59
  (22 shorter events, 6.7 us)
Async XLA Ops:
  2.3 6.5 %collective-permute-start = (f32[256,128]{1,0:T(8,128)S(1)}, f32[256,128]{1,0:T(8,128)S(1)}, u32[]{:S(2)}, u32[]{:S(2)}) collective-permute-start(f32[256,128]{1,0:T(8,128)S(1)} %get-tuple-element.53), channel_id=1, source_target_pairs={{0,4},{4,0},{8,12},{12,8},{16,20},{20,16},{24,28},{28,24},{1,5},{5... | collective-permute-start | bytes 393224 | tf_op jit(solution)/shard_map/ppermute | solution.py:308
  5.4 6.4 %collective-permute-start.1 = (f32[256,128]{1,0:T(8,128)S(1)}, f32[256,128]{1,0:T(8,128)S(1)}, u32[]{:S(2)}, u32[]{:S(2)}) collective-permute-start(f32[256,128]{1,0:T(8,128)S(1)} %get-tuple-element.54), channel_id=1, source_target_pairs={{0,8},{4,12},{8,0},{12,4},{16,24},{20,28},{24,16},{28,20},{1,9},{5... | collective-permute-start | bytes 393224 | tf_op jit(solution)/shard_map/ppermute | solution.py:308
  7.0 6.0 %collective-permute-start.2 = (f32[256,128]{1,0:T(8,128)S(1)}, f32[256,128]{1,0:T(8,128)S(1)}, u32[]{:S(2)}, u32[]{:S(2)}) collective-permute-start(f32[256,128]{1,0:T(8,128)S(1)} %get-tuple-element.55), channel_id=1, source_target_pairs={{0,12},{4,8},{8,4},{12,0},{16,28},{20,24},{24,20},{28,16},{1,13},{... | collective-permute-start | bytes 393224 | tf_op jit(solution)/shard_map/ppermute | solution.py:308
  13.0 7.5 %collective-permute-start.3 = (f32[256,128]{1,0:T(8,128)S(1)}, f32[256,128]{1,0:T(8,128)S(1)}, u32[]{:S(2)}, u32[]{:S(2)}) collective-permute-start(f32[256,128]{1,0:T(8,128)S(1)} %shard_map.95), channel_id=1, source_target_pairs={{0,24},{4,28},{8,16},{12,20},{16,8},{20,12},{24,0},{28,4},{1,25},{... | collective-permute-start | bytes 393224 | tf_op jit(solution)/shard_map/ppermute | solution.py:308
  20.6 6.4 %collective-permute-start.4 = (f32[256,128]{1,0:T(8,128)S(1)}, f32[256,128]{1,0:T(8,128)S(1)}, u32[]{:S(2)}, u32[]{:S(2)}) collective-permute-start(f32[256,128]{1,0:T(8,128)S(1)} %get-tuple-element.58), channel_id=1, source_target_pairs={{0,4},{4,0},{8,12},{12,8},{16,20},{20,16},{24,28},{28,24},{1,5},{5... | collective-permute-start | bytes 393224 | tf_op jit(solution)/shard_map/ppermute | solution.py:308
  22.2 5.3 %collective-permute-start.5 = (f32[256,128]{1,0:T(8,128)S(1)}, f32[256,128]{1,0:T(8,128)S(1)}, u32[]{:S(2)}, u32[]{:S(2)}) collective-permute-start(f32[256,128]{1,0:T(8,128)S(1)} %get-tuple-element.59), channel_id=1, source_target_pairs={{0,8},{4,12},{8,0},{12,4},{16,24},{20,28},{24,16},{28,20},{1,9},{5... | collective-permute-start | bytes 393224 | tf_op jit(solution)/shard_map/ppermute | solution.py:308
  23.0 5.9 %collective-permute-start.6 = (f32[256,128]{1,0:T(8,128)S(1)}, f32[256,128]{1,0:T(8,128)S(1)}, u32[]{:S(2)}, u32[]{:S(2)}) collective-permute-start(f32[256,128]{1,0:T(8,128)S(1)} %get-tuple-element.63), channel_id=1, source_target_pairs={{0,12},{4,8},{8,4},{12,0},{16,28},{20,24},{24,20},{28,16},{1,13},{... | collective-permute-start | bytes 393224 | tf_op jit(solution)/shard_map/ppermute | solution.py:308
  29.2 3.1 %collective-permute-start.9 = (f32[8,128]{1,0:T(8,128)S(1)}, f32[8,128]{1,0:T(8,128)S(1)}, u32[]{:S(2)}, u32[]{:S(2)}) collective-permute-start(f32[8,128]{1,0:T(8,128)S(1)} %get-tuple-element.67.refs_4_), channel_id=1, source_target_pairs={{0,3},{1,2},{2,1},{3,0},{4,7},{5,6},{6,5},{7,4},{8,11},{9,10},{10,... | collective-permute-start | bytes 12296 | tf_op jit(solution)/shard_map/ppermute | solution.py:308
  29.2 3.7 %collective-permute-start.8 = (f32[8,128]{1,0:T(8,128)S(1)}, f32[8,128]{1,0:T(8,128)S(1)}, u32[]{:S(2)}, u32[]{:S(2)}) collective-permute-start(f32[8,128]{1,0:T(8,128)S(1)} %get-tuple-element.67.refs_4_), channel_id=1, source_target_pairs={{0,2},{1,3},{2,0},{3,1},{4,6},{5,7},{6,4},{7,5},{8,10},{9,11},{10,... | collective-permute-start | bytes 12296 | tf_op jit(solution)/shard_map/ppermute | solution.py:308
  30.8 2.1 %collective-permute-start.7 = (f32[8,128]{1,0:T(8,128)S(1)}, f32[8,128]{1,0:T(8,128)S(1)}, u32[]{:S(2)}, u32[]{:S(2)}) collective-permute-start(f32[8,128]{1,0:T(8,128)S(1)} %get-tuple-element.67.refs_4_), channel_id=1, source_target_pairs={{0,1},{1,0},{2,3},{3,2},{4,5},{5,4},{6,7},{7,6},{8,9},{9,8},{10,11... | collective-permute-start | bytes 12296 | tf_op jit(solution)/shard_map/ppermute | solution.py:308
  33.4 9.8 %collective-permute-start.11 = (f32[264,128]{1,0:T(8,128)S(1)}, f32[264,128]{1,0:T(8,128)S(1)}, u32[]{:S(2)}, u32[]{:S(2)}) collective-permute-start(f32[264,128]{1,0:T(8,128)S(1)} %get-tuple-element.73), channel_id=1, source_target_pairs={{0,8},{4,12},{8,0},{12,4},{16,24},{20,28},{24,16},{28,20},{1,9},{5... | collective-permute-start | bytes 405512 | tf_op jit(solution)/shard_map/ppermute | solution.py:308
  35.1 8.0 %collective-permute-start.10 = (f32[256,128]{1,0:T(8,128)S(1)}, f32[256,128]{1,0:T(8,128)S(1)}, u32[]{:S(2)}, u32[]{:S(2)}) collective-permute-start(f32[256,128]{1,0:T(8,128)S(1)} %get-tuple-element.72), channel_id=1, source_target_pairs={{0,4},{4,0},{8,12},{12,8},{16,20},{20,16},{24,28},{28,24},{1,5},{5... | collective-permute-start | bytes 393224 | tf_op jit(solution)/shard_map/ppermute | solution.py:308
  35.5 7.6 %collective-permute-start.12 = (f32[256,128]{1,0:T(8,128)S(1)}, f32[256,128]{1,0:T(8,128)S(1)}, u32[]{:S(2)}, u32[]{:S(2)}) collective-permute-start(f32[256,128]{1,0:T(8,128)S(1)} %get-tuple-element.74), channel_id=1, source_target_pairs={{0,12},{4,8},{8,4},{12,0},{16,28},{20,24},{24,20},{28,16},{1,13},{... | collective-permute-start | bytes 393224 | tf_op jit(solution)/shard_map/ppermute | solution.py:308
  43.2 7.0 %collective-permute-start.13 = (f32[264,128]{1,0:T(8,128)S(1)}, f32[264,128]{1,0:T(8,128)S(1)}, u32[]{:S(2)}, u32[]{:S(2)}) collective-permute-start(f32[264,128]{1,0:T(8,128)S(1)} %shard_map.101.refs_4_), channel_id=1, source_target_pairs={{0,24},{4,28},{8,16},{12,20},{16,8},{20,12},{24,0},{28,4},{1,25},{... | collective-permute-start | bytes 405512 | tf_op jit(solution)/shard_map/ppermute | solution.py:308
  50.3 5.1 %collective-permute-start.14 = (f32[264,128]{1,0:T(8,128)S(1)}, f32[264,128]{1,0:T(8,128)S(1)}, u32[]{:S(2)}, u32[]{:S(2)}) collective-permute-start(f32[264,128]{1,0:T(8,128)S(1)} %get-tuple-element.75.sent), channel_id=1, source_target_pairs={{0,4},{4,0},{8,12},{12,8},{16,20},{20,16},{24,28},{28,24},{1,5},{5... | collective-permute-start | bytes 405512 | tf_op jit(solution)/shard_map/ppermute | solution.py:308
  50.9 7.1 %collective-permute-start.15 = (f32[256,128]{1,0:T(8,128)S(1)}, f32[256,128]{1,0:T(8,128)S(1)}, u32[]{:S(2)}, u32[]{:S(2)}) collective-permute-start(f32[256,128]{1,0:T(8,128)S(1)} %get-tuple-element.79), channel_id=1, source_target_pairs={{0,8},{4,12},{8,0},{12,4},{16,24},{20,28},{24,16},{28,20},{1,9},{5... | collective-permute-start | bytes 393224 | tf_op jit(solution)/shard_map/ppermute | solution.py:308
  53.6 6.0 %collective-permute-start.16 = (f32[256,128]{1,0:T(8,128)S(1)}, f32[256,128]{1,0:T(8,128)S(1)}, u32[]{:S(2)}, u32[]{:S(2)}) collective-permute-start(f32[256,128]{1,0:T(8,128)S(1)} %get-tuple-element.80), channel_id=1, source_target_pairs={{0,12},{4,8},{8,4},{12,0},{16,28},{20,24},{24,20},{28,16},{1,13},{... | collective-permute-start | bytes 393224 | tf_op jit(solution)/shard_map/ppermute | solution.py:308
